TPU v7x, 32 devices: a whole 2x2x4 slice. The times are simulated.
32 devices in a mesh: dp: 4 (over y, x), ctx: 8 (over z, core).
Axes of the slice: x: 2, y: 2, z: 4, core: 2. Of those that a mesh axis runs over, the one named last changes fastest.
Arguments:
- tokens: bfloat16 [8, 1024, 1024], P('dp', 'ctx'), may hold values from -6 to 6
- teacher: bfloat16 [8, 1024, 1024], P('dp', 'ctx'), may hold values from -6 to 6
- segments: int32 [8, 1024], P('dp'), may hold values from 0 to 13, as said below
- positions: int32 [8, 1024], P('dp', 'ctx'), may hold values from 0 to 639, as said below
- valid_mask: int32 [8, 1024], P('dp', 'ctx'), may hold values from 0 to 1, as said below
- norm_gain: bfloat16 [1024], P(('dp', 'ctx')), may hold values from 0.25 to 1.75
- norm_bias: bfloat16 [1024], P(('dp', 'ctx')), may hold values from -1.1953125 to 1.1953125
- qkv_weight: bfloat16 [1024, 3072], P(('dp', 'ctx')), may hold values from -0.1875 to 0.1875
- qkv_bias: bfloat16 [3072], P(('dp', 'ctx')), may hold values from -1.1953125 to 1.1953125
- proj_weight: bfloat16 [1024, 1024], P(('dp', 'ctx')), may hold values from -1 to 1
- proj_bias: bfloat16 [1024], P(('dp', 'ctx')), may hold values from -1.1953125 to 1.1953125
- up_weight: bfloat16 [1024, 4096], P(('dp', 'ctx')), may hold values from -0.1875 to 0.1875
- up_bias: bfloat16 [4096], P(('dp', 'ctx')), may hold values from -1.1953125 to 1.1953125
- down_weight: bfloat16 [4096, 1024], P(('dp', 'ctx')), may hold values from -0.09375 to 0.09375
- down_bias: bfloat16 [1024], P(('dp', 'ctx')), may hold values from -1.1953125 to 1.1953125
Outputs:
- layer_out: bfloat16 [8, 1024, 1024], P('dp', 'ctx')
- loss: float32 [], replicated
- input_grad: bfloat16 [8, 1024, 1024], P('dp', 'ctx')
- norm_gain_grad: float32 [1024], P(('dp', 'ctx'))
- norm_bias_grad: float32 [1024], P(('dp', 'ctx'))
- qkv_weight_grad: float32 [1024, 3072], P(('dp', 'ctx'))
- query_key_bias_grad: float32 [2048], P(('dp', 'ctx'))
- value_bias_grad: float32 [1024], P(('dp', 'ctx'))
- proj_weight_grad: float32 [1024, 1024], P(('dp', 'ctx'))
- proj_bias_grad: float32 [1024], P(('dp', 'ctx'))
- up_weight_grad: float32 [1024, 4096], P(('dp', 'ctx'))
- up_bias_grad: float32 [4096], P(('dp', 'ctx'))
- down_weight_grad: float32 [4096, 1024], P(('dp', 'ctx'))
- down_bias_grad: float32 [1024], P(('dp', 'ctx'))
Inputs may be any that keep to these rules, and one draw needn't show every extreme that they name: `segments`: along each sequence the segment numbers start at 0 on its first token, rise by one at the first token of each next document and never fall. The first document of every sequence has exactly 640 tokens; every document but the last of a sequence has 30 tokens or more (the sequence's end may cut the last one short); in one sequence every document after the first, except perhaps its last, has exactly 30 tokens. `positions`: A token's position within its document: 0 at a document's first token, one more at each following token of the same document. `valid_mask`: the first token of every sequence is marked 1.
All inputs are finite; a program needn't handle non-finite values.
Results may differ from a plain program's by a relative error of at most 0.01.
Values may be sent and summed in bfloat16 or wider, within the bound.
No kernel may reach another device: no remote copies, remote signals or barrier semaphores. Data moves between devices by JAX's collectives and lax.ppermute only.
A program may use at most 256 MiB of HBM per device.

v0:
```python
import math

import jax
import jax.numpy as jnp
from jax import lax
from jax.sharding import PartitionSpec as P

HEADS = 16
ROT = 16


NEG_FILL = -1000000000.0


def rotary_tables(places, rot_dims):
    half_dims = rot_dims // 2
    freq_steps = jnp.arange(half_dims, dtype=jnp.float32)
    inverse = jnp.power(10000.0, -2.0 * freq_steps / rot_dims)
    angles = places.astype(jnp.float32)[:, None] * inverse[None, :]
    return (jnp.cos(angles)[:, None, :], jnp.sin(angles)[:, None, :])


def rotate(heads_in, cosine, sine_table, rot_dims):
    half_dims = rot_dims // 2
    first_half = heads_in[..., :half_dims]
    second_half = heads_in[..., half_dims:rot_dims]
    return jnp.concatenate(
        [
            first_half * cosine - second_half * sine_table,
            second_half * cosine + first_half * sine_table,
            heads_in[..., rot_dims:],
        ],
        axis=-1,
    )


def layer_norm(rows_in, norm_gain, norm_bias):
    row_mean = jnp.mean(rows_in, axis=-1, keepdims=True)
    centered = rows_in - row_mean
    variance = jnp.mean(centered * centered, axis=-1, keepdims=True)
    return centered * lax.rsqrt(variance + 1e-05) * norm_gain + norm_bias


def gelu_exact(values):
    return jax.nn.gelu(values, approximate=False)


def split_heads(matrix, head_count):
    return matrix.reshape(matrix.shape[0], head_count, matrix.shape[1] // head_count)


def mask_for(row_place, col_place, row_segs, col_segs):
    return (col_place[None, :] <= row_place[:, None]) & (col_segs[None, :] == row_segs[:, None])


def masked_scores(query_blk, key_blk, allowed, head_count, score_scale):
    raw_scores = jnp.einsum(
        "qhd,khd->hqk",
        split_heads(query_blk, head_count),
        split_heads(key_blk, head_count),
        preferred_element_type=jnp.float32,
    )
    return jnp.where(allowed[None], raw_scores * score_scale, NEG_FILL)


def body(
    tokens,
    teacher,
    segments,
    positions,
    valid_mask,
    norm_gain,
    norm_bias,
    qkv_weight,
    qkv_bias,
    proj_weight,
    proj_bias,
    up_weight,
    up_bias,
    down_weight,
    down_bias,
):
    forward_set = (
        lax.all_gather(norm_gain, ("dp", "ctx"), axis=0, tiled=True),
        lax.all_gather(norm_bias, ("dp", "ctx"), axis=0, tiled=True),
        lax.all_gather(qkv_weight, ("dp", "ctx"), axis=0, tiled=True),
        lax.all_gather(qkv_bias, ("dp", "ctx"), axis=0, tiled=True),
        lax.all_gather(proj_weight, ("dp", "ctx"), axis=0, tiled=True),
        lax.all_gather(proj_bias, ("dp", "ctx"), axis=0, tiled=True),
        lax.all_gather(up_weight, ("dp", "ctx"), axis=0, tiled=True),
        lax.all_gather(up_bias, ("dp", "ctx"), axis=0, tiled=True),
        lax.all_gather(down_weight, ("dp", "ctx"), axis=0, tiled=True),
        lax.all_gather(down_bias, ("dp", "ctx"), axis=0, tiled=True),
    )
    seq_count, local_len, model_width = tokens.shape
    head_count = HEADS
    head_size = model_width // head_count
    length = segments.shape[1]
    row_count = seq_count * local_len
    total_tokens = seq_count * lax.axis_size("dp") * length
    score_scale = 1.0 / math.sqrt(head_size)
    offset = lax.axis_index("ctx") * local_len
    query_place = offset + jnp.arange(local_len, dtype=jnp.int32)
    key_place = jnp.arange(length, dtype=jnp.int32)
    query_segs = lax.dynamic_slice_in_dim(segments, offset, local_len, 1)
    inputs = tokens.reshape(row_count, model_width).astype(jnp.float32)
    normed_low = layer_norm(
        inputs, forward_set[0].astype(jnp.float32), forward_set[1].astype(jnp.float32)
    ).astype(jnp.bfloat16)
    qkv_full = jnp.dot(
        normed_low, forward_set[2], preferred_element_type=jnp.float32
    ) + forward_set[3].astype(jnp.float32)
    cosine, sine_table = rotary_tables(positions.reshape(row_count), ROT)
    query_low = (
        rotate(split_heads(qkv_full[:, :model_width], head_count), cosine, sine_table, ROT)
        .reshape(seq_count, local_len, model_width)
        .astype(jnp.bfloat16)
    )
    key_low = (
        rotate(
            split_heads(qkv_full[:, model_width : 2 * model_width], head_count),
            cosine,
            sine_table,
            ROT,
        )
        .reshape(seq_count, local_len, model_width)
        .astype(jnp.bfloat16)
    )
    value_low = (
        qkv_full[:, 2 * model_width :]
        .reshape(seq_count, local_len, model_width)
        .astype(jnp.bfloat16)
    )
    key_all, value_all = (
        lax.all_gather(key_low, "ctx", axis=1, tiled=True),
        lax.all_gather(value_low, "ctx", axis=1, tiled=True),
    )

    def attend_forward(sequence_in):
        query_blk, key_blk, value_blk, row_segs, col_segs = sequence_in
        allowed = mask_for(query_place, key_place, row_segs, col_segs)
        scores = masked_scores(query_blk, key_blk, allowed, head_count, score_scale)
        row_peak = jnp.max(scores, axis=-1)
        exp_scores = jnp.exp(scores - row_peak[..., None])
        row_total = jnp.sum(exp_scores, axis=-1)
        probs_low = (exp_scores / row_total[..., None]).astype(jnp.bfloat16)
        mixed = jnp.einsum(
            "hqk,khd->qhd",
            probs_low,
            split_heads(value_blk, head_count),
            preferred_element_type=jnp.float32,
        )
        return (mixed.reshape(local_len, model_width).astype(jnp.bfloat16), row_peak, row_total)

    mixed_low, row_peaks, row_totals = lax.map(
        attend_forward, (query_low, key_all, value_all, query_segs, segments)
    )
    mixed_rows = mixed_low.reshape(row_count, model_width)
    up_full = jnp.dot(normed_low, forward_set[6], preferred_element_type=jnp.float32) + forward_set[
        7
    ].astype(jnp.float32)
    act_low = gelu_exact(up_full).astype(jnp.bfloat16)
    attn_part = jnp.dot(
        mixed_rows, forward_set[4], preferred_element_type=jnp.float32
    ) + forward_set[5].astype(jnp.float32)
    ffn_part = jnp.dot(act_low, forward_set[8], preferred_element_type=jnp.float32) + forward_set[
        9
    ].astype(jnp.float32)
    outputs = inputs + (attn_part + ffn_part)
    error = outputs - teacher.reshape(row_count, model_width).astype(jnp.float32)
    valid_rows = valid_mask.reshape(row_count).astype(jnp.float32)
    valid_count, square_sum = lax.psum(
        (jnp.sum(valid_rows), jnp.sum(valid_rows[:, None] * error * error)), ("dp", "ctx")
    )
    loss_value = square_sum / (valid_count * model_width)
    out_grad = total_tokens / (2.0 * valid_count) * (2.0 * valid_rows[:, None] * error)
    back_set = (
        lax.all_gather(norm_gain, ("dp", "ctx"), axis=0, tiled=True),
        lax.all_gather(norm_bias, ("dp", "ctx"), axis=0, tiled=True),
        lax.all_gather(qkv_weight, ("dp", "ctx"), axis=0, tiled=True),
        lax.all_gather(qkv_bias, ("dp", "ctx"), axis=0, tiled=True),
        lax.all_gather(proj_weight, ("dp", "ctx"), axis=0, tiled=True),
        lax.all_gather(proj_bias, ("dp", "ctx"), axis=0, tiled=True),
        lax.all_gather(up_weight, ("dp", "ctx"), axis=0, tiled=True),
        lax.all_gather(up_bias, ("dp", "ctx"), axis=0, tiled=True),
        lax.all_gather(down_weight, ("dp", "ctx"), axis=0, tiled=True),
        lax.all_gather(down_bias, ("dp", "ctx"), axis=0, tiled=True),
    )
    branch_low = out_grad.astype(jnp.bfloat16)
    branch_sum = jnp.sum(branch_low, axis=0, dtype=jnp.float32)
    down_wgrad = jnp.einsum("rf,rd->fd", act_low, branch_low, preferred_element_type=jnp.float32)
    proj_wgrad = jnp.einsum("re,rd->ed", mixed_rows, branch_low, preferred_element_type=jnp.float32)
    act_grad = jnp.einsum("rd,fd->rf", branch_low, back_set[8], preferred_element_type=jnp.float32)
    gelu_value, gelu_pull = jax.vjp(gelu_exact, up_full)
    up_low = gelu_pull(act_grad)[0].astype(jnp.bfloat16)
    up_wgrad = jnp.einsum("rd,rf->df", normed_low, up_low, preferred_element_type=jnp.float32)
    up_bgrad = jnp.sum(up_low, axis=0, dtype=jnp.float32)
    normed_grad = jnp.einsum("rf,df->rd", up_low, back_set[6], preferred_element_type=jnp.float32)
    mixed_grad = (
        jnp.einsum("rd,ed->re", branch_low, back_set[4], preferred_element_type=jnp.float32)
        .astype(jnp.bfloat16)
        .reshape(seq_count, local_len, model_width)
    )

    def attend_back(sequence_in):
        query_blk, key_blk, value_blk, grad_blk, row_segs, col_segs, row_peak, row_total = (
            sequence_in
        )
        allowed = mask_for(query_place, key_place, row_segs, col_segs)
        scores = masked_scores(query_blk, key_blk, allowed, head_count, score_scale)
        probabilities = jnp.exp(scores - row_peak[..., None]) / row_total[..., None]
        prob_grad = jnp.einsum(
            "qhd,khd->hqk",
            split_heads(grad_blk, head_count),
            split_heads(value_blk, head_count),
            preferred_element_type=jnp.float32,
        )
        row_delta = jnp.sum(probabilities * prob_grad, axis=-1)
        score_low = (probabilities * (prob_grad - row_delta[..., None])).astype(jnp.bfloat16)
        query_grad = (
            jnp.einsum(
                "hqk,khd->qhd",
                score_low,
                split_heads(key_blk, head_count),
                preferred_element_type=jnp.float32,
            )
            * score_scale
        )
        key_grad = (
            jnp.einsum(
                "hqk,qhd->khd",
                score_low,
                split_heads(query_blk, head_count),
                preferred_element_type=jnp.float32,
            )
            * score_scale
        )
        value_grad = jnp.einsum(
            "hqk,qhd->khd",
            probabilities.astype(jnp.bfloat16),
            split_heads(grad_blk, head_count),
            preferred_element_type=jnp.float32,
        )
        return (
            query_grad.reshape(local_len, model_width),
            key_grad.reshape(length, model_width),
            value_grad.reshape(length, model_width),
        )

    query_grads, key_terms, value_terms = lax.map(
        attend_back,
        (query_low, key_all, value_all, mixed_grad, query_segs, segments, row_peaks, row_totals),
    )
    key_grads, value_grads = (
        lax.psum_scatter(
            key_terms.astype(jnp.bfloat16), "ctx", scatter_dimension=1, tiled=True
        ).astype(jnp.float32),
        lax.psum_scatter(
            value_terms.astype(jnp.bfloat16), "ctx", scatter_dimension=1, tiled=True
        ).astype(jnp.float32),
    )
    query_back = rotate(
        split_heads(query_grads.reshape(row_count, model_width), head_count),
        cosine,
        -sine_table,
        ROT,
    ).reshape(row_count, model_width)
    key_back = rotate(
        split_heads(key_grads.reshape(row_count, model_width), head_count), cosine, -sine_table, ROT
    ).reshape(row_count, model_width)
    qkv_low = jnp.concatenate(
        [query_back, key_back, value_grads.reshape(row_count, model_width)], axis=1
    ).astype(jnp.bfloat16)
    qkv_wgrad = jnp.einsum("rd,re->de", normed_low, qkv_low, preferred_element_type=jnp.float32)
    qkv_bgrad = jnp.sum(qkv_low, axis=0, dtype=jnp.float32)
    normed_grad = normed_grad + jnp.einsum(
        "re,de->rd", qkv_low, back_set[2], preferred_element_type=jnp.float32
    )
    norm_value, norm_pull = jax.vjp(
        layer_norm, inputs, back_set[0].astype(jnp.float32), back_set[1].astype(jnp.float32)
    )
    input_part, gain_grad, shift_grad = norm_pull(normed_grad)
    input_grad = (
        (out_grad + input_part).astype(jnp.bfloat16).reshape(seq_count, local_len, model_width)
    )
    owned_grads = (
        lax.psum_scatter(gain_grad, ("dp", "ctx"), scatter_dimension=0, tiled=True),
        lax.psum_scatter(shift_grad, ("dp", "ctx"), scatter_dimension=0, tiled=True),
        lax.psum_scatter(qkv_wgrad, ("dp", "ctx"), scatter_dimension=0, tiled=True),
        lax.psum_scatter(
            qkv_bgrad[: 2 * model_width], ("dp", "ctx"), scatter_dimension=0, tiled=True
        ),
        lax.psum_scatter(
            qkv_bgrad[2 * model_width :], ("dp", "ctx"), scatter_dimension=0, tiled=True
        ),
        lax.psum_scatter(proj_wgrad, ("dp", "ctx"), scatter_dimension=0, tiled=True),
        lax.psum_scatter(branch_sum, ("dp", "ctx"), scatter_dimension=0, tiled=True),
        lax.psum_scatter(up_wgrad, ("dp", "ctx"), scatter_dimension=0, tiled=True),
        lax.psum_scatter(up_bgrad, ("dp", "ctx"), scatter_dimension=0, tiled=True),
        lax.psum_scatter(down_wgrad, ("dp", "ctx"), scatter_dimension=0, tiled=True),
    )
    layer_out = outputs.astype(jnp.bfloat16).reshape(seq_count, local_len, model_width)
    return (
        layer_out,
        loss_value,
        input_grad,
        owned_grads[0],
        owned_grads[1],
        owned_grads[2],
        owned_grads[3],
        owned_grads[4],
        owned_grads[5],
        owned_grads[6],
        owned_grads[7],
        owned_grads[8],
        owned_grads[9],
        owned_grads[6],
    )


def solution(mesh):
    in_specs = (
        P("dp", "ctx", None),
        P("dp", "ctx", None),
        P("dp", None),
        P("dp", "ctx"),
        P("dp", "ctx"),
        P(("dp", "ctx")),
        P(("dp", "ctx")),
        P(("dp", "ctx"), None),
        P(("dp", "ctx")),
        P(("dp", "ctx"), None),
        P(("dp", "ctx")),
        P(("dp", "ctx"), None),
        P(("dp", "ctx")),
        P(("dp", "ctx"), None),
        P(("dp", "ctx")),
    )
    out_specs = (
        P("dp", "ctx", None),
        P(),
        P("dp", "ctx", None),
        P(("dp", "ctx")),
        P(("dp", "ctx")),
        P(("dp", "ctx"), None),
        P(("dp", "ctx")),
        P(("dp", "ctx")),
        P(("dp", "ctx"), None),
        P(("dp", "ctx")),
        P(("dp", "ctx"), None),
        P(("dp", "ctx")),
        P(("dp", "ctx"), None),
        P(("dp", "ctx")),
    )
    return jax.shard_map(body, mesh=mesh, in_specs=in_specs, out_specs=out_specs, check_vma=False)
```

profile of v0, /device:TPU:0, one launch (start us, length us, event | category | flops | bytes accessed | tf_op | source)
XLA Modules:
  0.0 1301.1 jit_solution(8235989427270973576)
XLA Ops:
  13.7 42.4 %all-reduce.12 = (bf16[1024]{0:T(1024)(128)(2,1)S(1)}, bf16[1024]{0:T(1024)(128)(2,1)S(1)}, bf16[1024]{0:T(1024)(128)(2,1)S(1)}, bf16[3072]{0:T(1024)(128)(2,1)S(1)}, bf16[1024]{0:T(1024)(128)(2,1)S(1)}) all-reduce(bf16[1024]{0:T(1024)(128)(2,1)S(1)} %dynamic-update-slice.1, ...), channel_id=1, replica_groups=mesh['dp'=4,'ctx'=8] {'dp','ctx'}, use_global_device_ids=true, to_apply=%add.1 | all-reduce | flops 7168 | bytes 28672
  61.4 22.0 %all-gather.8.cloned.1.call-done = bf16[1024,3072]{1,0:T(8,128)(2,1)} async-done(((bf16[32,3072]{1,0:T(8,128)(2,1)}), bf16[1024,3072]{1,0:T(8,128)(2,1)}) %all-gather.8.cloned.1.call-update) | async-done | bytes 6291472 | tf_op jit(solution)/shard_map/all_gather | solution.py:86
  83.5 4.6 convolution_add_fusion.1
  98.6 39.0 %all-gather = bf16[32,1,128]{2,1,0:T(2,128)(2,1)S(1)} all-gather(bf16[1,1,128]{2,1,0:T(2,128)(2,1)S(1)} %bitcast.230), channel_id=1, replica_groups=mesh['dp'=4,'ctx'=8] {'dp','ctx'}, dimensions={0}, use_global_device_ids=true | all-gather | bytes 8448 | tf_op jit(solution)/shard_map/all_gather | solution.py:91
  137.6 38.3 %psum.15 = f32[]{:T(128)} all-reduce(f32[]{:T(128)} %convert_reduce_fusion.4), channel_id=1, replica_groups=mesh['dp'=4,'ctx'=8] {'dp','ctx'}, use_global_device_ids=true, to_apply=%region_9.10 | all-reduce | flops 1 | bytes 8 | tf_op jit(solution)/shard_map/psum | solution.py:172
  177.6 15.9 %multiply_convert_fusion.1 = (bf16[256,4096]{1,0:T(8,128)(2,1)}, f32[256,4096]{1,0:T(8,128)}, f32[256,4096]{1,0:T(8,128)}) fusion(f32[4096]{0:T(1024)S(1)} %bitcast.229, bf16[256,1024]{1,0:T(8,128)(2,1)S(1)} %add_convert_fusion.2, bf16[1024,4096]{1,0:T(8,128)(2,1)} %all-gather.16.cloned.1.call-done), kind=kOutput, calls=%fused_computation.51 | convolution fusion | flops 2216689664 | bytes 19415040 | tf_op jit(solution)/shard_map/dot_general | solution.py:159
  193.5 49.0 %all-gather.18.cloned.1.call-done = bf16[4096,1024]{1,0:T(8,128)(2,1)} async-done(((bf16[128,1024]{1,0:T(8,128)(2,1)}), bf16[4096,1024]{1,0:T(8,128)(2,1)}) %all-gather.18.cloned.1.call-update) | async-done | bytes 8388624 | tf_op jit(solution)/shard_map/all_gather | solution.py:92
  242.5 6.3 convolution_add_fusion.4
  248.9 45.9 %all-gather.12.cloned.1.call-done = bf16[2,1024,1024]{1,0,2:T(2,128)(2,1)} async-done(((bf16[2,128,1024]{1,0,2:T(2,128)(2,1)}), bf16[2,1024,1024]{1,0,2:T(2,128)(2,1)}) %all-gather.12.cloned.1.call-update) | async-done | bytes 4194320 | tf_op jit(solution)/shard_map/all_gather | solution.py:135
  294.8 5.5 copy.48
  300.3 44.3 %all-gather.10.cloned.1.call-done = bf16[2,1024,1024]{1,2,0:T(8,128)(2,1)} async-done(((bf16[2,128,1024]{1,2,0:T(8,128)(2,1)}), bf16[2,1024,1024]{1,2,0:T(8,128)(2,1)}) %all-gather.10.cloned.1.call-update) | async-done | bytes 4194320 | tf_op jit(solution)/shard_map/all_gather | solution.py:136
  344.6 21.0 %while.30 = (s32[]{:T(128)}, bf16[2,128,1024]{2,1,0:T(8,128)(2,1)S(1)}, f32[2,16,128]{2,1,0:T(8,128)S(1)}, f32[2,16,128]{2,1,0:T(8,128)S(1)}, bf16[2,1024,1024]{...) while((s32[]{:T(128)}, ...), condition=%wide.region_5.6_spmd.clone, body=%wide.region_2.5_spmd.clone.sunk | while | flops 562557056 | bytes 57236144 | solution.py:155
  352.4 2.8 fusion.106
  362.6 2.8 fusion.106
  365.6 36.6 %all-gather.14.cloned.1.call-done = bf16[1024,1024]{1,0:T(8,128)(2,1)} async-done(((bf16[32,1024]{1,0:T(8,128)(2,1)}), bf16[1024,1024]{1,0:T(8,128)(2,1)}) %all-gather.14.cloned.1.call-update) | async-done | bytes 2097168 | tf_op jit(solution)/shard_map/all_gather | solution.py:88
  402.2 4.2 convert_reduce_fusion.2
  408.0 89.3 %while.31 = (s32[]{:T(128)}, f32[2,128,1024]{1,0,2:T(2,128)}, bf16[2,1024,1024]{1,2,0:T(8,128)(2,1)}, bf16[2,1024,1024]{2,1,0:T(8,128)(2,1)}, bf16[2,1024,1024]{...) while((s32[]{:T(128)}, f32[2,128,1024]{1,0,2:T(2,128)}, ...), condition=%wide.region_12.13_spmd.clone, body=%wide.region_10.12_spmd.clone.sunk | while | flops 1365768320 | bytes 186989392 | solution.py:250
  408.2 4.2 constant_dynamic-slice_fusion.24
  412.6 2.9 fusion.117
  416.7 3.7 multiply_reduce_fusion.5
  421.4 2.3 copy-done.1
  427.2 13.6 %dynamic_update_slice.42 = f32[2,128,1024]{1,0,2:T(2,128)} dynamic-update-slice(f32[2,128,1024]{1,0,2:T(2,128)} %get-tuple-element.580, f32[1,128,1024]{1,0,2:T(1,128)S(1)} %bitcast.201, s32[]{:T(128)S(6)} %copy.112, s32[]{:T(128)} %constant.37.clone.1..sunk, s32[]{:T(128)} %constant.37.clone.1..sunk) | dynamic-update-slice | bytes 1048580 | tf_op jit(solution)/shard_map/while/body/jit(dynamic_update_index_in_dim)/dynamic_update_slice | solution.py:250
  440.8 3.1 convolution_multiply_fusion.5
  448.3 2.9 copy.84
  452.7 4.2 constant_dynamic-slice_fusion.24
  457.1 2.9 fusion.117
  461.2 3.7 multiply_reduce_fusion.5
  465.9 2.3 copy-done.1
  471.7 13.6 %dynamic_update_slice.42 = f32[2,128,1024]{1,0,2:T(2,128)} dynamic-update-slice(f32[2,128,1024]{1,0,2:T(2,128)} %get-tuple-element.580, f32[1,128,1024]{1,0,2:T(1,128)S(1)} %bitcast.201, s32[]{:T(128)S(6)} %copy.112, s32[]{:T(128)} %constant.37.clone.1..sunk, s32[]{:T(128)} %constant.37.clone.1..sunk) | dynamic-update-slice | bytes 1048580 | tf_op jit(solution)/shard_map/while/body/jit(dynamic_update_index_in_dim)/dynamic_update_slice | solution.py:250
  485.3 3.1 convolution_multiply_fusion.5
  492.8 2.9 copy.84
  497.3 11.3 copy.57
  508.6 5.6 copy.78
  515.4 2.8 fusion.40
  520.6 42.7 %reduce-scatter.19.cloned.1.call-done = bf16[128,2048]{1,0:T(8,128)(2,1)} async-done(((bf16[1024,2048]{1,0:T(8,128)(2,1)}), bf16[128,2048]{1,0:T(8,128)(2,1)}) %reduce-scatter.19.cloned.1.call-update) | async-done | bytes 524304
  567.8 45.9 %reduce-scatter.9.cloned.1.call-done = bf16[2,128,1024]{2,1,0:T(8,128)(2,1)} async-done(((bf16[2,1024,1024]{2,1,0:T(8,128)(2,1)}), bf16[2,128,1024]{2,1,0:T(8,128)(2,1)}) %reduce-scatter.9.cloned.1.call-update) | async-done | bytes 524304 | tf_op jit(solution)/shard_map/reduce_scatter | solution.py:258
  616.1 6.3 fusion.32
  622.5 11.5 convert_reduce_fusion
  635.4 8.1 fusion.41
  643.8 9.7 fusion.42
  654.3 6.5 fusion.39
  661.4 5.0 fusion.34
  667.0 2.3 add_convert_fusion.1
  669.3 39.1 %all-reduce.11 = (f32[]{:T(128)}, f32[1024]{0:T(1024)S(1)}, f32[1024]{0:T(1024)S(1)}, f32[2048]{0:T(1024)S(1)}, f32[1024]{0:T(1024)S(1)}, /*index=5*/f32[1024]{0:T(1024)S(1)}, f32[4096]{0:T(1024)S(1)}) all-reduce(f32[]{:T(128)} %get-tuple-element.347, f32[1024]{0:T(1024)S(1)} %get-tuple-element.266, ...), channel_id=1, replica_groups=mesh['dp'=4,'ctx'=8] {'dp','ctx'}, use_global_device_ids=true, to_apply=%region_7.8 | all-reduce | flops 10241 | bytes 81928 | tf_op jit(solution)/shard_map/psum | solution.py:172
  712.1 45.3 %reduce-scatter.13.cloned.1.call-done = f32[32,1024]{1,0:T(8,128)} async-done(((f32[1024,1024]{1,0:T(8,128)}), f32[32,1024]{1,0:T(8,128)}) %reduce-scatter.13.cloned.1.call-update) | async-done | bytes 131088 | tf_op jit(solution)/shard_map/reduce_scatter | solution.py:296
  757.4 158.7 %reduce-scatter.11.cloned.1.call-done = f32[32,3072]{1,0:T(8,128)} async-done(((f32[1024,3072]{1,0:T(8,128)}), f32[32,3072]{1,0:T(8,128)}) %reduce-scatter.11.cloned.1.call-update) | async-done | bytes 393232 | tf_op jit(solution)/shard_map/reduce_scatter | solution.py:289
  916.2 188.7 %reduce-scatter.15.cloned.1.call-done = f32[32,4096]{1,0:T(8,128)} async-done(((f32[1024,4096]{1,0:T(8,128)}), f32[32,4096]{1,0:T(8,128)}) %reduce-scatter.15.cloned.1.call-update) | async-done | bytes 524304 | tf_op jit(solution)/shard_map/reduce_scatter | solution.py:298
  1104.9 187.2 %reduce-scatter.17.cloned.1.call-done = f32[128,1024]{1,0:T(8,128)} async-done(((f32[4096,1024]{1,0:T(8,128)}), f32[128,1024]{1,0:T(8,128)}) %reduce-scatter.17.cloned.1.call-update) | async-done | bytes 524304 | tf_op jit(solution)/shard_map/reduce_scatter | solution.py:300
  (240 shorter events, 79.6 us)
Async XLA Ops:
  7.2 76.3 %all-gather.8.cloned.1.call-start = ((), (), s32[]{:S(2)}) async-start(), calls=%async_computation.6 | async-start | bytes 6488064 | tf_op jit(solution)/shard_map/all_gather | solution.py:86
  7.9 169.7 %all-gather.16.cloned.1.call-start = ((), (), s32[]{:S(2)}) async-start(), calls=%async_computation.10 | async-start | bytes 8650752 | tf_op jit(solution)/shard_map/all_gather | solution.py:90
  8.7 233.9 %all-gather.18.cloned.1.call-start = ((), (), s32[]{:S(2)}) async-start(), calls=%async_computation.11 | async-start | bytes 8650752 | tf_op jit(solution)/shard_map/all_gather | solution.py:92
  9.4 285.4 %all-gather.12.cloned.1.call-start = ((), (), s32[]{:S(2)}) async-start(), calls=%async_computation.8 | async-start | bytes 4718592 | tf_op jit(solution)/shard_map/all_gather | solution.py:135
  56.1 27.4 %copy-start.24 = (f32[1024]{0:T(1024)}, f32[1024]{0:T(1024)S(1)}, u32[]{:S(2)}) copy-start(f32[1024]{0:T(1024)S(1)} %convert_element_type.138) | copy-start | bytes 12292
  57.3 26.1 %copy-start.28 = (f32[256]{0:T(256)}, f32[256]{0:T(256)S(1)}, u32[]{:S(2)}) copy-start(f32[256]{0:T(256)S(1)} %get-tuple-element.364) | copy-start | bytes 3076
  58.7 24.8 %copy-start.30 = (f32[256]{0:T(256)}, f32[256]{0:T(256)S(1)}, u32[]{:S(2)}) copy-start(f32[256]{0:T(256)S(1)} %bitcast_rsqrt_fusion) | copy-start | bytes 3076
  60.1 32.7 %copy-start.22 = (f32[256,8]{0,1:T(8,128)}, f32[256,8]{0,1:T(8,128)S(1)}, u32[]{:S(2)}) copy-start(f32[256,8]{0,1:T(8,128)S(1)} %get-tuple-element.363) | copy-start | bytes 24580
  61.4 116.2 %copy-start.6 = (bf16[256,1024]{1,0:T(8,128)(2,1)}, bf16[256,1024]{1,0:T(8,128)(2,1)S(1)}, u32[]{:S(2)}) copy-start(bf16[256,1024]{1,0:T(8,128)(2,1)S(1)} %add_convert_fusion.2) | copy-start | bytes 1572868
  92.7 5.3 copy-start.37
  92.7 5.9 copy-start.39
  92.7 83.9 %copy-start.21 = (s32[2,1024]{1,0:T(2,128)S(1)}, s32[2,1024]{1,0:T(2,128)}, u32[]{:S(2)}) copy-start(s32[2,1024]{1,0:T(2,128)} %param.21) | copy-start | bytes 24580
  94.9 249.6 %all-gather.10.cloned.1.call-start = ((), (), s32[]{:S(2)}) async-start(), calls=%async_computation.7 | async-start | bytes 4718592 | tf_op jit(solution)/shard_map/all_gather | solution.py:136
  97.3 304.9 %all-gather.14.cloned.1.call-start = ((), (), s32[]{:S(2)}) async-start(), calls=%async_computation.9 | async-start | bytes 2162688 | tf_op jit(solution)/shard_map/all_gather | solution.py:88
  97.9 465.3 %reduce-scatter.19.cloned.1.call-start = ((), (), s32[]{:S(2)}) async-start(), calls=%async_computation.17 | async-start | bytes 4718592
  98.0 304.2 %copy-start.35 = (f32[256]{0:T(256)}, f32[256]{0:T(256)S(1)}, u32[]{:S(2)}) copy-start(f32[256]{0:T(256)S(1)} %broadcast_multiply_fusion) | copy-start | bytes 3076
  294.8 107.4 %copy-start.17 = (bf16[2,128,1024]{2,1,0:T(8,128)(2,1)S(1)}, bf16[2,128,1024]{2,1,0:T(8,128)(2,1)}, u32[]{:S(2)}) copy-start(bf16[2,128,1024]{2,1,0:T(8,128)(2,1)} %param.20) | copy-start | bytes 1572868
  344.6 57.6 %copy-start.4 = (bf16[2,128,1024]{2,1,0:T(8,128)(2,1)S(1)}, bf16[2,128,1024]{2,1,0:T(8,128)(2,1)}, u32[]{:S(2)}) copy-start(bf16[2,128,1024]{2,1,0:T(8,128)(2,1)} %param.19) | copy-start | bytes 1572868
  345.1 3.2 copy-start.3
  355.4 3.2 copy-start.3
  365.6 42.4 %copy-start.11 = (bf16[2,128,1024]{2,1,0:T(8,128)(2,1)}, bf16[2,128,1024]{2,1,0:T(8,128)(2,1)S(1)}, u32[]{:S(2)}) copy-start(bf16[2,128,1024]{2,1,0:T(8,128)(2,1)S(1)} %get-tuple-element.147) | copy-start | bytes 1572868
  402.2 5.0 copy-start.16
  408.2 4.2 copy-start.13
  420.4 3.2 copy-start.1
  440.8 5.4 copy-start.2
  448.3 4.4 copy-start.14
  452.7 4.2 copy-start.13
  464.9 3.2 copy-start.1
  485.3 5.4 copy-start.2
  492.8 4.5 copy-start.14
  514.2 99.5 %reduce-scatter.9.cloned.1.call-start = ((), (), s32[]{:S(2)}) async-start(), calls=%async_computation.12 | async-start | bytes 4718592 | tf_op jit(solution)/shard_map/reduce_scatter | solution.py:258
  515.0 242.5 %reduce-scatter.13.cloned.1.call-start = ((), (), s32[]{:S(2)}) async-start(), calls=%async_computation.14 | async-start | bytes 4325376 | tf_op jit(solution)/shard_map/reduce_scatter | solution.py:296
  518.2 397.9 %reduce-scatter.11.cloned.1.call-start = ((), (), s32[]{:S(2)}) async-start(), calls=%async_computation.13 | async-start | bytes 12976128 | tf_op jit(solution)/shard_map/reduce_scatter | solution.py:289
  520.5 94.5 %copy-start.23 = (f32[256,8]{0,1:T(8,128)S(1)}, f32[256,8]{0,1:T(8,128)}, u32[]{:S(2)}) copy-start(f32[256,8]{0,1:T(8,128)} %copy-done.22) | copy-start | bytes 24580
  520.5 94.5 %copy-start.27 = (f32[256,8]{0,1:T(8,128)S(1)}, f32[256,8]{0,1:T(8,128)}, u32[]{:S(2)}) copy-start(f32[256,8]{0,1:T(8,128)} %get-tuple-element.361) | copy-start | bytes 24580
  564.7 51.5 %copy-start.7 = (bf16[256,1024]{1,0:T(8,128)(2,1)S(1)}, bf16[256,1024]{1,0:T(8,128)(2,1)}, u32[]{:S(2)}) copy-start(bf16[256,1024]{1,0:T(8,128)(2,1)} %copy-done.6) | copy-start | bytes 1572868
  622.5 482.4 %reduce-scatter.15.cloned.1.call-start = ((), (), s32[]{:S(2)}) async-start(), calls=%async_computation.15 | async-start | bytes 17301504 | tf_op jit(solution)/shard_map/reduce_scatter | solution.py:298
  643.5 648.6 %reduce-scatter.17.cloned.1.call-start = ((), (), s32[]{:S(2)}) async-start(), calls=%async_computation.16 | async-start | bytes 17301504 | tf_op jit(solution)/shard_map/reduce_scatter | solution.py:300
  654.3 7.0 copy-start.5
  654.3 7.0 copy-start.25
  654.3 7.0 copy-start.29
  661.3 5.1 copy-start.26
  661.3 5.0 copy-start.34
  661.3 5.1 copy-start.31
  661.3 5.6 copy-start.10
  661.3 5.6 copy-start.18
  661.4 5.6 copy-start.36
  710.3 582.4 %copy-start.40 = (f32[32]{0:T(128)}, f32[32]{0:T(128)S(1)}, u32[]{:S(2)}) copy-start(f32[32]{0:T(128)S(1)} %dynamic-slice.4) | copy-start | bytes 388
  (13 other events, 22.4 us)
Sparse Core Ops, SparseCore 0:
  11.0 72.3 all-gather.7
  86.4 76.9 all-gather.15
  166.4 76.0 all-gather.17
  244.6 50.1 all-gather.11
  296.8 47.7 all-gather.9
  347.4 54.7 all-gather.13
  514.3 48.8 reduce-scatter.18
  565.5 48.1 reduce-scatter.8
  616.6 140.8 reduce-scatter.12
  763.9 152.2 reduce-scatter.10
  919.1 185.6 reduce-scatter.14
  1107.7 184.3 reduce-scatter.16
where the time goes:
time: 1310 us; the launch traced here: 1300 us
  waiting for transfers between devices  870 us (66%)
  blocking collectives  159 us (12%)
  matrix products  117 us (9%)
  local copies, waits for them, and re-layouts  115 us (9%)
  other arithmetic  19.7 us (2%)
  between operations  18.4 us (1%)
    reduce_scatter x1, waiting for transfers between devices, body(): lax.psum_scatter(up_wgrad, ('dp', 'ctx'), scatter_dimension=0, tiled=True)  189 us
    reduce_scatter x1, waiting for transfers between devices, body(): lax.psum_scatter(down_wgrad, ('dp', 'ctx'), scatter_dimension=0, tiled=True)  187 us
    reduce_scatter x1, waiting for transfers between devices, body(): lax.psum_scatter(qkv_wgrad, ('dp', 'ctx'), scatter_dimension=0, tiled=True)  159 us
    psum x2, blocking collectives, body(): lax.psum((jnp.sum(valid_rows), jnp.sum(valid_rows[:, None] * error * erro...  77.4 us
    all_gather x1, waiting for transfers between devices, body(): lax.all_gather(down_weight, ('dp', 'ctx'), axis=0, tiled=True)  49 us
    unnamed x13, waiting for transfers between devices  46.1 us
    reduce_scatter x1, waiting for transfers between devices, body(): lax.psum_scatter(value_terms.astype(jnp.bfloat16), 'ctx', scatter_dimensi...  45.9 us
    all_gather x1, waiting for transfers between devices, body(): lax.all_gather(key_low, 'ctx', axis=1, tiled=True)  45.9 us
  transfers between devices with their start and end apart: 12, of which 11 were waited for; matrix products, arithmetic and copies ran while one was open for 10% of the time, Pallas kernels for 0%

commit v1 on v0

v1 whole, which is shorter than its diff:
```python
import functools
import math

import jax
import jax.numpy as jnp
from jax import lax
from jax.experimental import pallas as pl
from jax.experimental.pallas import tpu as pltpu
from jax.sharding import PartitionSpec as P

HEADS = 16
ROT = 16
BLK = 128
NEG_FILL = -1000000000.0
F32 = jnp.float32
BF16 = jnp.bfloat16
VMEM_LIMIT = 56 * 1024 * 1024


def mm(a, b, dims=((1,), (0,))):
    return lax.dot_general(a, b, (dims, ((), ())), preferred_element_type=F32)


def block_spans(length, first_len):
    spans = []
    for start in range(0, length, BLK):
        low = 0 if start < first_len else first_len
        spans.append((start, low))
    return spans


def head_stack(rows, heads, size):
    lane = lax.broadcasted_iota(jnp.int32, rows.shape, 1) // size
    parts = [jnp.where(lane == h, rows, jnp.zeros_like(rows)) for h in range(heads)]
    return parts[0] if heads == 1 else jnp.concatenate(parts, axis=0)


def head_pick(stacked, heads, size):
    rows = stacked.shape[0] // heads
    out = stacked[:rows]
    lane = lax.broadcasted_iota(jnp.int32, out.shape, 1) // size
    for h in range(1, heads):
        out = jnp.where(lane == h, stacked[h * rows : (h + 1) * rows], out)
    return out


def turn(values, cosine, sine, size):
    half = ROT // 2
    width = values.shape[1]
    place = lax.broadcasted_iota(jnp.int32, values.shape, 1) % size
    partner = jnp.where(
        place < half,
        pltpu.roll(values, width - half, 1),
        pltpu.roll(values, half, 1),
    )
    return values * cosine + partner * sine


def span_mask(start, low, first_len, seg_col, seg_row, heads):
    stop = start + BLK
    shape = (BLK, stop - low)
    row = lax.broadcasted_iota(jnp.int32, shape, 0) + start
    col = lax.broadcasted_iota(jnp.int32, shape, 1) + low
    allowed = col <= row
    if low >= first_len:
        allowed = allowed & (seg_col[start:stop, :] == seg_row[:, low:stop])
    if heads > 1:
        allowed = jnp.concatenate([allowed.astype(jnp.int32)] * heads, axis=0) > 0
    return allowed


def attend_forward(
    first_len, heads, size, scale,
    x_ref, w_ref, b_ref, cos_ref, sin_ref, segc_ref, segr_ref,
    q_ref, k_ref, v_ref, o_ref, l_ref,
):
    length = x_ref.shape[1]
    width = heads * size
    step = min(256, length)
    for at in range(0, length, step):
        rows = slice(at, at + step)
        full = mm(x_ref[0, rows, :], w_ref[...]) + b_ref[...]
        cosine, sine = cos_ref[0, rows, :], sin_ref[0, rows, :]
        q_ref[0, rows, :] = (
            turn(full[:, :width], cosine, sine, size).astype(BF16) * jnp.asarray(scale, BF16)
        )
        k_ref[0, rows, :] = turn(full[:, width : 2 * width], cosine, sine, size).astype(BF16)
        v_ref[0, rows, :] = full[:, 2 * width :].astype(BF16)
    for start, low in block_spans(length, first_len):
        stop = start + BLK
        query = head_stack(q_ref[0, start:stop, :], heads, size)
        key, value = k_ref[0, low:stop, :], v_ref[0, low:stop, :]
        allowed = span_mask(start, low, first_len, segc_ref[0], segr_ref[0], heads)
        scores = jnp.where(allowed, mm(query, key, ((1,), (1,))), NEG_FILL)
        peak = jnp.max(scores, axis=1, keepdims=True)
        grown = jnp.exp(scores - peak)
        total = jnp.sum(grown, axis=1, keepdims=True)
        probs = (grown * (1.0 / total)).astype(BF16)
        mixed = mm(probs, value)
        o_ref[0, start:stop, :] = head_pick(mixed, heads, size).astype(BF16)
        stat = jnp.broadcast_to(peak + jnp.log(total), mixed.shape)
        l_ref[0, start:stop, :] = head_pick(stat, heads, size)


def attend_backward(
    first_len, heads, size, scale,
    q_ref, k_ref, v_ref, g_ref, l_ref, cos_ref, sin_ref, segc_ref, segr_ref,
    out_ref, dk_ref, dv_ref,
):
    length = q_ref.shape[1]
    width = heads * size
    dk_ref[...] = jnp.zeros_like(dk_ref)
    dv_ref[...] = jnp.zeros_like(dv_ref)
    for start, low in block_spans(length, first_len):
        stop = start + BLK
        query = head_stack(q_ref[0, start:stop, :], heads, size)
        grad = head_stack(g_ref[0, start:stop, :], heads, size)
        key, value = k_ref[0, low:stop, :], v_ref[0, low:stop, :]
        allowed = span_mask(start, low, first_len, segc_ref[0], segr_ref[0], heads)
        stat = l_ref[0, start:stop, :]
        stat = jnp.concatenate([stat[:, h * size : h * size + 1] for h in range(heads)], axis=0)
        scores = jnp.where(allowed, mm(query, key, ((1,), (1,))), NEG_FILL)
        probs = jnp.exp(scores - stat)
        prob_grad = mm(grad, value, ((1,), (1,)))
        delta = jnp.sum(probs * prob_grad, axis=1, keepdims=True)
        score_grad = (probs * (prob_grad - delta)).astype(BF16)
        dq = head_pick(mm(score_grad, key), heads, size) * scale
        cosine, sine = cos_ref[0, start:stop, :], sin_ref[0, start:stop, :]
        out_ref[0, start:stop, :width] = turn(dq, cosine, -sine, size).astype(BF16)
        dk_ref[low:stop, :] += mm(score_grad, query, ((0,), (0,)))
        dv_ref[low:stop, :] += mm(probs.astype(BF16), grad, ((0,), (0,)))
    out_ref[0, :, width : 2 * width] = turn(
        dk_ref[...], cos_ref[0], -sin_ref[0], size
    ).astype(BF16)
    out_ref[0, :, 2 * width :] = dv_ref[...].astype(BF16)


def seq_spec(*dims):
    return pl.BlockSpec((1,) + dims, lambda s: (s,) + (0,) * len(dims))


def whole_spec(*dims):
    return pl.BlockSpec(dims, lambda s: (0,) * len(dims))


def gather_dp(block, n_dp, me_dp):
    out = jnp.zeros((n_dp,) + block.shape, block.dtype)
    out = lax.dynamic_update_index_in_dim(out, block, me_dp, 0)
    for k in range(1, n_dp):
        pairs = [(i, i ^ k) for i in range(n_dp)]
        other = lax.ppermute(block, "dp", pairs)
        out = lax.dynamic_update_index_in_dim(out, other, me_dp ^ k, 0)
    return out.reshape((n_dp * block.shape[0],) + block.shape[1:])


def reduce_dp(terms, n_dp, me_dp):
    rows = terms.shape[0] // n_dp
    blocks = terms.reshape((n_dp, rows) + terms.shape[1:])
    total = lax.dynamic_index_in_dim(blocks, me_dp, 0, keepdims=False).astype(F32)
    low = blocks.astype(BF16)
    for k in range(1, n_dp):
        pairs = [(i, i ^ k) for i in range(n_dp)]
        block = lax.dynamic_index_in_dim(low, me_dp ^ k, 0, keepdims=False)
        total = total + lax.ppermute(block, "dp", pairs).astype(F32)
    return total


def body(
    n_dp, n_ctx,
    tokens, teacher, segments, positions, valid_mask,
    norm_gain, norm_bias, qkv_weight, qkv_bias, proj_weight, proj_bias,
    up_weight, up_bias, down_weight, down_bias,
):
    seqs, local_len, width = tokens.shape
    length = segments.shape[1]
    rows = seqs * local_len
    n_all = n_dp * n_ctx
    first_len = length // 2 + local_len
    heads = HEADS // n_ctx
    size = width // HEADS
    part = heads * size
    units = up_weight.shape[1] // n_ctx
    unit_rows = down_weight.shape[0]
    own = width // n_all
    scale = 1.0 / math.sqrt(size)
    me_dp = lax.axis_index("dp")
    me_ctx = lax.axis_index("ctx")
    both = ("dp", "ctx")

    tokens_all = lax.all_gather(tokens, "ctx", axis=1, tiled=True)

    valid_rows = valid_mask.reshape(rows).astype(F32)
    small = jnp.concatenate(
        [a.astype(F32) for a in (norm_gain, norm_bias, proj_bias, down_bias, qkv_bias, up_bias)]
        + [jnp.sum(valid_rows)[None]]
    )
    pad = -small.shape[0] % 128
    small = jnp.pad(small, (0, pad))
    small = lax.all_to_all(
        jnp.broadcast_to(small[None], (n_all, small.shape[0])), both, 0, 0, tiled=True
    )
    gain = small[:, :own].reshape(1, width)
    shift = small[:, own : 2 * own].reshape(1, width)
    out_bias = (small[:, 2 * own : 3 * own] + small[:, 3 * own : 4 * own]).reshape(1, width)
    at = 4 * own
    qkv_b = small[:, at : at + 3 * own].reshape(3, n_ctx, part)
    qkv_b = lax.dynamic_index_in_dim(qkv_b, me_ctx, 1, keepdims=False).reshape(1, 3 * part)
    at += 3 * own
    up_b = small[:, at : at + unit_rows].reshape(n_dp, n_ctx, unit_rows)
    up_b = lax.dynamic_index_in_dim(up_b, me_ctx, 1, keepdims=False).reshape(1, units)
    at += unit_rows
    valid_count = jnp.sum(small[:, at])

    qkv_cols = qkv_weight.reshape(own, 3, n_ctx, part).transpose(2, 0, 1, 3)
    up_cols = up_weight.reshape(own, n_dp, n_ctx, unit_rows).transpose(2, 0, 1, 3)
    cols = jnp.concatenate(
        [qkv_cols.reshape(n_ctx, own, 3 * part), up_cols.reshape(n_ctx, own, units)], axis=2
    )
    cols = lax.all_to_all(cols, "ctx", 0, 0, tiled=True).reshape(n_ctx * own, 3 * part + units)
    w_cols = gather_dp(cols, n_dp, me_dp)
    w_qkv, w_up = w_cols[:, : 3 * part], w_cols[:, 3 * part :]
    w_down = gather_dp(down_weight, n_dp, me_dp)
    to_plan = [(n_dp * j + i, i * n_ctx + j) for i in range(n_dp) for j in range(n_ctx)]
    from_plan = [(b, a) for a, b in to_plan]
    w_proj = gather_dp(lax.ppermute(proj_weight, both, to_plan), n_dp, me_dp)

    place = jnp.arange(length, dtype=jnp.int32)
    same = segments[:, :, None] == segments[:, None, :]
    before = place[None, None, :] < place[None, :, None]
    in_doc = jnp.sum((same & before).astype(F32), axis=2)
    half = ROT // 2
    lane = jnp.arange(part, dtype=jnp.int32) % size
    steps = jnp.arange(half, dtype=F32)
    inverse = jnp.power(10000.0, -2.0 * steps / ROT)
    lane_inverse = jnp.where(lane < ROT, inverse[lane % half], 0.0)
    angles = in_doc[:, :, None] * lane_inverse[None, None, :]
    cosine = jnp.cos(angles)
    sine = jnp.sin(angles) * jnp.where(lane < half, -1.0, 1.0)
    seg_col = segments[:, :, None]
    seg_row = segments[:, None, :]

    inputs_all = tokens_all.astype(F32)
    row_mean = jnp.mean(inputs_all, axis=-1, keepdims=True)
    centered = inputs_all - row_mean
    variance = jnp.mean(centered * centered, axis=-1, keepdims=True)
    normed = (centered * lax.rsqrt(variance + 1e-05) * gain + shift).astype(BF16)
    normed_rows = normed.reshape(seqs * length, width)

    params = pltpu.CompilerParams(vmem_limit_bytes=VMEM_LIMIT)
    head_shape = jax.ShapeDtypeStruct((seqs, length, part), BF16)
    query, key, value, mixed, stat = pl.pallas_call(
        functools.partial(attend_forward, first_len, heads, size, scale),
        grid=(seqs,),
        in_specs=[
            seq_spec(length, width),
            whole_spec(width, 3 * part),
            whole_spec(1, 3 * part),
            seq_spec(length, part),
            seq_spec(length, part),
            seq_spec(length, 1),
            seq_spec(1, length),
        ],
        out_specs=[seq_spec(length, part)] * 5,
        out_shape=[head_shape] * 4 + [jax.ShapeDtypeStruct((seqs, length, part), F32)],
        compiler_params=params,
        name="attend_forward",
    )(normed, w_qkv, qkv_b, cosine, sine, seg_col, seg_row)

    up = mm(normed_rows, w_up) + up_b
    cdf = 0.5 * (1.0 + lax.erf(up * math.sqrt(0.5)))
    act = (up * cdf).astype(BF16)
    gelu_slope = cdf + up * jnp.exp(-0.5 * up * up) * (1.0 / math.sqrt(2.0 * math.pi))
    mixed_rows = mixed.reshape(seqs * length, part)
    terms = mm(act, w_down) + mm(mixed_rows, w_proj)
    branch = lax.psum_scatter(
        terms.astype(BF16).reshape(seqs, length, width), "ctx", scatter_dimension=1, tiled=True
    )

    inputs = tokens.astype(F32)
    outputs = inputs + (branch.astype(F32) + out_bias)
    error = outputs - teacher.astype(F32)
    valid = valid_rows.reshape(seqs, local_len, 1)
    square = jnp.sum(valid * error * error)
    total_tokens = seqs * n_dp * length
    out_grad = (total_tokens / valid_count) * (valid * error)
    branch_low = out_grad.astype(BF16)
    branch_sum = jnp.sum(branch_low, axis=(0, 1), dtype=F32)
    layer_out = outputs.astype(BF16)

    grad_rows = lax.all_gather(branch_low, "ctx", axis=1, tiled=True).reshape(
        seqs * length, width
    )
    act_grad = mm(grad_rows, w_down, ((1,), (1,)))
    up_grad = (act_grad * gelu_slope).astype(BF16)
    mixed_grad = mm(grad_rows, w_proj, ((1,), (1,))).astype(BF16)
    qkv_grad = pl.pallas_call(
        functools.partial(attend_backward, first_len, heads, size, scale),
        grid=(seqs,),
        in_specs=[seq_spec(length, part)] * 7 + [seq_spec(length, 1), seq_spec(1, length)],
        out_specs=seq_spec(length, 3 * part),
        out_shape=jax.ShapeDtypeStruct((seqs, length, 3 * part), BF16),
        scratch_shapes=[pltpu.VMEM((length, part), F32), pltpu.VMEM((length, part), F32)],
        compiler_params=params,
        name="attend_backward",
    )(
        query, key, value, mixed_grad.reshape(seqs, length, part), stat,
        cosine, sine, seg_col, seg_row,
    ).reshape(seqs * length, 3 * part)
    back = mm(up_grad, w_up, ((1,), (1,))) + mm(qkv_grad, w_qkv, ((1,), (1,)))
    normed_grad = lax.psum_scatter(
        back.astype(BF16).reshape(seqs, length, width), "ctx", scatter_dimension=1, tiled=True
    ).astype(F32)

    first = ((0,), (0,))
    down_wgrad = reduce_dp(mm(act, grad_rows, first), n_dp, me_dp)
    proj_wgrad = reduce_dp(mm(mixed_rows, grad_rows, first), n_dp, me_dp)
    proj_wgrad = lax.ppermute(proj_wgrad.astype(BF16), both, from_plan).astype(F32)
    col_wgrad = jnp.concatenate(
        [mm(normed_rows, qkv_grad, first), mm(normed_rows, up_grad, first)], axis=1
    )
    col_wgrad = reduce_dp(col_wgrad, n_dp, me_dp).astype(BF16)
    col_wgrad = lax.all_to_all(
        col_wgrad.reshape(n_ctx, own, 3 * part + units), "ctx", 0, 0, tiled=True
    )
    qkv_wgrad = (
        col_wgrad[:, :, : 3 * part].reshape(n_ctx, own, 3, part).transpose(1, 2, 0, 3)
    ).reshape(own, 3 * width).astype(F32)
    up_wgrad = (
        col_wgrad[:, :, 3 * part :].reshape(n_ctx, own, n_dp, unit_rows).transpose(1, 2, 0, 3)
    ).reshape(own, n_ctx * units).astype(F32)

    row_mean = jnp.mean(inputs, axis=-1, keepdims=True)
    centered = inputs - row_mean
    variance = jnp.mean(centered * centered, axis=-1, keepdims=True)
    root = lax.rsqrt(variance + 1e-05)
    standard = centered * root
    gain_sum = jnp.sum(normed_grad * standard, axis=(0, 1))
    shift_sum = jnp.sum(normed_grad, axis=(0, 1))
    inner = normed_grad * gain
    input_part = root * (
        inner
        - jnp.mean(inner, axis=-1, keepdims=True)
        - standard * jnp.mean(inner * standard, axis=-1, keepdims=True)
    )
    input_grad = (out_grad + input_part).astype(BF16)

    qkv_bsum = jnp.sum(qkv_grad, axis=0, dtype=F32).reshape(3, 1, part)
    qkv_bsum = lax.dynamic_update_slice(
        jnp.zeros((3, n_ctx, part), F32), qkv_bsum, (0, me_ctx, 0)
    )
    up_bsum = jnp.sum(up_grad, axis=0, dtype=F32).reshape(n_dp, 1, unit_rows)
    up_bsum = lax.dynamic_update_slice(
        jnp.zeros((n_dp, n_ctx, unit_rows), F32), up_bsum, (0, me_ctx, 0)
    )
    sums = jnp.concatenate(
        [
            gain_sum.reshape(n_all, own),
            shift_sum.reshape(n_all, own),
            branch_sum.reshape(n_all, own),
            qkv_bsum[2].reshape(n_all, own),
            qkv_bsum[:2].reshape(n_all, 2 * own),
            up_bsum.reshape(n_all, unit_rows),
            jnp.broadcast_to(square, (n_all, 1)),
        ],
        axis=1,
    )
    sums = jnp.pad(sums, ((0, 0), (0, -sums.shape[1] % 128)))
    sums = jnp.sum(lax.all_to_all(sums, both, 0, 0, tiled=True), axis=0)
    gain_grad, shift_grad, bias_grad, value_bgrad = (
        sums[k * own : (k + 1) * own] for k in range(4)
    )
    qk_bgrad = sums[4 * own : 6 * own]
    up_bgrad = sums[6 * own : 6 * own + unit_rows]
    loss = sums[6 * own + unit_rows] / (valid_count * width)
    return (
        layer_out, loss, input_grad, gain_grad, shift_grad, qkv_wgrad, qk_bgrad, value_bgrad,
        proj_wgrad, bias_grad, up_wgrad, up_bgrad, down_wgrad, bias_grad,
    )


def solution(mesh):
    n_dp, n_ctx = mesh.shape["dp"], mesh.shape["ctx"]
    seq, flat = P("dp", "ctx", None), P(("dp", "ctx"))
    mat = P(("dp", "ctx"), None)
    in_specs = (
        seq, seq, P("dp", None), P("dp", "ctx"), P("dp", "ctx"),
        flat, flat, mat, flat, mat, flat, mat, flat, mat, flat,
    )
    out_specs = (seq, P(), seq, flat, flat, mat, flat, flat, mat, flat, mat, flat, mat, flat)
    return jax.shard_map(
        functools.partial(body, n_dp, n_ctx),
        mesh=mesh, in_specs=in_specs, out_specs=out_specs, check_vma=False,
    )
```

time: 1310 us -> 372 us (0.28)
  waiting for transfers between devices: 870 us -> 143 us
  blocking collectives: 159 us -> 0 us
  local copies, waits for them, and re-layouts: 115 us -> 45.4 us
  matrix products: 117 us -> 49.6 us
  starting transfers between devices: 0.94 us -> 48.9 us
  Pallas kernels: 0 us -> 23.4 us
  other arithmetic: 19.7 us -> 38.9 us
    reduce_scatter x5 -> x2, waiting for transfers between devices: 626 us -> 45.6 us  [the longest x1 45.6 us: body(): lax.psum_scatter(terms.astype(BF16).reshape(seqs, length, width), 'ctx',...]
    all_gather x6 -> x2, waiting for transfers between devices: 198 us -> 45.2 us  [the longest x1 45.2 us: body(): lax.all_gather(branch_low, 'ctx', axis=1, tiled=True)]
    psum x2 -> x0, blocking collectives: 77.4 us -> none  [body(): lax.psum((jnp.sum(valid_rows), jnp.sum(valid_rows[:, None] * error * erro...]
    dot_general x26 -> x11, matrix products: 117 us -> 49.6 us  [mm(): return lax.dot_general(a, b, (dims, ((), ())), preferred_element_type=F32)]
    unnamed x13 -> x4, waiting for transfers between devices: 46.1 us -> 0.73 us
    unnamed x1 -> x0, blocking collectives: 42.4 us -> none
    ppermute x0 -> x20, waiting for transfers between devices: none -> 40.2 us  [the longest x9 24.1 us: gather_dp(): other = lax.ppermute(block, 'dp', pairs)]
    all_gather x1 -> x0, blocking collectives: 39 us -> none  [body(): lax.all_gather(up_bias, ('dp', 'ctx'), axis=0, tiled=True)]
  transfers between devices with their start and end apart: 12 -> 28, of which waited for: 11 -> 11; matrix products, arithmetic and copies ran while one was open for 10% -> 22% of each run, Pallas kernels for 0% -> 0%
where the time goes in v1:
time: 372 us; the launch traced here: 368 us
  waiting for transfers between devices  143 us (38%)
  matrix products  49.6 us (13%)
  starting transfers between devices  48.9 us (13%)
  local copies, waits for them, and re-layouts  45.4 us (12%)
  other arithmetic  38.9 us (10%)
  Pallas kernels  23.4 us (6%)
  between operations  18 us (5%)
    dot_general x11, matrix products, mm(): return lax.dot_general(a, b, (dims, ((), ())), preferred_element_type=F32)  49.6 us
    reduce_scatter x1, waiting for transfers between devices, body(): lax.psum_scatter(terms.astype(BF16).reshape(seqs, length, width), 'ctx',...  45.6 us
    all_gather x1, waiting for transfers between devices, body(): lax.all_gather(branch_low, 'ctx', axis=1, tiled=True)  45.2 us
    ppermute x9, waiting for transfers between devices, gather_dp(): other = lax.ppermute(block, 'dp', pairs)  24.1 us
    ppermute x9, waiting for transfers between devices, reduce_dp(): total = total + lax.ppermute(block, 'dp', pairs).astype(F32)  16.1 us
    ppermute x9, starting transfers between devices, gather_dp(): other = lax.ppermute(block, 'dp', pairs)  15.1 us
    pallas_call x1, Pallas kernels, body(): pl.pallas_call(functools.partial(attend_backward, first_len, heads, size,...  11.9 us
    pallas_call x1, Pallas kernels, body(): pl.pallas_call(functools.partial(attend_forward, first_len, heads, size,...  11.5 us
  transfers between devices with their start and end apart: 28, of which 11 were waited for; matrix products, arithmetic and copies ran while one was open for 22% of the time, Pallas kernels for 0%

profile of v1, /device:TPU:0, one launch (start us, length us, event | category | flops | bytes accessed | tf_op | source)
XLA Modules:
  0.0 367.5 jit_solution(11913793321401290617)
XLA Ops:
  7.9 3.0 collective-permute-start.3
  13.8 4.7 %concatenate.12 = f32[353]{0:T(512)S(1)} concatenate(bf16[32]{0:T(256)(128)(2,1)} %param.19, bf16[32]{0:T(256)(128)(2,1)} %param.20, bf16[32]{0:T(256)(128)(2,1)} %param.24, bf16[32]{0:T(256)(128)(2,1)} %param.28, bf16[96]{0:T(256)(128)(2,1)} %param.22, bf16[128]{0:T(256)(128)(2,1)} %param.26, f32[1]{0:T(128)} %bitcast), dimensions={0} | concatenate | bytes 2120 | tf_op jit(solution)/shard_map/concatenate | solution.py:193
  19.2 6.3 %all-to-all-start = ((f32[32,1,384]{2,1,0:T(1,128)}), f32[32,1,384]{2,1,0:T(1,128)S(1)}, u32[]{:S(2)}, u32[]{:S(2)}) async-start(f32[32,1,384]{2,1,0:T(1,128)} %broadcast_in_dim.99), calls=%async_computation | async-start | bytes 98304 | tf_op jit(solution)/shard_map/all_to_all | solution.py:199
  30.7 2.0 copy.64.segc_ref
  33.4 5.2 %compare_select_fusion.9 = (f32[128]{0:T(128)S(1)}, f32[128]{0:T(128)S(1)}) fusion(f32[]{:T(128)} %bitcast.26, f32[]{:T(128)} %bitcast.25, f32[]{:T(128)} %bitcast.24, f32[]{:T(128)} %bitcast.23, f32[]{:T(128)} %bitcast.22, f32[]{:T(128)} %bitcast.21, f32[]{:T(128)} %bitcast.20, f32[]{:T(128)} %bitcast.19), kind=kLoop, calls=%fused_computation.124 | loop fusion | flops 5632 | bytes 1056 | tf_op jit(solution)/shard_map/jit(_where)/select_n | solution.py:238
  39.1 2.2 convert_reduce_fusion.1
  41.3 5.7 %fusion.30 = (f32[2,1024,128]{2,1,0:T(8,128)}, f32[2,1024,128]{2,1,0:T(8,128)}) fusion(f32[128]{0:T(128)S(1)} %get-tuple-element.68, f32[128]{0:T(128)S(1)} %get-tuple-element.69, f32[2,1024]{1,0:T(2,128)S(1)} %convert_reduce_fusion.1), kind=kLoop, calls=%fused_computation.56 | loop fusion | flops 524288 | bytes 2106368 | tf_op jit(solution)/shard_map/mul | solution.py:238
  47.8 3.7 collective-permute-start.7
  51.5 3.3 collective-permute-start.8
  54.8 3.5 all-to-all-start.1
  60.0 5.2 %collective-permute-done.9 = bf16[32,1024]{1,0:T(8,128)(2,1)S(1)} collective-permute-done((bf16[32,1024]{1,0:T(8,128)(2,1)S(1)}, bf16[32,1024]{1,0:T(8,128)(2,1)S(1)}, u32[]{:S(2)}, u32[]{:S(2)}) %collective-permute-start.9) | collective-permute-done | bytes 65568 | tf_op jit(solution)/shard_map/ppermute | solution.py:151
  65.2 7.0 %all-to-all-done.1 = bf16[8,32,896]{2,1,0:T(8,128)(2,1)S(1)} async-done(((bf16[8,32,896]{2,1,0:T(8,128)(2,1)}), bf16[8,32,896]{2,1,0:T(8,128)(2,1)S(1)}, u32[]{:S(2)}, u32[]{:S(2)}) %all-to-all-start.1) | async-done | bytes 458784 | tf_op jit(solution)/shard_map/all_to_all | solution.py:219
  73.2 2.7 collective-permute-start.2
  76.1 9.5 %collective-permute-done = bf16[256,896]{1,0:T(8,128)(2,1)S(1)} collective-permute-done((bf16[256,896]{1,0:T(8,128)(2,1)S(1)}, bf16[256,896]{1,0:T(8,128)(2,1)S(1)}, u32[]{:S(2)}, u32[]{:S(2)}) %collective-permute-start) | collective-permute-done | bytes 458784 | tf_op jit(solution)/shard_map/ppermute | solution.py:151
  85.7 9.3 %collective-permute-done.1 = bf16[256,896]{1,0:T(8,128)(2,1)S(1)} collective-permute-done((bf16[256,896]{1,0:T(8,128)(2,1)S(1)}, bf16[256,896]{1,0:T(8,128)(2,1)S(1)}, u32[]{:S(2)}, u32[]{:S(2)}) %collective-permute-start.1) | collective-permute-done | bytes 458784 | tf_op jit(solution)/shard_map/ppermute | solution.py:151
  96.2 3.0 convert_reduce_fusion
  102.8 4.1 %fusion.15 = (bf16[512,2048]{1,0:T(8,128)(2,1)}, f32[2048,512]{0,1:T(8,128)S(1)}) fusion(f32[512]{0:T(512)S(1)} %bitcast.216, bf16[2048,1024]{1,0:T(8,128)(2,1)S(1)} %bitcast.173, bf16[1024,896]{1,0:T(8,128)(2,1)S(1)} %bitcast.182), kind=kOutput, calls=%fused_computation.27 | convolution fusion | flops 2153775104 | bytes 11536384 | tf_op jit(solution)/shard_map/dot_general | solution.py:21
  107.0 4.9 %fusion.16 = f32[2048,1024]{1,0:T(8,128)} fusion(bf16[512,1024]{1,0:T(8,128)(2,1)S(1)} %bitcast.200, f32[2048,512]{0,1:T(8,128)S(1)} %get-tuple-element.65, f32[512]{0:T(512)S(1)} %bitcast.217), kind=kOutput, calls=%fused_computation.31 | convolution fusion | flops 2153775104 | bytes 13633536 | tf_op jit(solution)/shard_map/dot_general | solution.py:21
  111.9 11.5 %attend_forward.1 = (bf16[2,1024,128]{2,1,0:T(8,128)(2,1)}, bf16[2,1024,128]{2,1,0:T(8,128)(2,1)}, bf16[2,1024,128]{2,1,0:T(8,128)(2,1)}, bf16[2,1024,128]{2,1,0:T(8,128)(2,1)}, f32[2,1024,128]{2,1,0:T(8,128)}) custom-call(bf16[2,1024,1024]{2,1,0:T(8,128)(2,1)} %copy-done.1, bf16[1024,384]{1,0:T(8,128)(2,1)} %slice.93.w_ref, f32[1,384]{1,0:T(1,128)} %fusion.46.b_ref, ...), custom_call_target="tpu_custom_call" | custom-call | tf_op jit(solution)/shard_map/attend_forward/pallas_call | solution.py:251
  123.4 6.8 %add_convert_fusion.1 = bf16[2048,1024]{1,0:T(8,128)(2,1)} fusion(f32[2048,1024]{1,0:T(8,128)} %fusion.16, bf16[2048,128]{1,0:T(8,128)(2,1)} %bitcast.187, bf16[128,1024]{1,0:T(8,128)(2,1)S(1)} %bitcast.198), kind=kOutput, calls=%fused_computation.9 | convolution fusion | flops 541065216 | bytes 13369344 | tf_op jit(solution)/shard_map/dot_general | solution.py:21
  132.8 45.6 %reduce-scatter.3.cloned.1.call-done = bf16[2,128,1024]{2,1,0:T(8,128)(2,1)} async-done(((bf16[2,1024,1024]{2,1,0:T(8,128)(2,1)}), bf16[2,128,1024]{2,1,0:T(8,128)(2,1)}) %reduce-scatter.3.cloned.1.call-update) | async-done | bytes 524304 | tf_op jit(solution)/shard_map/reduce_scatter | solution.py:275
  178.5 2.3 convert_reduce_fusion.6
  181.1 45.2 %all-gather.5.cloned.1.call-done = bf16[2,1024,1024]{2,1,0:T(8,128)(2,1)} async-done(((bf16[2,128,1024]{2,1,0:T(8,128)(2,1)}), bf16[2,1024,1024]{2,1,0:T(8,128)(2,1)}) %all-gather.5.cloned.1.call-update) | async-done | bytes 4194320 | tf_op jit(solution)/shard_map/all_gather | solution.py:290
  226.3 4.4 %convolution_convert_fusion = bf16[2048,128]{1,0:T(8,128)(2,1)} fusion(bf16[2048,1024]{1,0:T(8,128)(2,1)} %bitcast.177, bf16[128,1024]{1,0:T(8,128)(2,1)S(1)} %bitcast.199), kind=kOutput, calls=%fused_computation.30 | convolution fusion | flops 537133056 | bytes 4980736 | tf_op jit(solution)/shard_map/dot_general | solution.py:21
  230.7 6.2 %convert_reduce_fusion.2 = (f32[512]{0:T(512)}, bf16[2048,512]{0,1:T(8,128)(2,1)S(1)}) fusion(f32[2048,512]{0,1:T(8,128)} %copy-done.27, f32[512]{0:T(512)S(1)} %bitcast.218, bf16[2048,1024]{1,0:T(8,128)(2,1)S(1)} %bitcast.179, bf16[512,1024]{1,0:T(8,128)(2,1)S(1)} %bitcast.201), kind=kOutput, calls=%fused_computation.23 | convolution fusion | flops 2161114624 | bytes 11538432 | tf_op jit(solution)/shard_map/dot_general | solution.py:21
  236.9 11.9 %attend_backward.1 = bf16[2,1024,384]{2,1,0:T(8,128)(2,1)} custom-call(bf16[2,1024,128]{2,1,0:T(8,128)(2,1)} %get-tuple-element.20.q_ref, bf16[2,1024,128]{2,1,0:T(8,128)(2,1)} %get-tuple-element.21.k_ref, bf16[2,1024,128]{2,1,0:T(8,128)(2,1)} %get-tuple-element.22.v_ref, bf16[2,1024,128]{2,1,0:T(8,128)(2,1)} %bitcast.209, ...), custom_call_target="tpu_custom_call" | custom-call | tf_op jit(solution)/shard_map/attend_backward/pallas_call | solution.py:296
  248.8 3.8 %fusion.49 = f32[2048,1024]{1,0:T(8,128)S(1)} fusion(bf16[2048,384]{1,0:T(8,128)(2,1)} %bitcast.176, bf16[1024,896]{1,0:T(8,128)(2,1)S(1)} %bitcast.183), kind=kOutput, calls=%fused_computation.138 | convolution fusion | flops 1610612736 | bytes 10747904 | tf_op jit(solution)/shard_map/dot_general | solution.py:21
  252.6 4.6 %add_convert_fusion = bf16[2048,1024]{1,0:T(8,128)(2,1)} fusion(f32[2048,1024]{1,0:T(8,128)S(1)} %fusion.49, bf16[2048,512]{0,1:T(8,128)(2,1)S(1)} %get-tuple-element.61, bf16[1024,896]{1,0:T(8,128)(2,1)S(1)} %bitcast.184), kind=kOutput, calls=%fused_computation.8 | convolution fusion | flops 2151677952 | bytes 15728640 | tf_op jit(solution)/shard_map/dot_general | solution.py:21
  260.5 4.5 %convolution_bitcast_fusion = f32[1024,384]{0,1:T(8,128)S(1)} fusion(bf16[2,1024,1024]{2,1,0:T(8,128)(2,1)} %copy-done.1, bf16[2,1024,384]{2,1,0:T(8,128)(2,1)S(1)} %copy-done.3), kind=kOutput, calls=%fused_computation.43 | convolution fusion | flops 1610612736 | bytes 7340032 | tf_op jit(solution)/shard_map/dot_general | solution.py:21
  265.1 2.3 fusion.56
  267.4 2.3 pad_maximum_fusion
  269.7 5.3 %reshape.302 = f32[4,256,896]{1,0,2:T(4,128)} reshape(f32[1024,896]{0,1:T(8,128)} %pad_maximum_fusion) | data formatting | bytes 7340032 | tf_op jit(solution)/shard_map/reshape | solution.py:158
  275.0 4.5 %copy.69 = bf16[4,256,896]{2,1,0:T(8,128)(2,1)} copy(f32[4,256,896]{1,0,2:T(4,128)} %reshape.302) | data formatting | bytes 5505024 | tf_op jit(solution)/shard_map/reshape | solution.py:158
  279.6 2.9 constant_dynamic-slice_fusion
  282.4 2.7 copy.68
  286.6 2.4 collective-permute-start.12
  290.2 3.9 %fusion.54 = (bf16[4,32,1024]{2,1,0:T(8,128)(2,1)S(1)}, f32[4,32,1024]{2,1,0:T(8,128)}) fusion(bf16[4,32,2048]{2,1,0:T(8,128)(2,1)} %bitcast.186, bf16[2048,1024,1]{1,0,2:T(8,128)(2,1)} %bitcast.178), kind=kOutput, calls=%fused_computation.142 | convolution fusion | flops 537001984 | bytes 5505024 | tf_op jit(solution)/shard_map/dot_general | solution.py:21
  294.8 2.4 collective-permute-start.15
  297.7 4.0 %fusion.55 = (bf16[4,128,1024]{2,1,0:T(8,128)(2,1)}, f32[4,128,1024]{2,1,0:T(8,128)}) fusion(bf16[4,128,2048]{2,1,0:T(8,128)(2,1)S(1)} %bitcast.220, bf16[2048,1024,1]{1,0,2:T(8,128)(2,1)S(1)} %bitcast.180), kind=kOutput, calls=%fused_computation.143 | convolution fusion | flops 2148007936 | bytes 9437184 | tf_op jit(solution)/shard_map/dot_general | solution.py:21
  302.4 8.4 %collective-permute-done.11 = bf16[256,896]{1,0:T(8,128)(2,1)S(1)} collective-permute-done((bf16[256,896]{1,0:T(8,128)(2,1)S(1)}, bf16[256,896]{1,0:T(8,128)(2,1)S(1)}, u32[]{:S(2)}, u32[]{:S(2)}) %collective-permute-start.11) | collective-permute-done | bytes 458784 | tf_op jit(solution)/shard_map/ppermute | solution.py:164
  311.8 3.5 all-to-all-start.3
  317.3 2.4 collective-permute-start.19
  327.7 5.4 %collective-permute-done.18 = bf16[128,1024]{1,0:T(8,128)(2,1)} collective-permute-done((bf16[128,1024]{1,0:T(8,128)(2,1)}, bf16[128,1024]{1,0:T(8,128)(2,1)}, u32[]{:S(2)}, u32[]{:S(2)}) %collective-permute-start.18) | collective-permute-done | bytes 262176 | tf_op jit(solution)/shard_map/ppermute | solution.py:164
  333.4 2.3 fusion.42
  338.6 2.6 fusion.29
  342.8 6.0 %all-to-all-start.2 = ((f32[32,1,384]{2,1,0:T(1,128)}), f32[32,1,384]{2,1,0:T(1,128)S(1)}, u32[]{:S(2)}, u32[]{:S(2)}) async-start(f32[32,1,384]{2,1,0:T(1,128)} %all_to_all.21), calls=%async_computation.4 | async-start | bytes 98304 | tf_op jit(solution)/shard_map/all_to_all | solution.py:368
  348.8 2.7 fusion.27
  351.5 4.6 %all-to-all-done.2 = f32[32,1,384]{2,1,0:T(1,128)S(1)} async-done(((f32[32,1,384]{2,1,0:T(1,128)}), f32[32,1,384]{2,1,0:T(1,128)S(1)}, u32[]{:S(2)}, u32[]{:S(2)}) %all-to-all-start.2) | async-done | bytes 49184 | tf_op jit(solution)/shard_map/all_to_all | solution.py:368
  (185 shorter events, 46.6 us)
Async XLA Ops:
  7.2 31.9 %copy-start.16 = (bf16[128,1024]{1,0:T(8,128)(2,1)S(1)}, bf16[128,1024]{1,0:T(8,128)(2,1)}, u32[]{:S(2)}) copy-start(bf16[128,1024]{1,0:T(8,128)(2,1)} %param.27) | copy-start | bytes 786436
  7.2 31.9 %copy-start.17 = (s32[2,1024]{1,0:T(2,128)S(1)}, s32[2,1024]{1,0:T(2,128)}, u32[]{:S(2)}) copy-start(s32[2,1024]{1,0:T(2,128)} %param.17) | copy-start | bytes 24580
  7.2 89.0 %all-gather.3.cloned.1.call-start = ((), (), s32[]{:S(2)}) async-start(), calls=%async_computation.6 | async-start | bytes 4718592 | tf_op jit(solution)/shard_map/all_gather | solution.py:190
  7.9 57.3 %collective-permute-start.3 = (bf16[128,1024]{1,0:T(8,128)(2,1)}, bf16[128,1024]{1,0:T(8,128)(2,1)S(1)}, u32[]{:S(2)}, u32[]{:S(2)}) collective-permute-start(bf16[128,1024]{1,0:T(8,128)(2,1)} %param.27), channel_id=1, source_target_pairs={{0,8},{8,0},{16,24},{24,16},{1,9},{9,1},{17,25},{25,17},{2,10},{10... | collective-permute-start | bytes 786440 | tf_op jit(solution)/shard_map/ppermute | solution.py:151
  10.9 62.1 %collective-permute-start.4 = (bf16[128,1024]{1,0:T(8,128)(2,1)}, bf16[128,1024]{1,0:T(8,128)(2,1)S(1)}, u32[]{:S(2)}, u32[]{:S(2)}) collective-permute-start(bf16[128,1024]{1,0:T(8,128)(2,1)} %param.27), channel_id=1, source_target_pairs={{0,16},{8,24},{16,0},{24,8},{1,17},{9,25},{17,1},{25,9},{2,18},{10... | collective-permute-start | bytes 786440 | tf_op jit(solution)/shard_map/ppermute | solution.py:151
  12.5 60.7 %collective-permute-start.5 = (bf16[128,1024]{1,0:T(8,128)(2,1)}, bf16[128,1024]{1,0:T(8,128)(2,1)S(1)}, u32[]{:S(2)}, u32[]{:S(2)}) collective-permute-start(bf16[128,1024]{1,0:T(8,128)(2,1)} %param.27), channel_id=1, source_target_pairs={{0,24},{8,16},{16,8},{24,0},{1,25},{9,17},{17,9},{25,1},{2,26},{10... | collective-permute-start | bytes 786440 | tf_op jit(solution)/shard_map/ppermute | solution.py:151
  19.2 35.7 %all-to-all-start = ((f32[32,1,384]{2,1,0:T(1,128)}), f32[32,1,384]{2,1,0:T(1,128)S(1)}, u32[]{:S(2)}, u32[]{:S(2)}) async-start(f32[32,1,384]{2,1,0:T(1,128)} %broadcast_in_dim.99), calls=%async_computation | async-start | bytes 98304 | tf_op jit(solution)/shard_map/all_to_all | solution.py:199
  25.5 22.3 %collective-permute-start.6 = (bf16[32,1024]{1,0:T(8,128)(2,1)}, bf16[32,1024]{1,0:T(8,128)(2,1)S(1)}, u32[]{:S(2)}, u32[]{:S(2)}) collective-permute-start(bf16[32,1024]{1,0:T(8,128)(2,1)} %param.23), channel_id=1, source_target_pairs={{0,0},{4,1},{8,2},{12,3},{16,4},{20,5},{24,6},{28,7},{1,8},{5,9},{... | collective-permute-start | bytes 196616 | tf_op jit(solution)/shard_map/ppermute | solution.py:225
  47.8 12.1 %collective-permute-start.7 = (bf16[32,1024]{1,0:T(8,128)(2,1)S(1)}, bf16[32,1024]{1,0:T(8,128)(2,1)S(1)}, u32[]{:S(2)}, u32[]{:S(2)}) collective-permute-start(bf16[32,1024]{1,0:T(8,128)(2,1)S(1)} %collective-permute-done.6), channel_id=1, source_target_pairs={{0,8},{8,0},{16,24},{24,16},{1,9},{9,1},{17,25},{25,17},{2,10},{10... | collective-permute-start | bytes 196616 | tf_op jit(solution)/shard_map/ppermute | solution.py:151
  51.5 8.5 %collective-permute-start.8 = (bf16[32,1024]{1,0:T(8,128)(2,1)S(1)}, bf16[32,1024]{1,0:T(8,128)(2,1)S(1)}, u32[]{:S(2)}, u32[]{:S(2)}) collective-permute-start(bf16[32,1024]{1,0:T(8,128)(2,1)S(1)} %collective-permute-done.6), channel_id=1, source_target_pairs={{0,16},{8,24},{16,0},{24,8},{1,17},{9,25},{17,1},{25,9},{2,18},{10... | collective-permute-start | bytes 196616 | tf_op jit(solution)/shard_map/ppermute | solution.py:151
  54.8 17.4 %all-to-all-start.1 = ((bf16[8,32,896]{2,1,0:T(8,128)(2,1)}), bf16[8,32,896]{2,1,0:T(8,128)(2,1)S(1)}, u32[]{:S(2)}, u32[]{:S(2)}) async-start(bf16[8,32,896]{2,1,0:T(8,128)(2,1)} %pad_maximum_fusion.1), calls=%async_computation.1 | async-start | bytes 917504 | tf_op jit(solution)/shard_map/all_to_all | solution.py:219
  58.3 120.2 %reduce-scatter.3.cloned.1.call-start = ((), (), s32[]{:S(2)}) async-start(), calls=%async_computation.7 | async-start | bytes 4718592 | tf_op jit(solution)/shard_map/reduce_scatter | solution.py:275
  59.3 47.6 %copy-start.20 = (f32[4,1,128]{2,1,0:T(1,128)}, f32[4,1,128]{2,1,0:T(1,128)S(1)}, u32[]{:S(2)}) copy-start(f32[4,1,128]{2,1,0:T(1,128)S(1)} %constant_dynamic-slice_fusion.2) | copy-start | bytes 6148
  59.9 5.3 %collective-permute-start.9 = (bf16[32,1024]{1,0:T(8,128)(2,1)S(1)}, bf16[32,1024]{1,0:T(8,128)(2,1)S(1)}, u32[]{:S(2)}, u32[]{:S(2)}) collective-permute-start(bf16[32,1024]{1,0:T(8,128)(2,1)S(1)} %collective-permute-done.6), channel_id=1, source_target_pairs={{0,24},{8,16},{16,8},{24,0},{1,25},{9,17},{17,9},{25,1},{2,26},{10... | collective-permute-start | bytes 196616 | tf_op jit(solution)/shard_map/ppermute | solution.py:151
  72.2 13.4 %collective-permute-start = (bf16[256,896]{1,0:T(8,128)(2,1)S(1)}, bf16[256,896]{1,0:T(8,128)(2,1)S(1)}, u32[]{:S(2)}, u32[]{:S(2)}) collective-permute-start(bf16[256,896]{1,0:T(8,128)(2,1)S(1)} %bitcast.192), channel_id=1, source_target_pairs={{0,8},{8,0},{16,24},{24,16},{1,9},{9,1},{17,25},{25,17},{2,10},{10... | collective-permute-start | bytes 1376264 | tf_op jit(solution)/shard_map/ppermute | solution.py:151
  73.0 22.0 %collective-permute-start.1 = (bf16[256,896]{1,0:T(8,128)(2,1)S(1)}, bf16[256,896]{1,0:T(8,128)(2,1)S(1)}, u32[]{:S(2)}, u32[]{:S(2)}) collective-permute-start(bf16[256,896]{1,0:T(8,128)(2,1)S(1)} %bitcast.193), channel_id=1, source_target_pairs={{0,16},{8,24},{16,0},{24,8},{1,17},{9,25},{17,1},{25,9},{2,18},{10... | collective-permute-start | bytes 1376264 | tf_op jit(solution)/shard_map/ppermute | solution.py:151
  73.2 21.9 %collective-permute-start.2 = (bf16[256,896]{1,0:T(8,128)(2,1)S(1)}, bf16[256,896]{1,0:T(8,128)(2,1)S(1)}, u32[]{:S(2)}, u32[]{:S(2)}) collective-permute-start(bf16[256,896]{1,0:T(8,128)(2,1)S(1)} %bitcast.194), channel_id=1, source_target_pairs={{0,24},{8,16},{16,8},{24,0},{1,25},{9,17},{17,9},{25,1},{2,26},{10... | collective-permute-start | bytes 1376264 | tf_op jit(solution)/shard_map/ppermute | solution.py:151
  95.1 7.6 %copy-start.7 = (bf16[4,256,896]{2,1,0:T(8,128)(2,1)}, bf16[4,256,896]{2,1,0:T(8,128)(2,1)S(1)}, u32[]{:S(2)}) copy-start(bf16[4,256,896]{2,1,0:T(8,128)(2,1)S(1)} %bitcast_dynamic-update-slice_fusion) | copy-start | bytes 5505028
  102.8 4.2 %copy-start.1 = (bf16[2,1024,1024]{2,1,0:T(8,128)(2,1)}, bf16[2,1024,1024]{2,1,0:T(8,128)(2,1)S(1)}, u32[]{:S(2)}) copy-start(bf16[2,1024,1024]{2,1,0:T(8,128)(2,1)S(1)} %fusion.5.x_ref) | copy-start | bytes 12582916
  106.9 4.9 %copy-start.27 = (f32[2048,512]{0,1:T(8,128)}, f32[2048,512]{0,1:T(8,128)S(1)}, u32[]{:S(2)}) copy-start(f32[2048,512]{0,1:T(8,128)S(1)} %get-tuple-element.65) | copy-start | bytes 12582916
  130.2 48.3 %copy-start.9 = (bf16[2,128,1024]{2,1,0:T(8,128)(2,1)S(1)}, bf16[2,128,1024]{2,1,0:T(8,128)(2,1)}, u32[]{:S(2)}) copy-start(bf16[2,128,1024]{2,1,0:T(8,128)(2,1)} %param.16) | copy-start | bytes 1572868
  130.2 96.1 %all-gather.5.cloned.1.call-start = ((), (), s32[]{:S(2)}) async-start(), calls=%async_computation.8 | async-start | bytes 4718592 | tf_op jit(solution)/shard_map/all_gather | solution.py:290
  132.8 97.9 %copy-start.15 = (bf16[4,128,1024]{2,1,0:T(8,128)(2,1)S(1)}, bf16[4,128,1024]{2,1,0:T(8,128)(2,1)}, u32[]{:S(2)}) copy-start(bf16[4,128,1024]{2,1,0:T(8,128)(2,1)} %copy-done.13) | copy-start | bytes 3145732
  132.8 97.9 %copy-start.21 = (f32[4,1,128]{2,1,0:T(1,128)S(1)}, f32[4,1,128]{2,1,0:T(1,128)}, u32[]{:S(2)}) copy-start(f32[4,1,128]{2,1,0:T(1,128)} %copy-done.20) | copy-start | bytes 6148
  180.9 157.8 %reduce-scatter.5.cloned.1.call-start = ((), (), s32[]{:S(2)}) async-start(), calls=%async_computation.9 | async-start | bytes 4718592 | tf_op jit(solution)/shard_map/reduce_scatter | solution.py:310
  226.3 4.4 %copy-start.5 = (bf16[2,1024,1024]{2,1,0:T(8,128)(2,1)S(1)}, bf16[2,1024,1024]{2,1,0:T(8,128)(2,1)}, u32[]{:S(2)}) copy-start(bf16[2,1024,1024]{2,1,0:T(8,128)(2,1)} %all-gather.5.cloned.1.call-done) | copy-start | bytes 12582916
  236.9 15.7 %copy-start.25 = (bf16[2048,512]{0,1:T(8,128)(2,1)}, bf16[2048,512]{0,1:T(8,128)(2,1)S(1)}, u32[]{:S(2)}) copy-start(bf16[2048,512]{0,1:T(8,128)(2,1)S(1)} %get-tuple-element.61) | copy-start | bytes 6291460
  236.9 11.9 %copy-start.8 = (bf16[4,256,896]{2,1,0:T(8,128)(2,1)S(1)}, bf16[4,256,896]{2,1,0:T(8,128)(2,1)}, u32[]{:S(2)}) copy-start(bf16[4,256,896]{2,1,0:T(8,128)(2,1)} %copy-done.7) | copy-start | bytes 5505028
  260.5 4.6 %copy-start.2 = (bf16[2,1024,1024]{2,1,0:T(8,128)(2,1)S(1)}, bf16[2,1024,1024]{2,1,0:T(8,128)(2,1)}, u32[]{:S(2)}) copy-start(bf16[2,1024,1024]{2,1,0:T(8,128)(2,1)} %copy-done.1) | copy-start | bytes 12582916
  260.5 4.6 %copy-start.26 = (bf16[2048,512]{0,1:T(8,128)(2,1)S(1)}, bf16[2048,512]{0,1:T(8,128)(2,1)}, u32[]{:S(2)}) copy-start(bf16[2048,512]{0,1:T(8,128)(2,1)} %copy-done.25) | copy-start | bytes 6291460
  286.6 11.1 %copy-start.6 = (bf16[2,1024,1024]{2,1,0:T(8,128)(2,1)S(1)}, bf16[2,1024,1024]{2,1,0:T(8,128)(2,1)}, u32[]{:S(2)}) copy-start(bf16[2,1024,1024]{2,1,0:T(8,128)(2,1)} %all-gather.5.cloned.1.call-done) | copy-start | bytes 12582916
  286.6 11.1 %copy-start.24 = (bf16[512,2048]{1,0:T(8,128)(2,1)S(1)}, bf16[512,2048]{1,0:T(8,128)(2,1)}, u32[]{:S(2)}) copy-start(bf16[512,2048]{1,0:T(8,128)(2,1)} %get-tuple-element.64) | copy-start | bytes 6291460
  286.6 15.1 %collective-permute-start.12 = (bf16[256,896]{1,0:T(8,128)(2,1)S(1)}, bf16[256,896]{1,0:T(8,128)(2,1)S(1)}, u32[]{:S(2)}, u32[]{:S(2)}) collective-permute-start(bf16[256,896]{1,0:T(8,128)(2,1)S(1)} %get-tuple-element.33), channel_id=1, source_target_pairs={{0,24},{8,16},{16,8},{24,0},{1,25},{9,17},{17,9},{25,1},{2,26},{10... | collective-permute-start | bytes 1376264 | tf_op jit(solution)/shard_map/ppermute | solution.py:164
  289.1 21.8 %collective-permute-start.11 = (bf16[256,896]{1,0:T(8,128)(2,1)S(1)}, bf16[256,896]{1,0:T(8,128)(2,1)S(1)}, u32[]{:S(2)}, u32[]{:S(2)}) collective-permute-start(bf16[256,896]{1,0:T(8,128)(2,1)S(1)} %get-tuple-element.32), channel_id=1, source_target_pairs={{0,16},{8,24},{16,0},{24,8},{1,17},{9,25},{17,1},{25,9},{2,18},{10... | collective-permute-start | bytes 1376264 | tf_op jit(solution)/shard_map/ppermute | solution.py:164
  289.6 21.3 %collective-permute-start.10 = (bf16[256,896]{1,0:T(8,128)(2,1)S(1)}, bf16[256,896]{1,0:T(8,128)(2,1)S(1)}, u32[]{:S(2)}, u32[]{:S(2)}) collective-permute-start(bf16[256,896]{1,0:T(8,128)(2,1)S(1)} %get-tuple-element.31), channel_id=1, source_target_pairs={{0,8},{8,0},{16,24},{24,16},{1,9},{9,1},{17,25},{25,17},{2,10},{10... | collective-permute-start | bytes 1376264 | tf_op jit(solution)/shard_map/ppermute | solution.py:164
  294.8 25.5 %collective-permute-start.15 = (bf16[32,1024]{1,0:T(8,128)(2,1)}, bf16[32,1024]{1,0:T(8,128)(2,1)S(1)}, u32[]{:S(2)}, u32[]{:S(2)}) collective-permute-start(bf16[32,1024]{1,0:T(8,128)(2,1)} %get-tuple-element.41), channel_id=1, source_target_pairs={{0,24},{8,16},{16,8},{24,0},{1,25},{9,17},{17,9},{25,1},{2,26},{10... | collective-permute-start | bytes 196616 | tf_op jit(solution)/shard_map/ppermute | solution.py:164
  297.2 23.7 %collective-permute-start.14 = (bf16[32,1024]{1,0:T(8,128)(2,1)}, bf16[32,1024]{1,0:T(8,128)(2,1)S(1)}, u32[]{:S(2)}, u32[]{:S(2)}) collective-permute-start(bf16[32,1024]{1,0:T(8,128)(2,1)} %get-tuple-element.42), channel_id=1, source_target_pairs={{0,16},{8,24},{16,0},{24,8},{1,17},{9,25},{17,1},{25,9},{2,18},{10... | collective-permute-start | bytes 196616 | tf_op jit(solution)/shard_map/ppermute | solution.py:164
  297.7 13.2 %copy-start.11 = (f32[1,256,896]{2,1,0:T(8,128)S(1)}, f32[1,256,896]{2,1,0:T(8,128)}, u32[]{:S(2)}) copy-start(f32[1,256,896]{2,1,0:T(8,128)} %copy.68) | copy-start | bytes 2752516
  301.7 19.1 %collective-permute-start.13 = (bf16[32,1024]{1,0:T(8,128)(2,1)S(1)}, bf16[32,1024]{1,0:T(8,128)(2,1)}, u32[]{:S(2)}, u32[]{:S(2)}) collective-permute-start(bf16[32,1024]{1,0:T(8,128)(2,1)S(1)} %get-tuple-element.40), channel_id=1, source_target_pairs={{0,8},{8,0},{16,24},{24,16},{1,9},{9,1},{17,25},{25,17},{2,10},{10... | collective-permute-start | bytes 196616 | tf_op jit(solution)/shard_map/ppermute | solution.py:164
  311.8 23.9 %all-to-all-start.3 = ((bf16[8,32,896]{2,1,0:T(8,128)(2,1)}), bf16[8,32,896]{2,1,0:T(8,128)(2,1)S(1)}, u32[]{:S(2)}, u32[]{:S(2)}) async-start(bf16[8,32,896]{2,1,0:T(8,128)(2,1)} %bitcast.48), calls=%async_computation.5 | async-start | bytes 917504 | tf_op jit(solution)/shard_map/all_to_all | solution.py:322
  317.3 10.4 %collective-permute-start.19 = (bf16[128,1024]{1,0:T(8,128)(2,1)}, bf16[128,1024]{1,0:T(8,128)(2,1)}, u32[]{:S(2)}, u32[]{:S(2)}) collective-permute-start(bf16[128,1024]{1,0:T(8,128)(2,1)} %get-tuple-element.37), channel_id=1, source_target_pairs={{0,24},{8,16},{16,8},{24,0},{1,25},{9,17},{17,9},{25,1},{2,26},{10... | collective-permute-start | bytes 786440 | tf_op jit(solution)/shard_map/ppermute | solution.py:164
  319.7 13.4 %collective-permute-start.18 = (bf16[128,1024]{1,0:T(8,128)(2,1)}, bf16[128,1024]{1,0:T(8,128)(2,1)}, u32[]{:S(2)}, u32[]{:S(2)}) collective-permute-start(bf16[128,1024]{1,0:T(8,128)(2,1)} %get-tuple-element.38), channel_id=1, source_target_pairs={{0,16},{8,24},{16,0},{24,8},{1,17},{9,25},{17,1},{25,9},{2,18},{10... | collective-permute-start | bytes 786440 | tf_op jit(solution)/shard_map/ppermute | solution.py:164
  320.2 13.2 %collective-permute-start.17 = (bf16[128,1024]{1,0:T(8,128)(2,1)S(1)}, bf16[128,1024]{1,0:T(8,128)(2,1)}, u32[]{:S(2)}, u32[]{:S(2)}) collective-permute-start(bf16[128,1024]{1,0:T(8,128)(2,1)S(1)} %get-tuple-element.36), channel_id=1, source_target_pairs={{0,8},{8,0},{16,24},{24,16},{1,9},{9,1},{17,25},{25,17},{2,10},{10... | collective-permute-start | bytes 786440 | tf_op jit(solution)/shard_map/ppermute | solution.py:164
  322.4 2.7 collective-permute-start.16
  333.4 5.2 %copy-start.10 = (bf16[2,128,1024]{2,1,0:T(8,128)(2,1)S(1)}, bf16[2,128,1024]{2,1,0:T(8,128)(2,1)}, u32[]{:S(2)}) copy-start(bf16[2,128,1024]{2,1,0:T(8,128)(2,1)} %reduce-scatter.3.cloned.1.call-done) | copy-start | bytes 1572868
  333.4 5.2 %copy-start.19 = (f32[2,128]{1,0:T(2,128)S(1)}, f32[2,128]{1,0:T(2,128)}, u32[]{:S(2)}) copy-start(f32[2,128]{1,0:T(2,128)} %add_rsqrt_fusion.1) | copy-start | bytes 3076
  335.7 6.3 %copy-start.18 = (f32[32,32]{1,0:T(8,128)S(1)}, f32[32,32]{1,0:T(8,128)}, u32[]{:S(2)}) copy-start(f32[32,32]{1,0:T(8,128)} %reshape.297) | copy-start | bytes 12292
  342.8 13.3 %all-to-all-start.2 = ((f32[32,1,384]{2,1,0:T(1,128)}), f32[32,1,384]{2,1,0:T(1,128)S(1)}, u32[]{:S(2)}, u32[]{:S(2)}) async-start(f32[32,1,384]{2,1,0:T(1,128)} %all_to_all.21), calls=%async_computation.4 | async-start | bytes 98304 | tf_op jit(solution)/shard_map/all_to_all | solution.py:368
  (8 other events, 18.7 us)
Sparse Core Ops, SparseCore 0:
  9.6 53.6 all-gather.2
  130.3 48.1 reduce-scatter.2
  181.0 45.2 all-gather.4
  257.3 48.7 reduce-scatter.4

commit v2 on v1

v2 whole, which is shorter than its diff:
```python
import functools
import math

import jax
import jax.numpy as jnp
from jax import lax
from jax.experimental import pallas as pl
from jax.experimental.pallas import tpu as pltpu
from jax.sharding import PartitionSpec as P

HEADS = 16
ROT = 16
BLK = 128
NEG_FILL = -1000000000.0
F32 = jnp.float32
BF16 = jnp.bfloat16
PARAMS = pltpu.CompilerParams(vmem_limit_bytes=56 * 1024 * 1024)
COPIES = 128
STEP = 512
LAST = ((1,), (1,))
FIRST = ((0,), (0,))


def mm(a, b, dims=((1,), (0,))):
    return lax.dot_general(a, b, (dims, ((), ())), preferred_element_type=F32)


def block_spans(length, first_len):
    return [(at, 0 if at < first_len else first_len) for at in range(0, length, BLK)]


def head_stack(rows, heads, size):
    lane = lax.broadcasted_iota(jnp.int32, rows.shape, 1) // size
    parts = [jnp.where(lane == h, rows, jnp.zeros_like(rows)) for h in range(heads)]
    return parts[0] if heads == 1 else jnp.concatenate(parts, axis=0)


def head_pick(stacked, heads, size):
    rows = stacked.shape[0] // heads
    out = stacked[:rows]
    lane = lax.broadcasted_iota(jnp.int32, out.shape, 1) // size
    for h in range(1, heads):
        out = jnp.where(lane == h, stacked[h * rows : (h + 1) * rows], out)
    return out


def turn(values, cosine, sine, size):
    half = ROT // 2
    width = values.shape[1]
    place = lax.broadcasted_iota(jnp.int32, values.shape, 1) % size
    partner = jnp.where(
        place < half,
        pltpu.roll(values, width - half, 1),
        pltpu.roll(values, half, 1),
    )
    return values * cosine + partner * sine


def span_mask(start, low, first_len, seg_row, heads):
    stop = start + BLK
    shape = (heads * BLK, stop - low)
    row = lax.rem(lax.broadcasted_iota(jnp.int32, shape, 0), BLK) + start
    col = lax.broadcasted_iota(jnp.int32, shape, 1) + low
    allowed = col <= row
    if low >= first_len:
        turned = jnp.transpose(jnp.broadcast_to(seg_row[:, start:stop], (BLK, BLK)))[:, :1]
        turned = jnp.concatenate([turned] * heads, axis=0)
        allowed = allowed & (turned == seg_row[:, low:stop])
    return allowed


def standardize(rows):
    centered = rows - jnp.mean(rows, axis=-1, keepdims=True)
    variance = jnp.mean(centered * centered, axis=-1, keepdims=True)
    root = lax.rsqrt(variance + 1e-05)
    return centered * root, root


class Copier:
    def __init__(self, sems):
        self.sems, self.used = sems, 0

    def start(self, source, target):
        copy = pltpu.make_async_copy(source, target, self.sems.at[self.used])
        self.used += 1
        copy.start()
        return copy

    def rows(self, pairs, at, step):
        return [self.start(a.at[at : at + step], b.at[at : at + step]) for a, b in pairs]


def view_columns(refs, part, units):
    if len(refs) == 2:
        return refs
    return refs[0].at[:, pl.ds(0, 3 * part)], refs[0].at[:, pl.ds(3 * part, units)]


def wait_all(copies):
    for copy in copies:
        copy.wait()


def forward_kernel(
    first_len, heads, size, scale, length, step,
    gain, shift, bqkv, bup, seg_row, x_in, cos_in, sin_in, wdown_in, wproj_in, *refs,
):
    (x, cosine, sine, wdown, wproj,
     normed, q, k, v, act, slope, mixed, stat, terms, sems) = refs[-15:]
    split = (len(refs) - 24) // 2
    w_in, w = refs[:split], refs[split + 9 : 2 * split + 9]
    (n_out, q_out, k_out, v_out, act_out, slope_out, mixed_out, stat_out, terms_out) = refs[
        split : split + 9
    ]
    copier = Copier(sems)
    part = heads * size
    wqkv, wup = view_columns(w, part, act.shape[1])
    total = x.shape[0]
    starts = range(0, total, step)
    tables = ((cos_in, cosine), (sin_in, sine))
    x_copies = {0: copier.rows([(x_in, x)], 0, step)}
    w_copies = [copier.start(a, b) for a, b in zip(w_in, w)]
    t_copies = {0: copier.rows(tables, 0, step)}
    for at in starts[1:]:
        x_copies[at] = copier.rows([(x_in, x)], at, step)
        t_copies[at] = copier.rows(tables, at, step)
    w_copies += [copier.start(wdown_in, wdown), copier.start(wproj_in, wproj)]
    out = []
    for seq in range(total // length):
        origin = seq * length
        for at in range(origin, origin + length, step):
            rows = slice(at, at + step)
            wait_all(x_copies[at])
            standard, _ = standardize(x[rows, :].astype(F32))
            low = (standard * gain[...] + shift[...]).astype(BF16)
            normed[rows, :] = low
            out += copier.rows([(normed, n_out)], at, step)
            if at == 0:
                wait_all(w_copies[:split])
            full = mm(low, wqkv[...]) + bqkv[...]
            wait_all(t_copies[at])
            cos_rows, sin_rows = cosine[rows, :], sine[rows, :]
            q[rows, :] = turn(full[:, :part], cos_rows, sin_rows, size).astype(
                BF16
            ) * jnp.asarray(scale, BF16)
            k[rows, :] = turn(full[:, part : 2 * part], cos_rows, sin_rows, size).astype(BF16)
            v[rows, :] = full[:, 2 * part :].astype(BF16)
            out += copier.rows(((q, q_out), (k, k_out), (v, v_out)), at, step)
            up = mm(low, wup[...]) + bup[...]
            cdf = 0.5 * (1.0 + lax.erf(up * math.sqrt(0.5)))
            act[rows, :] = (up * cdf).astype(BF16)
            slope[rows, :] = cdf + up * jnp.exp(-0.5 * up * up) * (
                1.0 / math.sqrt(2.0 * math.pi)
            )
            out += copier.rows(((act, act_out), (slope, slope_out)), at, step)
        for start, low in block_spans(length, first_len):
            rows, cols = slice(origin + start, origin + start + BLK), slice(
                origin + low, origin + start + BLK
            )
            query = head_stack(q[rows, :], heads, size)
            allowed = span_mask(start, low, first_len, seg_row[seq : seq + 1, :], heads)
            scores = jnp.where(allowed, mm(query, k[cols, :], LAST), NEG_FILL)
            peak = jnp.max(scores, axis=1, keepdims=True)
            grown = jnp.exp(scores - peak)
            summed = jnp.sum(grown, axis=1, keepdims=True)
            probs = (grown * (1.0 / summed)).astype(BF16)
            result = mm(probs, v[cols, :])
            mixed[rows, :] = head_pick(result, heads, size).astype(BF16)
            stat[rows, :] = head_pick(
                jnp.broadcast_to(peak + jnp.log(summed), result.shape), heads, size
            )
        out += copier.rows(((mixed, mixed_out), (stat, stat_out)), origin, length)
        if seq == 0:
            wait_all(w_copies[split:])
        for at in range(origin, origin + length, step):
            rows = slice(at, at + step)
            terms[rows, :] = (mm(act[rows, :], wdown[...]) + mm(mixed[rows, :], wproj[...])).astype(
                BF16
            )
            out += copier.rows([(terms, terms_out)], at, step)
    wait_all(out)


def backward_kernel(
    first_len, heads, size, scale, length, step,
    seg_row,
    g_in, slope_in, q_in, k_in, v_in, stat_in, cos_in, sin_in, wdown_in, wproj_in, *refs,
):
    (g, slope, q, k, v, stat, cosine, sine, wdown, wproj,
     mg, ug, qg, dk, dv, back, sems) = refs[-17:]
    split = (len(refs) - 20) // 2
    w_in, w = refs[:split], refs[split + 3 : 2 * split + 3]
    ug_out, qg_out, back_out = refs[split : split + 3]
    copier = Copier(sems)
    width = heads * size
    wqkv, wup = view_columns(w, width, ug.shape[1])
    total = g.shape[0]
    starts = range(0, total, step)
    loads = ((g_in, g), (slope_in, slope))
    saved = (
        (q_in, q), (k_in, k), (v_in, v), (stat_in, stat), (cos_in, cosine), (sin_in, sine)
    )
    g_copies = {0: copier.rows(loads[:1], 0, step)}
    w_copies = [copier.start(wdown_in, wdown)]
    g_copies[0] += copier.rows(loads[1:], 0, step)
    w_copies.append(copier.start(wproj_in, wproj))
    s_copies = {}
    for at in starts[1:]:
        g_copies[at] = copier.rows(loads, at, step)
        if (at + step) % length == 0:
            origin = at + step - length
            s_copies[origin] = copier.rows(saved, origin, length)
            if origin == 0:
                w_copies += [copier.start(a, b) for a, b in zip(w_in, w)]
    out = []
    for seq in range(total // length):
        origin = seq * length
        for at in range(origin, origin + length, step):
            rows = slice(at, at + step)
            wait_all(g_copies[at])
            if at == 0:
                wait_all(w_copies[:2])
            grad = g[rows, :]
            ug[rows, :] = (mm(grad, wdown[...], LAST) * slope[rows, :]).astype(BF16)
            out += copier.rows([(ug, ug_out)], at, step)
            mg[rows, :] = mm(grad, wproj[...], LAST).astype(BF16)
        dk[...] = jnp.zeros_like(dk)
        dv[...] = jnp.zeros_like(dv)
        wait_all(s_copies[origin])
        for start, low in block_spans(length, first_len):
            stop = start + BLK
            rows, cols = slice(origin + start, origin + stop), slice(origin + low, origin + stop)
            query = head_stack(q[rows, :], heads, size)
            grad = head_stack(mg[rows, :], heads, size)
            key, value = k[cols, :], v[cols, :]
            allowed = span_mask(start, low, first_len, seg_row[seq : seq + 1, :], heads)
            peak = stat[rows, :]
            peak = jnp.concatenate(
                [peak[:, h * size : h * size + 1] for h in range(heads)], axis=0
            )
            scores = jnp.where(allowed, mm(query, key, LAST), NEG_FILL)
            probs = jnp.exp(scores - peak)
            prob_grad = mm(grad, value, LAST)
            delta = jnp.sum(probs * prob_grad, axis=1, keepdims=True)
            score_grad = (probs * (prob_grad - delta)).astype(BF16)
            dq = head_pick(mm(score_grad, key), heads, size) * scale
            qg[rows, :width] = turn(dq, cosine[rows, :], -sine[rows, :], size).astype(BF16)
            dk[low:stop, :] += mm(score_grad, query, FIRST)
            dv[low:stop, :] += mm(probs.astype(BF16), grad, FIRST)
        rows = slice(origin, origin + length)
        qg[rows, width : 2 * width] = turn(
            dk[...], cosine[rows, :], -sine[rows, :], size
        ).astype(BF16)
        qg[rows, 2 * width :] = dv[...].astype(BF16)
        out += copier.rows([(qg, qg_out)], origin, length)
        if seq == 0:
            wait_all(w_copies[2:])
        for at in range(origin, origin + length, step):
            rows = slice(at, at + step)
            back[rows, :] = (
                mm(ug[rows, :], wup[...], LAST) + mm(qg[rows, :], wqkv[...], LAST)
            ).astype(BF16)
            out += copier.rows([(back, back_out)], at, step)
    wait_all(out)


def column_kernel(cut, order, n, qg, ug, *outs):
    outs, sums = outs[:-1], outs[-1]
    rows, split = outs[0].shape[0], qg.shape[1]
    ones = jnp.ones((8, n.shape[0]), BF16)
    sums[:, :split] = mm(ones, qg[...])
    sums[:, split:] = mm(ones, ug[...])
    for k in list(range(1, len(outs))) + [0]:
        if cut:
            block = n[:, pl.ds(pl.multiple_of(order[k] * rows, rows), rows)]
        else:
            block = n[...]
        outs[k][:, :split] = mm(block, qg[...], FIRST).astype(outs[k].dtype)
        outs[k][:, split:] = mm(block, ug[...], FIRST).astype(outs[k].dtype)


def down_kernel(act, mixed, g, dw, pw):
    dw[...] = mm(act[...], g[...], FIRST).astype(BF16)
    pw[...] = mm(mixed[...], g[...], FIRST).astype(BF16)


def sums_kernel(x, back, gain_sum, shift_sum):
    @pl.when(pl.program_id(0) == 0)
    def _():
        for ref in (gain_sum, shift_sum):
            ref[...] = jnp.zeros_like(ref)

    standard, _ = standardize(x[...].astype(F32))
    terms = back[...].astype(F32)
    gain_sum[...] += jnp.sum(terms * standard, axis=0, keepdims=True)
    shift_sum[...] += jnp.sum(terms, axis=0, keepdims=True)


def loss_kernel(branch, x, teacher, valid, bias, factor, out, grad, low, column, square):
    full = x[...].astype(F32) + (branch[...].astype(F32) + bias[...])
    out[...] = full.astype(BF16)
    error = valid[...] * (full - teacher[...].astype(F32))
    square[...] = jnp.sum(jnp.sum(error * error, axis=0, keepdims=True), axis=1, keepdims=True)
    scaled = factor[...] * error
    grad[...] = scaled
    rounded = scaled.astype(BF16)
    low[...] = rounded
    column[...] = jnp.sum(rounded.astype(F32), axis=0, keepdims=True)


def norm_back_kernel(ng, x, og, gain, out):
    standard, root = standardize(x[...].astype(F32))
    inner = ng[...].astype(F32) * gain[...]
    out[...] = (
        og[...]
        + root
        * (
            inner
            - jnp.mean(inner, axis=-1, keepdims=True)
            - standard * jnp.mean(inner * standard, axis=-1, keepdims=True)
        )
    ).astype(BF16)


def head_of(local, ctx, heads, n_ctx, paired):
    if not paired:
        return ctx * heads + local
    return (heads * (ctx % 2) + local) * (n_ctx // 2) + ctx // 2


def pack_columns(heads, size, paired, units, n_dp, n_ctx, qkv_ref, up_ref, valid_ref, *refs):
    vectors, out_ref = refs[:-1], refs[-1]
    part = heads * size
    width, unit_rows = n_ctx * part, units // n_dp
    count = jnp.sum(jnp.sum(valid_ref[...].astype(F32), axis=1, keepdims=True), axis=0, keepdims=True)
    high = jnp.floor(count * (1.0 / 128.0))
    small = [
        jnp.pad(ref[...].astype(F32).reshape(1, ref.shape[0]), ((0, 0), (0, 128 - ref.shape[0])))
        for ref in vectors
    ]
    small += [jnp.broadcast_to(a, (1, 128)) for a in (high, count - 128.0 * high)]
    small = jnp.concatenate(small, axis=0).astype(BF16)
    small = jnp.concatenate([small, jnp.zeros((out_ref.shape[1] - 8, 128), BF16)], axis=0)
    for j in range(n_ctx):
        out_ref[j, :, 3 * part + units :] = small
        for p in range(3):
            at = [p * width + head_of(h, j, heads, n_ctx, paired) * size for h in range(heads)]
            out_ref[j, :, p * part : (p + 1) * part] = jnp.concatenate(
                [qkv_ref[:, a : a + size] for a in at], axis=1
            )
        for i in range(n_dp):
            at = (i * n_ctx + j) * unit_rows
            out_ref[j, :, 3 * part + i * unit_rows : 3 * part + (i + 1) * unit_rows] = up_ref[
                :, at : at + unit_rows
            ]


def unpack_columns(heads, size, paired, units, n_dp, n_ctx, in_ref, qkv_ref, up_ref):
    part = heads * size
    width, unit_rows = n_ctx * part, units // n_dp
    held = {
        head_of(h, j, heads, n_ctx, paired): (j, h) for j in range(n_ctx) for h in range(heads)
    }
    for p in range(3):
        for first in range(0, n_ctx * heads, heads):
            pieces = []
            for head in range(first, first + heads):
                j, h = held[head]
                pieces.append(in_ref[j, :, p * part : (p + 1) * part][:, h * size : (h + 1) * size])
            qkv_ref[:, p * width + first * size : p * width + (first + heads) * size] = (
                jnp.concatenate(pieces, axis=1).astype(F32)
            )
    for j in range(n_ctx):
        for i in range(n_dp):
            at = (i * n_ctx + j) * unit_rows
            up_ref[:, at : at + unit_rows] = in_ref[
                j, :, 3 * part + i * unit_rows : 3 * part + (i + 1) * unit_rows
            ].astype(F32)


def shape_of(dims, dtype):
    return jax.ShapeDtypeStruct(dims, dtype)


def row_spec(rows, *dims):
    return pl.BlockSpec((rows,) + dims, lambda s: (s,) + (0,) * len(dims))


def whole_spec(*dims):
    return pl.BlockSpec(dims, lambda s: (0,) * len(dims))


HBM = pl.BlockSpec(memory_space=pl.ANY)
LOCAL = pl.BlockSpec(memory_space=pltpu.VMEM)
SCALAR = pl.BlockSpec(memory_space=pltpu.SMEM)


def kernel_call(kernel, name, in_specs, out, scratch=(), flops=0, moved=0, grid=None):
    return pl.pallas_call(
        kernel,
        in_specs=in_specs,
        out_specs=[spec for spec, _ in out],
        out_shape=[shape for _, shape in out],
        scratch_shapes=list(scratch),
        compiler_params=PARAMS,
        cost_estimate=pl.CostEstimate(flops=flops, bytes_accessed=moved, transcendentals=0),
        name=name,
        **({"grid": grid} if grid else {}),
    )


def gather_dp(block, n_dp, me_dp):
    out = jnp.zeros((n_dp,) + block.shape, block.dtype)
    out = lax.dynamic_update_index_in_dim(out, block, me_dp, 0)
    for k in range(1, n_dp):
        pairs = [(i, i ^ k) for i in range(n_dp)]
        other = lax.ppermute(block, "dp", pairs)
        out = lax.dynamic_update_index_in_dim(out, other, me_dp ^ k, 0)
    return out.reshape((n_dp * block.shape[0],) + block.shape[1:])


def exchange_dp(terms, n_dp):
    total = terms[0]
    for k in range(1, n_dp):
        pairs = [(i, i ^ k) for i in range(n_dp)]
        total = total + lax.ppermute(terms[k], "dp", pairs).astype(F32)
    return total


def reduce_dp(terms, n_dp, me_dp):
    rows = terms.shape[0] // n_dp
    blocks = terms.reshape((n_dp, rows) + terms.shape[1:])
    total = lax.dynamic_index_in_dim(blocks, me_dp, 0, keepdims=False).astype(F32)
    for k in range(1, n_dp):
        pairs = [(i, i ^ k) for i in range(n_dp)]
        block = lax.dynamic_index_in_dim(blocks, me_dp ^ k, 0, keepdims=False)
        total = total + lax.ppermute(block, "dp", pairs).astype(F32)
    return total


def body(
    n_dp, n_ctx,
    tokens, teacher, segments, positions, valid_mask,
    norm_gain, norm_bias, qkv_weight, qkv_bias, proj_weight, proj_bias,
    up_weight, up_bias, down_weight, down_bias,
):
    seqs, local_len, width = tokens.shape
    length = segments.shape[1]
    rows = seqs * local_len
    all_rows = seqs * length
    n_all = n_dp * n_ctx
    first_len = length // 2 + local_len
    heads = HEADS // n_ctx
    size = width // HEADS
    part = heads * size
    hidden = up_weight.shape[1]
    units = hidden // n_ctx
    unit_rows = down_weight.shape[0]
    own = width // n_all
    scale = 1.0 / math.sqrt(size)
    me_dp = lax.axis_index("dp")
    me_ctx = lax.axis_index("ctx")
    both = ("dp", "ctx")
    aligned = part % 128 == 0 and unit_rows % 128 == 0 and own % 16 == 0
    paired = aligned and 2 * own == size and 2 * heads == n_dp
    me_core, me_chip = me_ctx % 2, me_ctx // 2
    swap = [(j, j ^ 1) for j in range(n_ctx)]

    to_plan = [(n_dp * j + i, i * n_ctx + j) for i in range(n_dp) for j in range(n_ctx)]
    from_plan = [(b, a) for a, b in to_plan]
    valid = valid_mask.astype(F32).reshape(rows, 1)
    vectors = [norm_gain, norm_bias, proj_bias, down_bias, qkv_bias, up_bias]
    extra = 128 * max(1, 8 // own)
    total_cols = 3 * part + units + extra
    if aligned:
        cols = pl.pallas_call(
            functools.partial(pack_columns, heads, size, paired, units, n_dp, n_ctx),
            out_shape=shape_of((n_ctx, own, total_cols), BF16),
            compiler_params=PARAMS,
            name="pack_columns",
        )(qkv_weight, up_weight, valid_mask, *vectors)
    else:
        count = jnp.sum(valid_mask)
        small = jnp.stack(
            [jnp.pad(a, (0, 128 - a.shape[0])) for a in vectors]
            + [jnp.broadcast_to(a.astype(BF16), (128,)) for a in (count // 128, count % 128)]
        ).reshape(8 * 128)
        small = jnp.pad(small, (0, own * extra - 8 * 128)).reshape(own, extra)
        qkv_cols = qkv_weight.reshape(own, 3, n_ctx, part).transpose(2, 0, 1, 3)
        up_cols = up_weight.reshape(own, n_dp, n_ctx, unit_rows).transpose(2, 0, 1, 3)
        cols = jnp.concatenate(
            [
                qkv_cols.reshape(n_ctx, own, 3 * part), up_cols.reshape(n_ctx, own, units),
                jnp.broadcast_to(small[None], (n_ctx, own, extra)),
            ],
            axis=2,
        )
    cols, down_weight, proj_weight = lax.optimization_barrier((cols, down_weight, proj_weight))
    x_rows = lax.all_gather(tokens, "ctx", axis=1, tiled=True).reshape(all_rows, width)
    cols = lax.all_to_all(cols, "ctx", 0, 0, tiled=True).reshape(n_ctx * own, total_cols)
    cols, segments = lax.optimization_barrier((cols, segments))
    w_cols = gather_dp(cols, n_dp, me_dp)
    small = w_cols[:, 3 * part + units :].reshape(n_all, own * extra)[:, : 8 * 128]
    small = small.reshape(n_all, 8, 128).astype(F32)
    gain = small[:, 0, :own].reshape(1, width)
    shift = small[:, 1, :own].reshape(1, width)
    out_bias = (small[:, 2, :own] + small[:, 3, :own]).reshape(1, width)
    qkv_b = small[:, 4, : 3 * own]
    if paired:
        qkv_b = lax.dynamic_slice(
            qkv_b.reshape(3, 2, heads, n_ctx // 2, size), (0, me_core, 0, me_chip, 0),
            (3, 1, heads, 1, size),
        )
    else:
        qkv_b = lax.dynamic_index_in_dim(qkv_b.reshape(3, n_ctx, part), me_ctx, 1)
    qkv_b = qkv_b.reshape(1, 3 * part)
    up_b = small[:, 5, :unit_rows].reshape(n_dp, n_ctx, unit_rows)
    up_b = lax.dynamic_index_in_dim(up_b, me_ctx, 1, keepdims=False).reshape(1, units)
    valid_count = 128.0 * jnp.sum(small[:, 6, 0]) + jnp.sum(small[:, 7, 0])
    sliced = (3 * part) % 128 == 0 and units % 128 == 0
    if sliced:
        w_split = [w_cols]
    else:
        w_split = [w_cols[:, : 3 * part], w_cols[:, 3 * part : 3 * part + units]]
    token = jnp.arange(length, dtype=jnp.int32)
    half = ROT // 2
    lane = jnp.arange(part, dtype=jnp.int32) % size
    steps = jnp.arange(half, dtype=F32)
    inverse = jnp.power(10000.0, -2.0 * steps / ROT)
    lane_inverse = jnp.where(lane < ROT, inverse[lane % half], 0.0)
    same = segments[:, :, None] == segments[:, None, :]
    before = token[None, None, :] < token[None, :, None]
    in_doc = jnp.sum((same & before).astype(F32), axis=2)
    angles = in_doc.reshape(all_rows, 1) * lane_inverse[None, :]
    cosine = jnp.cos(angles)
    sine = jnp.sin(angles) * jnp.where(lane < half, -1.0, 1.0)

    w_down = gather_dp(down_weight, n_dp, me_dp)
    if paired:
        halves = gather_dp(proj_weight, n_dp, me_dp).reshape(2, heads, own, width)
        keep = lax.dynamic_index_in_dim(halves, me_core, 0, keepdims=False)
        got = lax.ppermute(
            lax.dynamic_index_in_dim(halves, 1 - me_core, 0, keepdims=False), "ctx", swap
        )
        w_proj = jnp.stack(
            [jnp.where(me_core == 0, keep, got), jnp.where(me_core == 0, got, keep)], axis=1
        ).reshape(part, width)
    else:
        w_proj = gather_dp(lax.ppermute(proj_weight, both, to_plan), n_dp, me_dp)

    def wide(columns, dtype=BF16):
        return pltpu.VMEM((all_rows, columns), dtype)

    def store(columns, dtype=BF16):
        return (HBM, shape_of((all_rows, columns), dtype))

    w_scratch = [pltpu.VMEM(a.shape, BF16) for a in w_split]
    weights = [pltpu.VMEM((units, width), BF16), pltpu.VMEM((part, width), BF16)]
    sems = pltpu.SemaphoreType.DMA((COPIES,))
    normed, query, key, value, act, slope, mixed, stat, terms = kernel_call(
        functools.partial(forward_kernel, first_len, heads, size, scale, length, STEP),
        "forward_kernel",
        [LOCAL] * 5 + [HBM] * (5 + len(w_split)),
        [
            store(width), store(part), store(part), store(part), store(units), store(units, F32),
            store(part), store(part, F32), store(width),
        ],
        [
            *w_scratch, wide(width), wide(part, F32), wide(part, F32), *weights,
            wide(width), wide(part), wide(part), wide(part), wide(units), wide(units, F32),
            wide(part), wide(part, F32), wide(width), sems,
        ],
        flops=10 * 10**9, moved=2 * 10**7,
    )(
        gain, shift, qkv_b, up_b, segments, x_rows, cosine, sine, w_down, w_proj, *w_split
    )
    branch = lax.psum_scatter(
        terms.reshape(seqs, length, width), "ctx", scatter_dimension=1, tiled=True
    ).reshape(rows, width)

    total_tokens = seqs * n_dp * length
    factor = (total_tokens / valid_count).reshape(1, 1)
    tokens_rows = tokens.reshape(rows, width)
    own_block = (rows, width)
    layer_out, out_grad, low, column, square = kernel_call(
        loss_kernel, "loss_kernel", [LOCAL] * 6,
        [
            (LOCAL, shape_of(own_block, BF16)), (LOCAL, shape_of(own_block, F32)),
            (LOCAL, shape_of(own_block, BF16)), (LOCAL, shape_of((1, width), F32)),
            (LOCAL, shape_of((1, 1), F32)),
        ],
        flops=10**6, moved=3 * 10**6,
    )(branch, tokens_rows, teacher.reshape(rows, width), valid, out_bias, factor)

    grads = lax.all_gather(
        low.reshape(tokens.shape), "ctx", axis=1, tiled=True
    ).reshape(all_rows, width)
    up_grad, qkv_grad, back = kernel_call(
        functools.partial(backward_kernel, first_len, heads, size, scale, length, STEP),
        "backward_kernel",
        [LOCAL] + [HBM] * (10 + len(w_split)),
        [store(units), store(3 * part), store(width)],
        [
            *w_scratch, wide(width), wide(units, F32), wide(part), wide(part), wide(part),
            wide(part, F32), wide(part, F32), wide(part, F32), *weights, wide(part), wide(units), wide(3 * part),
            pltpu.VMEM((length, part), F32), pltpu.VMEM((length, part), F32), wide(width), sems,
        ],
        flops=12 * 10**9, moved=2 * 10**7,
    )(
        segments, grads, slope, query, key, value, stat, cosine, sine, w_down, w_proj, *w_split
    )
    normed_grad = lax.psum_scatter(
        back.reshape(seqs, length, width), "ctx", scatter_dimension=1, tiled=True
    ).reshape(rows, width)

    order = jnp.stack([me_dp ^ k for k in range(n_dp)]).astype(jnp.int32)
    cut = (width // n_dp) % 128 == 0
    block = (width // n_dp if cut else width, 3 * part + units)
    *col_terms, col_sums = kernel_call(
        functools.partial(column_kernel, cut), "column_kernel",
        [SCALAR] + [LOCAL] * 3,
        [(LOCAL, shape_of(block, BF16 if k else F32)) for k in range(n_dp if cut else 1)]
        + [(LOCAL, shape_of((8, block[1]), F32))],
        flops=4 * 10**9, moved=10**7,
    )(order, normed, qkv_grad, up_grad)
    col_terms, x_rows = lax.optimization_barrier((col_terms, x_rows))
    if cut:
        col_wgrad = exchange_dp(col_terms, n_dp).astype(BF16)
    else:
        col_wgrad = reduce_dp(col_terms[0].astype(BF16), n_dp, me_dp).astype(BF16)
    sum_rows = 512
    gain_sum, shift_sum = kernel_call(
        sums_kernel, "sums_kernel",
        [row_spec(sum_rows, width)] * 2,
        [(whole_spec(1, width), shape_of((1, width), F32))] * 2,
        flops=10**6, moved=10**5, grid=(all_rows // sum_rows,),
    )(x_rows, back)
    qkv_bsum, up_bsum = col_sums[:1, : 3 * part], col_sums[:1, 3 * part :]
    if paired:
        qkv_bsum = lax.dynamic_update_slice(
            jnp.zeros((3, 2, heads, n_ctx // 2, size), F32),
            qkv_bsum.reshape(3, 1, heads, 1, size), (0, me_core, 0, me_chip, 0),
        )
    else:
        qkv_bsum = lax.dynamic_update_slice(
            jnp.zeros((3, n_ctx, part), F32), qkv_bsum.reshape(3, 1, part), (0, me_ctx, 0)
        )
    up_bsum = lax.dynamic_update_slice(
        jnp.zeros((n_dp, n_ctx, unit_rows), F32), up_bsum.reshape(n_dp, 1, unit_rows),
        (0, me_ctx, 0),
    )
    parts = [
        gain_sum.reshape(n_all, own), shift_sum.reshape(n_all, own),
        column.reshape(n_all, own), qkv_bsum[2].reshape(n_all, own),
        qkv_bsum[:2].reshape(n_all, 2 * own), up_bsum.reshape(n_all, unit_rows),
        jnp.broadcast_to(square, (n_all, 1)),
    ]
    sums = jnp.concatenate(parts, axis=1)
    sums = jnp.pad(sums, ((0, 0), (0, -sums.shape[1] % 128)))
    sums = lax.all_to_all(sums, both, 0, 0, tiled=True)
    col_wgrad, sums = lax.optimization_barrier((col_wgrad, sums))
    col_wgrad, act = lax.optimization_barrier((col_wgrad, act))
    col_wgrad = lax.all_to_all(
        col_wgrad.reshape(n_ctx, own, 3 * part + units), "ctx", 0, 0, tiled=True
    )
    sums = jnp.sum(sums, axis=0)
    gain_grad, shift_grad, bias_grad, value_bgrad = (
        sums[k * own : (k + 1) * own] for k in range(4)
    )
    qk_bgrad = sums[4 * own : 6 * own]
    up_bgrad = sums[6 * own : 6 * own + unit_rows]
    loss = sums[6 * own + unit_rows] / (valid_count * width)

    down_wgrad, proj_wgrad = kernel_call(
        down_kernel, "down_kernel", [LOCAL] * 3,
        [(LOCAL, shape_of((units, width), BF16)), (LOCAL, shape_of((part, width), BF16))],
        flops=10**6, moved=10**5,
    )(act, mixed, grads)
    down_wgrad = reduce_dp(down_wgrad, n_dp, me_dp)
    if paired:
        halves = proj_wgrad.reshape(heads, 2, own, width)
        keep = lax.dynamic_index_in_dim(halves, me_core, 1, keepdims=False)
        got = lax.ppermute(
            lax.dynamic_index_in_dim(halves, 1 - me_core, 1, keepdims=False), "ctx", swap
        )
        proj_wgrad = jnp.concatenate(
            [jnp.where(me_core == 0, keep, got), jnp.where(me_core == 0, got, keep)], axis=0
        ).reshape(n_dp * own, width)
        proj_wgrad = reduce_dp(proj_wgrad, n_dp, me_dp)
    else:
        proj_wgrad = reduce_dp(proj_wgrad, n_dp, me_dp)
        proj_wgrad = lax.ppermute(proj_wgrad.astype(BF16), both, from_plan).astype(F32)

    (input_grad,) = kernel_call(
        norm_back_kernel, "norm_back_kernel", [LOCAL] * 4, [(LOCAL, shape_of(own_block, BF16))],
        flops=10**6, moved=3 * 10**6,
    )(normed_grad, tokens_rows, out_grad, gain)
    input_grad, col_wgrad = lax.optimization_barrier((input_grad, col_wgrad))
    if aligned:
        qkv_wgrad, up_wgrad = pl.pallas_call(
            functools.partial(unpack_columns, heads, size, paired, units, n_dp, n_ctx),
            out_shape=[shape_of((own, 3 * width), F32), shape_of((own, hidden), F32)],
            compiler_params=PARAMS,
            name="unpack_columns",
        )(col_wgrad)
    else:
        qkv_wgrad = (
            col_wgrad[:, :, : 3 * part].reshape(n_ctx, own, 3, part).transpose(1, 2, 0, 3)
        ).reshape(own, 3 * width).astype(F32)
        up_wgrad = (
            col_wgrad[:, :, 3 * part :].reshape(n_ctx, own, n_dp, unit_rows).transpose(1, 2, 0, 3)
        ).reshape(own, hidden).astype(F32)

    return (
        layer_out.reshape(tokens.shape), loss, input_grad.reshape(tokens.shape), gain_grad,
        shift_grad, qkv_wgrad, qk_bgrad, value_bgrad, proj_wgrad, bias_grad, up_wgrad, up_bgrad,
        down_wgrad, bias_grad,
    )


def solution(mesh):
    n_dp, n_ctx = mesh.shape["dp"], mesh.shape["ctx"]
    seq, flat = P("dp", "ctx", None), P(("dp", "ctx"))
    mat = P(("dp", "ctx"), None)
    in_specs = (
        seq, seq, P("dp", None), P("dp", "ctx"), P("dp", "ctx"),
        flat, flat, mat, flat, mat, flat, mat, flat, mat, flat,
    )
    out_specs = (seq, P(), seq, flat, flat, mat, flat, flat, mat, flat, mat, flat, mat, flat)
    return jax.shard_map(
        functools.partial(body, n_dp, n_ctx),
        mesh=mesh, in_specs=in_specs, out_specs=out_specs, check_vma=False,
    )
```

time: 372 us -> 315 us (0.85)
  Pallas kernels: 23.4 us -> 79.8 us
  matrix products: 49.6 us -> 0 us
  local copies, waits for them, and re-layouts: 45.4 us -> 17.8 us
  other arithmetic: 38.9 us -> 22.8 us
  starting transfers between devices: 48.9 us -> 33.5 us
  waiting for transfers between devices: 143 us -> 128 us
  blocking collectives: 0 us -> 10.8 us
    pallas_call x2 -> x9, Pallas kernels: 23.4 us -> 79.8 us  [the longest x1 23 us: body(): kernel_call(functools.partial(backward_kernel, first_len, heads, size, sc...]
    dot_general x11 -> x0, matrix products: 49.6 us -> none  [mm(): return lax.dot_general(a, b, (dims, ((), ())), preferred_element_type=F32)]
    all_to_all x2 -> x0, starting transfers between devices: 12.3 us -> none  [the longest x1 6.31 us: body(): lax.all_to_all(jnp.broadcast_to(small[None], (n_all, small.shape[0])), bo...]
    reduce_sum x9 -> x2, other arithmetic: 11.7 us -> 0.67 us  [the longest x1 0.65 us: body(): valid_count = 128.0 * jnp.sum(small[:, 6, 0]) + jnp.sum(small[:, 7, 0])]
    all_to_all x0 -> x1, blocking collectives: none -> 10.8 us  [body(): sums = lax.all_to_all(sums, both, 0, 0, tiled=True)]
    reshape x12 -> x7, local copies, waits for them, and re-layouts: 11.8 us -> 3 us  [the longest x1 0.8 us: body(): valid = valid_mask.astype(F32).reshape(rows, 1)]
    ppermute x9 -> x6, waiting for transfers between devices: 16.1 us -> 8.25 us  [reduce_dp(): total = total + lax.ppermute(block, 'dp', pairs).astype(F32)]
    convert_element_type x8 -> x2, other arithmetic: 7.7 us -> 0.97 us  [the longest x1 0.97 us: body(): col_wgrad = exchange_dp(col_terms, n_dp).astype(BF16)]
  transfers between devices with their start and end apart: 28 -> 26, of which waited for: 11 -> 9; matrix products, arithmetic and copies ran while one was open for 22% -> 12% of each run, Pallas kernels for 0% -> 9%
where the time goes in v2:
time: 315 us; the launch traced here: 311 us
  waiting for transfers between devices  128 us (41%)
  Pallas kernels  79.8 us (25%)
  starting transfers between devices  33.5 us (11%)
  other arithmetic  22.8 us (7%)
  local copies, waits for them, and re-layouts  17.8 us (6%)
  between operations  17.7 us (6%)
  blocking collectives  10.8 us (3%)
    all_gather x1, waiting for transfers between devices, body(): lax.all_gather(low.reshape(tokens.shape), 'ctx', axis=1, tiled=True)  45.4 us
    reduce_scatter x1, waiting for transfers between devices, body(): lax.psum_scatter(terms.reshape(seqs, length, width), 'ctx', scatter_dimen...  44.3 us
    pallas_call x1, Pallas kernels, body(): kernel_call(functools.partial(backward_kernel, first_len, heads, size, sc...  23 us
    pallas_call x1, Pallas kernels, body(): kernel_call(functools.partial(forward_kernel, first_len, heads, size, sca...  23 us
    ppermute x9, waiting for transfers between devices, gather_dp(): other = lax.ppermute(block, 'dp', pairs)  17.7 us
    ppermute x9, starting transfers between devices, gather_dp(): other = lax.ppermute(block, 'dp', pairs)  14.1 us
    all_to_all x1, waiting for transfers between devices, body(): lax.all_to_all(cols, 'ctx', 0, 0, tiled=True)  12.1 us
    all_to_all x1, blocking collectives, body(): sums = lax.all_to_all(sums, both, 0, 0, tiled=True)  10.8 us
  transfers between devices with their start and end apart: 26, of which 9 were waited for; matrix products, arithmetic and copies ran while one was open for 12% of the time, Pallas kernels for 9%

profile of v2, /device:TPU:0, one launch (start us, length us, event | category | flops | bytes accessed | tf_op | source)
XLA Modules:
  0.0 310.9 jit_solution(12740944177526728988)
XLA Ops:
  7.9 2.0 pack_columns.1
  10.0 2.9 collective-permute-start.3
  12.9 1.5 collective-permute-start.4
  14.4 2.0 collective-permute-start.6
  16.4 1.5 collective-permute-start.7
  17.9 4.9 %all-to-all-start = ((bf16[8,32,1024]{2,1,0:T(8,128)(2,1)}), bf16[8,32,1024]{2,1,0:T(8,128)(2,1)S(1)}, u32[]{:S(2)}, u32[]{:S(2)}) async-start(bf16[8,32,1024]{2,1,0:T(8,128)(2,1)} %pack_columns.1), calls=%async_computation | async-start | bytes 1048576 | tf_op jit(solution)/shard_map/all_to_all | solution.py:500
  23.5 3.1 %collective-permute-done.6 = bf16[32,1024]{1,0:T(8,128)(2,1)} collective-permute-done((bf16[32,1024]{1,0:T(8,128)(2,1)}, bf16[32,1024]{1,0:T(8,128)(2,1)}, u32[]{:S(2)}, u32[]{:S(2)}) %collective-permute-start.6) | collective-permute-done | bytes 65568 | tf_op jit(solution)/shard_map/ppermute | solution.py:417
  26.6 2.7 collective-permute-start.8
  29.3 0.8 bitcast_dynamic-update-slice_fusion.10
  30.2 1.6 collective-permute-done.8
  32.5 5.2 %compare_select_fusion.9 = (f32[128]{0:T(128)S(1)}, f32[128]{0:T(128)S(1)}) fusion(f32[]{:T(128)} %bitcast.17, f32[]{:T(128)} %bitcast.16, f32[]{:T(128)} %bitcast.15, f32[]{:T(128)} %bitcast.14, f32[]{:T(128)} %bitcast.13, f32[]{:T(128)} %bitcast.12, f32[]{:T(128)} %bitcast.11, f32[]{:T(128)} %bitcast.10), kind=kLoop, calls=%fused_computation.77 | loop fusion | flops 5632 | bytes 1056 | tf_op jit(solution)/shard_map/jit(_where)/select_n | solution.py:536
  38.5 1.0 bitcast_dynamic-update-slice_fusion.6
  39.5 1.0 bitcast_dynamic-update-slice_fusion.5
  40.5 12.1 %all-to-all-done = bf16[8,32,1024]{2,1,0:T(8,128)(2,1)S(1)} async-done(((bf16[8,32,1024]{2,1,0:T(8,128)(2,1)}), bf16[8,32,1024]{2,1,0:T(8,128)(2,1)S(1)}, u32[]{:S(2)}, u32[]{:S(2)}) %all-to-all-start) | async-done | bytes 524320 | tf_op jit(solution)/shard_map/all_to_all | solution.py:500
  53.3 2.8 collective-permute-start.2
  56.1 2.2 convert_reduce_fusion
  58.3 5.7 %fusion = (f32[2048,128]{1,0:T(8,128)}, f32[2048,128]{1,0:T(8,128)}) fusion(f32[128]{0:T(128)S(1)} %get-tuple-element.131, f32[128]{0:T(128)S(1)} %get-tuple-element.132, f32[2048]{0:T(1024)S(1)} %bitcast.171), kind=kLoop, calls=%fused_computation.4 | loop fusion | flops 524288 | bytes 2106368 | tf_op jit(solution)/shard_map/mul | solution.py:536
  64.4 3.0 collective-permute-done
  67.5 9.9 %collective-permute-done.1 = bf16[256,1024]{1,0:T(8,128)(2,1)S(1)} collective-permute-done((bf16[256,1024]{1,0:T(8,128)(2,1)S(1)}, bf16[256,1024]{1,0:T(8,128)(2,1)S(1)}, u32[]{:S(2)}, u32[]{:S(2)}) %collective-permute-start.1) | collective-permute-done | bytes 524320 | tf_op jit(solution)/shard_map/ppermute | solution.py:417
  77.9 0.9 reshape_squeeze.15.gain
  80.8 23.0 %forward_kernel.1 = (bf16[2048,1024]{1,0:T(8,128)(2,1)}, bf16[2048,128]{1,0:T(8,128)(2,1)}, bf16[2048,128]{1,0:T(8,128)(2,1)}, bf16[2048,128]{1,0:T(8,128)(2,1)}...) custom-call(f32[1,1024]{1,0:T(1,128)} %reshape_squeeze.15.gain, ...), custom_call_target="tpu_custom_call" | custom-call | flops 10000000000 | bytes 20000000 | tf_op jit(solution)/shard_map/forward_kernel/pallas_call | solution.py:560
  104.5 0.8 copy.47.valid
  107.9 44.3 %reduce-scatter.3.cloned.1.call-done = bf16[2,128,1024]{2,1,0:T(8,128)(2,1)} async-done(((bf16[2,1024,1024]{2,1,0:T(8,128)(2,1)}), bf16[2,128,1024]{2,1,0:T(8,128)(2,1)}) %reduce-scatter.3.cloned.1.call-update) | async-done | bytes 524304 | tf_op jit(solution)/shard_map/reduce_scatter | solution.py:577
  152.2 3.2 %loss_kernel.1 = (bf16[256,1024]{1,0:T(8,128)(2,1)}, f32[256,1024]{1,0:T(8,128)}, bf16[256,1024]{1,0:T(8,128)(2,1)}, f32[1,1024]{1,0:T(1,128)}, f32[1,1]{1,0:T(1,128)}) custom-call(bf16[256,1024]{1,0:T(8,128)(2,1)} %bitcast.162, bf16[256,1024]{1,0:T(8,128)(2,1)} %bitcast.135, bf16[256,1024]{1,0:T(8,128)(2,1)} %bitcast.161, f32[256,1]{1,0:T(8,128)} %copy.47.valid, ...), custom_call_target="tpu_custom_call" | custom-call | flops 1000000 | bytes 3000000 | tf_op jit(solution)/shard_map/loss_kernel/pallas_call | solution.py:585
  155.5 45.4 %all-gather.5.cloned.1.call-done = bf16[2,1024,1024]{2,1,0:T(8,128)(2,1)} async-done(((bf16[2,128,1024]{2,1,0:T(8,128)(2,1)}), bf16[2,1024,1024]{2,1,0:T(8,128)(2,1)}) %all-gather.5.cloned.1.call-update) | async-done | bytes 4194320 | tf_op jit(solution)/shard_map/all_gather | solution.py:595
  200.9 23.0 %backward_kernel.1 = (bf16[2048,512]{1,0:T(8,128)(2,1)}, bf16[2048,384]{1,0:T(8,128)(2,1)}, bf16[2048,1024]{1,0:T(8,128)(2,1)}) custom-call(s32[2,1024]{1,0:T(2,128)} %seg_row.1, bf16[2048,1024]{1,0:T(8,128)(2,1)} %bitcast.140, f32[2048,512]{1,0:T(8,128)} %get-tuple-element.67.slope_in, bf16[2048,128]{1,0:T(8,128)(2,1)} %get-tuple-element.68.q_in, ...), custom_call_target="tpu_custom_call" | custom-call | flops 12000000000 | bytes 20000000 | tf_op jit(solution)/shard_map/backward_kernel/pallas_call | solution.py:598
  225.8 9.5 %column_kernel.1 = (f32[256,896]{1,0:T(8,128)}, bf16[256,896]{1,0:T(8,128)(2,1)}, bf16[256,896]{1,0:T(8,128)(2,1)}, bf16[256,896]{1,0:T(8,128)(2,1)}, f32[8,896]{1,0:T(8,128)}) custom-call(s32[4]{0:T(128)} %pad_add_fusion.order, bf16[2048,1024]{1,0:T(8,128)(2,1)} %get-tuple-element.65.n, bf16[2048,384]{1,0:T(8,128)(2,1)} %get-tuple-element.72.qg, ...), custom_call_target="tpu_custom_call" | custom-call | flops 4000000000 | bytes 10000000 | tf_op jit(solution)/shard_map/column_kernel/pallas_call | solution.py:619
  235.3 2.1 collective-permute-start.12
  238.0 0.8 collective-permute-start.10
  239.7 7.4 %sums_kernel.1 = (f32[1,1024]{1,0:T(1,128)}, f32[1,1024]{1,0:T(1,128)}) custom-call(bf16[2048,1024]{1,0:T(8,128)(2,1)} %bitcast.138, bf16[2048,1024]{1,0:T(8,128)(2,1)} %get-tuple-element.83.back), custom_call_target="tpu_custom_call" | custom-call | flops 1000000 | bytes 100000 | tf_op jit(solution)/shard_map/sums_kernel/pallas_call | solution.py:632
  247.1 1.3 reduce.29
  248.5 1.3 reduce.30
  251.6 10.8 %all_to_all.22 = f32[32,1,384]{2,1,0:T(1,128)S(1)} all-to-all(f32[32,1,384]{2,1,0:T(1,128)S(1)} %copy.50), channel_id=1, replica_groups=mesh['dp'=4,'ctx'=8] {'dp','ctx'}, dimensions={0} | all-to-all | bytes 98304 | tf_op jit(solution)/shard_map/all_to_all | solution.py:660
  262.4 1.0 add_convert_fusion
  263.4 6.7 %down_kernel.1 = (bf16[512,1024]{1,0:T(8,128)(2,1)}, bf16[128,1024]{1,0:T(8,128)(2,1)}) custom-call(bf16[2048,512]{1,0:T(8,128)(2,1)} %get-tuple-element.97.act, bf16[2048,128]{1,0:T(8,128)(2,1)} %get-tuple-element.98.mixed, bf16[2048,1024]{1,0:T(8,128)(2,1)} %bitcast.141), custom_call_target="tpu_custom_call" | custom-call | flops 1000000 | bytes 100000 | tf_op jit(solution)/shard_map/down_kernel/pallas_call | solution.py:674
  270.1 1.0 dynamic-slice_bitcast_fusion.3
  271.5 3.5 %all-to-all-start.2 = ((bf16[8,32,896]{2,1,0:T(8,128)(2,1)}), bf16[8,32,896]{2,1,0:T(8,128)(2,1)S(1)}, u32[]{:S(2)}, u32[]{:S(2)}) async-start(bf16[8,32,896]{2,1,0:T(8,128)(2,1)} %bitcast.57), calls=%async_computation.4 | async-start | bytes 917504 | tf_op jit(solution)/shard_map/all_to_all | solution.py:663
  275.0 0.9 bitcast_select_fusion
  276.1 0.8 collective-permute-start.16
  277.0 2.3 collective-permute-start.19
  280.5 1.3 collective-permute-start.15
  282.1 1.2 collective-permute-start.14
  286.2 7.9 %collective-permute-done.15 = bf16[32,1024]{1,0:T(8,128)(2,1)} collective-permute-done((bf16[32,1024]{1,0:T(8,128)(2,1)S(1)}, bf16[32,1024]{1,0:T(8,128)(2,1)}, u32[]{:S(2)}, u32[]{:S(2)}) %collective-permute-start.15) | collective-permute-done | bytes 65568 | tf_op jit(solution)/shard_map/ppermute | solution.py:437
  294.2 1.6 fusion.4
  295.8 1.0 fusion.2
  296.7 3.0 norm_back_kernel.1
  299.8 0.8 copy-done.1
  300.5 2.0 unpack_columns.1
  (119 shorter events, 18.4 us)
Async XLA Ops:
  7.2 16.1 %copy-start.6 = (bf16[32,1024]{1,0:T(8,128)(2,1)S(1)}, bf16[32,1024]{1,0:T(8,128)(2,1)}, u32[]{:S(2)}) copy-start(bf16[32,1024]{1,0:T(8,128)(2,1)} %param.23) | copy-start | bytes 196612
  7.2 73.6 %all-gather.3.cloned.1.call-start = ((), (), s32[]{:S(2)}) async-start(), calls=%async_computation.5 | async-start | bytes 4718592 | tf_op jit(solution)/shard_map/all_gather | solution.py:499
  7.9 15.5 %copy-start.5 = (bf16[128,1024]{1,0:T(8,128)(2,1)S(1)}, bf16[128,1024]{1,0:T(8,128)(2,1)}, u32[]{:S(2)}) copy-start(bf16[128,1024]{1,0:T(8,128)(2,1)} %param.27) | copy-start | bytes 786436
  10.0 28.5 %collective-permute-start.3 = (bf16[128,1024]{1,0:T(8,128)(2,1)}, bf16[128,1024]{1,0:T(8,128)(2,1)}, u32[]{:S(2)}, u32[]{:S(2)}) collective-permute-start(bf16[128,1024]{1,0:T(8,128)(2,1)} %param.27), channel_id=1, source_target_pairs={{0,8},{8,0},{16,24},{24,16},{1,9},{9,1},{17,25},{25,17},{2,10},{10... | collective-permute-start | bytes 786440 | tf_op jit(solution)/shard_map/ppermute | solution.py:417
  12.9 26.6 %collective-permute-start.4 = (bf16[128,1024]{1,0:T(8,128)(2,1)}, bf16[128,1024]{1,0:T(8,128)(2,1)}, u32[]{:S(2)}, u32[]{:S(2)}) collective-permute-start(bf16[128,1024]{1,0:T(8,128)(2,1)} %param.27), channel_id=1, source_target_pairs={{0,16},{8,24},{16,0},{24,8},{1,17},{9,25},{17,1},{25,9},{2,18},{10... | collective-permute-start | bytes 786440 | tf_op jit(solution)/shard_map/ppermute | solution.py:417
  14.4 26.0 %collective-permute-start.5 = (bf16[128,1024]{1,0:T(8,128)(2,1)}, bf16[128,1024]{1,0:T(8,128)(2,1)S(1)}, u32[]{:S(2)}, u32[]{:S(2)}) collective-permute-start(bf16[128,1024]{1,0:T(8,128)(2,1)} %param.27), channel_id=1, source_target_pairs={{0,24},{8,16},{16,8},{24,0},{1,25},{9,17},{17,9},{25,1},{2,26},{10... | collective-permute-start | bytes 786440 | tf_op jit(solution)/shard_map/ppermute | solution.py:417
  14.4 12.2 %collective-permute-start.6 = (bf16[32,1024]{1,0:T(8,128)(2,1)}, bf16[32,1024]{1,0:T(8,128)(2,1)}, u32[]{:S(2)}, u32[]{:S(2)}) collective-permute-start(bf16[32,1024]{1,0:T(8,128)(2,1)} %param.23), channel_id=1, source_target_pairs={{0,8},{8,0},{16,24},{24,16},{1,9},{9,1},{17,25},{25,17},{2,10},{10... | collective-permute-start | bytes 196616 | tf_op jit(solution)/shard_map/ppermute | solution.py:417
  16.4 13.7 %collective-permute-start.7 = (bf16[32,1024]{1,0:T(8,128)(2,1)}, bf16[32,1024]{1,0:T(8,128)(2,1)S(1)}, u32[]{:S(2)}, u32[]{:S(2)}) collective-permute-start(bf16[32,1024]{1,0:T(8,128)(2,1)} %param.23), channel_id=1, source_target_pairs={{0,16},{8,24},{16,0},{24,8},{1,17},{9,25},{17,1},{25,9},{2,18},{10... | collective-permute-start | bytes 196616 | tf_op jit(solution)/shard_map/ppermute | solution.py:417
  17.9 34.7 %all-to-all-start = ((bf16[8,32,1024]{2,1,0:T(8,128)(2,1)}), bf16[8,32,1024]{2,1,0:T(8,128)(2,1)S(1)}, u32[]{:S(2)}, u32[]{:S(2)}) async-start(bf16[8,32,1024]{2,1,0:T(8,128)(2,1)} %pack_columns.1), calls=%async_computation | async-start | bytes 1048576 | tf_op jit(solution)/shard_map/all_to_all | solution.py:500
  22.8 129.5 %reduce-scatter.3.cloned.1.call-start = ((), (), s32[]{:S(2)}) async-start(), calls=%async_computation.6 | async-start | bytes 4718592 | tf_op jit(solution)/shard_map/reduce_scatter | solution.py:577
  23.4 32.7 %copy-start.7 = (s32[2,1024]{1,0:T(2,128)S(1)}, s32[2,1024]{1,0:T(2,128)}, u32[]{:S(2)}) copy-start(s32[2,1024]{1,0:T(2,128)} %seg_row.1) | copy-start | bytes 24580
  26.6 5.2 %collective-permute-start.8 = (bf16[32,1024]{1,0:T(8,128)(2,1)S(1)}, bf16[32,1024]{1,0:T(8,128)(2,1)S(1)}, u32[]{:S(2)}, u32[]{:S(2)}) collective-permute-start(bf16[32,1024]{1,0:T(8,128)(2,1)S(1)} %copy-done.6), channel_id=1, source_target_pairs={{0,24},{8,16},{16,8},{24,0},{1,25},{9,17},{17,9},{25,1},{2,26},{10... | collective-permute-start | bytes 196616 | tf_op jit(solution)/shard_map/ppermute | solution.py:417
  31.8 5.9 %collective-permute-start.9 = (bf16[2,32,1024]{2,1,0:T(8,128)(2,1)S(1)}, bf16[2,32,1024]{2,1,0:T(8,128)(2,1)S(1)}, u32[]{:S(2)}, u32[]{:S(2)}) collective-permute-start(bf16[2,32,1024]{2,1,0:T(8,128)(2,1)S(1)} %dynamic-slice_bitcast_fusion.4), channel_id=1, source_target_pairs={{0,1},{1,0},{2,3},{3,2},{4,5},{5,4},{6,7},{7,6},{8,9},{9,8},{10,11... | collective-permute-start | bytes 393224 | tf_op jit(solution)/shard_map/ppermute | solution.py:542
  40.5 17.8 %copy-start.3 = (bf16[4,128,1024]{2,1,0:T(8,128)(2,1)}, bf16[4,128,1024]{2,1,0:T(8,128)(2,1)S(1)}, u32[]{:S(2)}) copy-start(bf16[4,128,1024]{2,1,0:T(8,128)(2,1)S(1)} %bitcast_dynamic-update-slice_fusion.4) | copy-start | bytes 3145732
  52.6 14.8 %collective-permute-start = (bf16[256,1024]{1,0:T(8,128)(2,1)S(1)}, bf16[256,1024]{1,0:T(8,128)(2,1)S(1)}, u32[]{:S(2)}, u32[]{:S(2)}) collective-permute-start(bf16[256,1024]{1,0:T(8,128)(2,1)S(1)} %bitcast.145), channel_id=1, source_target_pairs={{0,8},{8,0},{16,24},{24,16},{1,9},{9,1},{17,25},{25,17},{2,10},{10... | collective-permute-start | bytes 1572872 | tf_op jit(solution)/shard_map/ppermute | solution.py:417
  53.2 24.1 %collective-permute-start.1 = (bf16[256,1024]{1,0:T(8,128)(2,1)S(1)}, bf16[256,1024]{1,0:T(8,128)(2,1)S(1)}, u32[]{:S(2)}, u32[]{:S(2)}) collective-permute-start(bf16[256,1024]{1,0:T(8,128)(2,1)S(1)} %bitcast.146), channel_id=1, source_target_pairs={{0,16},{8,24},{16,0},{24,8},{1,17},{9,25},{17,1},{25,9},{2,18},{10... | collective-permute-start | bytes 1572872 | tf_op jit(solution)/shard_map/ppermute | solution.py:417
  53.3 24.2 %collective-permute-start.2 = (bf16[256,1024]{1,0:T(8,128)(2,1)S(1)}, bf16[256,1024]{1,0:T(8,128)(2,1)S(1)}, u32[]{:S(2)}, u32[]{:S(2)}) collective-permute-start(bf16[256,1024]{1,0:T(8,128)(2,1)S(1)} %bitcast.147), channel_id=1, source_target_pairs={{0,24},{8,16},{16,8},{24,0},{1,25},{9,17},{17,9},{25,1},{2,26},{10... | collective-permute-start | bytes 1572872 | tf_op jit(solution)/shard_map/ppermute | solution.py:417
  77.5 3.3 %copy-start = (bf16[4,256,1024]{2,1,0:T(8,128)(2,1)}, bf16[4,256,1024]{2,1,0:T(8,128)(2,1)S(1)}, u32[]{:S(2)}) copy-start(bf16[4,256,1024]{2,1,0:T(8,128)(2,1)S(1)} %bitcast_dynamic-update-slice_fusion) | copy-start | bytes 6291460
  103.8 0.7 copy-start.9
  103.8 97.1 %all-gather.5.cloned.1.call-start = ((), (), s32[]{:S(2)}) async-start(), calls=%async_computation.7 | async-start | bytes 4718592 | tf_op jit(solution)/shard_map/all_gather | solution.py:595
  155.4 141.3 %reduce-scatter.5.cloned.1.call-start = ((), (), s32[]{:S(2)}) async-start(), calls=%async_computation.8 | async-start | bytes 4718592 | tf_op jit(solution)/shard_map/reduce_scatter | solution.py:612
  223.9 1.1 copy-start.8
  235.3 27.0 %collective-permute-start.12 = (bf16[256,896]{1,0:T(8,128)(2,1)}, bf16[256,896]{1,0:T(8,128)(2,1)S(1)}, u32[]{:S(2)}, u32[]{:S(2)}) collective-permute-start(bf16[256,896]{1,0:T(8,128)(2,1)} %get-tuple-element.81), channel_id=1, source_target_pairs={{0,24},{8,16},{16,8},{24,0},{1,25},{9,17},{17,9},{25,1},{2,26},{10... | collective-permute-start | bytes 1376264 | tf_op jit(solution)/shard_map/ppermute | solution.py:426
  237.5 24.9 %collective-permute-start.11 = (bf16[256,896]{1,0:T(8,128)(2,1)}, bf16[256,896]{1,0:T(8,128)(2,1)S(1)}, u32[]{:S(2)}, u32[]{:S(2)}) collective-permute-start(bf16[256,896]{1,0:T(8,128)(2,1)} %get-tuple-element.80), channel_id=1, source_target_pairs={{0,16},{8,24},{16,0},{24,8},{1,17},{9,25},{17,1},{25,9},{2,18},{10... | collective-permute-start | bytes 1376264 | tf_op jit(solution)/shard_map/ppermute | solution.py:426
  238.0 24.4 %collective-permute-start.10 = (bf16[256,896]{1,0:T(8,128)(2,1)}, bf16[256,896]{1,0:T(8,128)(2,1)S(1)}, u32[]{:S(2)}, u32[]{:S(2)}) collective-permute-start(bf16[256,896]{1,0:T(8,128)(2,1)} %get-tuple-element.79), channel_id=1, source_target_pairs={{0,8},{8,0},{16,24},{24,16},{1,9},{9,1},{17,25},{25,17},{2,10},{10... | collective-permute-start | bytes 1376264 | tf_op jit(solution)/shard_map/ppermute | solution.py:426
  239.7 22.7 %copy-start.4 = (f32[256,896]{1,0:T(8,128)S(1)}, f32[256,896]{1,0:T(8,128)}, u32[]{:S(2)}) copy-start(f32[256,896]{1,0:T(8,128)} %get-tuple-element.78) | copy-start | bytes 2752516
  270.1 6.8 %copy-start.2 = (bf16[512,1024]{1,0:T(8,128)(2,1)S(1)}, bf16[512,1024]{1,0:T(8,128)(2,1)}, u32[]{:S(2)}) copy-start(bf16[512,1024]{1,0:T(8,128)(2,1)} %get-tuple-element.101) | copy-start | bytes 3145732
  271.1 3.9 %collective-permute-start.13 = (bf16[2,32,1024]{2,1,0:T(8,128)(2,1)S(1)}, bf16[2,32,1024]{2,1,0:T(8,128)(2,1)S(1)}, u32[]{:S(2)}, u32[]{:S(2)}) collective-permute-start(bf16[2,32,1024]{2,1,0:T(8,128)(2,1)S(1)} %dynamic-slice_bitcast_fusion.3), channel_id=1, source_target_pairs={{0,1},{1,0},{2,3},{3,2},{4,5},{5,4},{6,7},{7,6},{8,9},{9,8},{10,11... | collective-permute-start | bytes 393224 | tf_op jit(solution)/shard_map/ppermute | solution.py:683
  271.5 28.2 %all-to-all-start.2 = ((bf16[8,32,896]{2,1,0:T(8,128)(2,1)}), bf16[8,32,896]{2,1,0:T(8,128)(2,1)S(1)}, u32[]{:S(2)}, u32[]{:S(2)}) async-start(bf16[8,32,896]{2,1,0:T(8,128)(2,1)} %bitcast.57), calls=%async_computation.4 | async-start | bytes 917504 | tf_op jit(solution)/shard_map/all_to_all | solution.py:663
  276.1 6.0 %collective-permute-start.16 = (bf16[32,1024]{1,0:T(8,128)(2,1)S(1)}, bf16[32,1024]{1,0:T(8,128)(2,1)}, u32[]{:S(2)}, u32[]{:S(2)}) collective-permute-start(bf16[32,1024]{1,0:T(8,128)(2,1)S(1)} %get-tuple-element.116), channel_id=1, source_target_pairs={{0,24},{8,16},{16,8},{24,0},{1,25},{9,17},{17,9},{25,1},{2,26},{10... | collective-permute-start | bytes 196616 | tf_op jit(solution)/shard_map/ppermute | solution.py:437
  277.0 18.8 %collective-permute-start.19 = (bf16[128,1024]{1,0:T(8,128)(2,1)S(1)}, bf16[128,1024]{1,0:T(8,128)(2,1)S(1)}, u32[]{:S(2)}, u32[]{:S(2)}) collective-permute-start(bf16[128,1024]{1,0:T(8,128)(2,1)S(1)} %get-tuple-element.108), channel_id=1, source_target_pairs={{0,24},{8,16},{16,8},{24,0},{1,25},{9,17},{17,9},{25,1},{2,26},{10... | collective-permute-start | bytes 786440 | tf_op jit(solution)/shard_map/ppermute | solution.py:437
  279.2 16.5 %collective-permute-start.18 = (bf16[128,1024]{1,0:T(8,128)(2,1)S(1)}, bf16[128,1024]{1,0:T(8,128)(2,1)S(1)}, u32[]{:S(2)}, u32[]{:S(2)}) collective-permute-start(bf16[128,1024]{1,0:T(8,128)(2,1)S(1)} %get-tuple-element.109), channel_id=1, source_target_pairs={{0,16},{8,24},{16,0},{24,8},{1,17},{9,25},{17,1},{25,9},{2,18},{10... | collective-permute-start | bytes 786440 | tf_op jit(solution)/shard_map/ppermute | solution.py:437
  279.8 16.0 %collective-permute-start.17 = (bf16[128,1024]{1,0:T(8,128)(2,1)S(1)}, bf16[128,1024]{1,0:T(8,128)(2,1)S(1)}, u32[]{:S(2)}, u32[]{:S(2)}) collective-permute-start(bf16[128,1024]{1,0:T(8,128)(2,1)S(1)} %get-tuple-element.107), channel_id=1, source_target_pairs={{0,8},{8,0},{16,24},{24,16},{1,9},{9,1},{17,25},{25,17},{2,10},{10... | collective-permute-start | bytes 786440 | tf_op jit(solution)/shard_map/ppermute | solution.py:437
  280.5 13.7 %collective-permute-start.15 = (bf16[32,1024]{1,0:T(8,128)(2,1)S(1)}, bf16[32,1024]{1,0:T(8,128)(2,1)}, u32[]{:S(2)}, u32[]{:S(2)}) collective-permute-start(bf16[32,1024]{1,0:T(8,128)(2,1)S(1)} %get-tuple-element.115), channel_id=1, source_target_pairs={{0,16},{8,24},{16,0},{24,8},{1,17},{9,25},{17,1},{25,9},{2,18},{10... | collective-permute-start | bytes 196616 | tf_op jit(solution)/shard_map/ppermute | solution.py:437
  282.1 12.1 %collective-permute-start.14 = (bf16[32,1024]{1,0:T(8,128)(2,1)S(1)}, bf16[32,1024]{1,0:T(8,128)(2,1)S(1)}, u32[]{:S(2)}, u32[]{:S(2)}) collective-permute-start(bf16[32,1024]{1,0:T(8,128)(2,1)S(1)} %get-tuple-element.114), channel_id=1, source_target_pairs={{0,8},{8,0},{16,24},{24,16},{1,9},{9,1},{17,25},{25,17},{2,10},{10... | collective-permute-start | bytes 196616 | tf_op jit(solution)/shard_map/ppermute | solution.py:437
  283.9 18.7 %copy-start.10 = (f32[32]{0:T(128)}, f32[32]{0:T(128)S(1)}, u32[]{:S(2)}) copy-start(f32[32]{0:T(128)S(1)} %get-tuple-element.160) | copy-start | bytes 388
  299.8 0.8 copy-start.1
Sparse Core Ops, SparseCore 0:
  9.6 60.9 all-gather.2
  103.9 48.2 reduce-scatter.2
  155.6 45.2 all-gather.4
  224.1 49.4 reduce-scatter.4

commit v3 on v2

--- a/solution.py
+++ b/solution.py
@@ -149,9 +149,9 @@
             up = mm(low, wup[...]) + bup[...]
             cdf = 0.5 * (1.0 + lax.erf(up * math.sqrt(0.5)))
             act[rows, :] = (up * cdf).astype(BF16)
-            slope[rows, :] = cdf + up * jnp.exp(-0.5 * up * up) * (
-                1.0 / math.sqrt(2.0 * math.pi)
-            )
+            slope[rows, :] = (
+                cdf + up * jnp.exp(-0.5 * up * up) * (1.0 / math.sqrt(2.0 * math.pi))
+            ).astype(BF16)
             out += copier.rows(((act, act_out), (slope, slope_out)), at, step)
         for start, low in block_spans(length, first_len):
             rows, cols = slice(origin + start, origin + start + BLK), slice(
@@ -182,36 +182,42 @@
 
 
 def backward_kernel(
-    first_len, heads, size, scale, length, step,
-    seg_row,
-    g_in, slope_in, q_in, k_in, v_in, stat_in, cos_in, sin_in, wdown_in, wproj_in, *refs,
+    first_len, heads, size, scale, length, step, cut,
+    order, seg_row, g_in, slope_in, q_in, k_in, v_in, stat_in, cos_in, sin_in, x_in, n_in,
+    act_in, mixed_in, wdown_in, wproj_in, *refs,
 ):
-    (g, slope, q, k, v, stat, cosine, sine, wdown, wproj,
-     mg, ug, qg, dk, dv, back, sems) = refs[-17:]
-    split = (len(refs) - 20) // 2
-    w_in, w = refs[:split], refs[split + 3 : 2 * split + 3]
-    ug_out, qg_out, back_out = refs[split : split + 3]
+    (g, slope, q, k, v, stat, cosine, sine, x, normed, act, mixed, wdown, wproj,
+     mg, ug, qg, dk, dv, sems) = refs[-20:]
+    split = 1 if refs[0].shape[1] > 3 * heads * size else 2
+    w_in, refs = refs[:split], refs[split:-20]
+    back_out, gain_sum, shift_sum, up_sum, qkv_sum, pw = refs[:6]
+    outs, w = refs[6 : len(refs) - split], refs[len(refs) - split :]
+    col_out, down_out = outs[: len(outs) // 2], outs[len(outs) // 2 :]
+    for ref in (gain_sum, shift_sum, up_sum, qkv_sum):
+        ref[...] = jnp.zeros_like(ref)
     copier = Copier(sems)
     width = heads * size
     wqkv, wup = view_columns(w, width, ug.shape[1])
     total = g.shape[0]
-    starts = range(0, total, step)
     loads = ((g_in, g), (slope_in, slope))
     saved = (
         (q_in, q), (k_in, k), (v_in, v), (stat_in, stat), (cos_in, cosine), (sin_in, sine)
     )
-    g_copies = {0: copier.rows(loads[:1], 0, step)}
-    w_copies = [copier.start(wdown_in, wdown)]
-    g_copies[0] += copier.rows(loads[1:], 0, step)
-    w_copies.append(copier.start(wproj_in, wproj))
-    s_copies = {}
-    for at in starts[1:]:
-        g_copies[at] = copier.rows(loads, at, step)
+    g_copies, s_copies, x_copies = {}, {}, {}
+    for at in range(0, total, step):
+        g_copies[at] = copier.rows(loads[:1], at, step)
+        if at == 0:
+            w_copies = [copier.start(wdown_in, wdown)]
+        g_copies[at] += copier.rows(loads[1:], at, step)
+        if at == 0:
+            w_copies.append(copier.start(wproj_in, wproj))
         if (at + step) % length == 0:
             origin = at + step - length
             s_copies[origin] = copier.rows(saved, origin, length)
             if origin == 0:
                 w_copies += [copier.start(a, b) for a, b in zip(w_in, w)]
+            x_copies[origin] = copier.rows([(x_in, x)], origin, length)
+    late = [copier.start(a, b) for a, b in ((act_in, act), (mixed_in, mixed), (n_in, normed))]
     out = []
     for seq in range(total // length):
         origin = seq * length
@@ -221,8 +227,9 @@
             if at == 0:
                 wait_all(w_copies[:2])
             grad = g[rows, :]
-            ug[rows, :] = (mm(grad, wdown[...], LAST) * slope[rows, :]).astype(BF16)
-            out += copier.rows([(ug, ug_out)], at, step)
+            up_grad = (mm(grad, wdown[...], LAST) * slope[rows, :].astype(F32)).astype(BF16)
+            ug[rows, :] = up_grad
+            up_sum[...] += jnp.sum(up_grad.astype(F32), axis=0, keepdims=True)
             mg[rows, :] = mm(grad, wproj[...], LAST).astype(BF16)
         dk[...] = jnp.zeros_like(dk)
         dv[...] = jnp.zeros_like(dv)
@@ -252,48 +259,32 @@
             dk[...], cosine[rows, :], -sine[rows, :], size
         ).astype(BF16)
         qg[rows, 2 * width :] = dv[...].astype(BF16)
-        out += copier.rows([(qg, qg_out)], origin, length)
+        wait_all(x_copies[origin])
         if seq == 0:
             wait_all(w_copies[2:])
         for at in range(origin, origin + length, step):
             rows = slice(at, at + step)
-            back[rows, :] = (
-                mm(ug[rows, :], wup[...], LAST) + mm(qg[rows, :], wqkv[...], LAST)
-            ).astype(BF16)
-            out += copier.rows([(back, back_out)], at, step)
+            terms = mm(ug[rows, :], wup[...], LAST) + mm(qg[rows, :], wqkv[...], LAST)
+            standard, _ = standardize(x[rows, :].astype(F32))
+            x[rows, :] = terms.astype(BF16)
+            out += copier.rows([(x, back_out)], at, step)
+            gain_sum[...] += jnp.sum(terms * standard, axis=0, keepdims=True)
+            shift_sum[...] += jnp.sum(terms, axis=0, keepdims=True)
+            qkv_sum[...] += jnp.sum(qg[rows, :].astype(F32), axis=0, keepdims=True)
+    wait_all(late)
+    for left, rights, parts in ((act, (g,), down_out), (normed, (qg, ug), col_out)):
+        rows = parts[0].shape[0]
+        for i, part in enumerate(parts):
+            block = left[...]
+            if cut:
+                block = left[:, pl.ds(pl.multiple_of(order[i] * rows, rows), rows)]
+            column = 0
+            for right in rights:
+                stop = column + right.shape[1]
+                part[:, column:stop] = mm(block, right[...], FIRST).astype(part.dtype)
+                column = stop
+    pw[...] = mm(mixed[...], g[...], FIRST).astype(BF16)
     wait_all(out)
-
-
-def column_kernel(cut, order, n, qg, ug, *outs):
-    outs, sums = outs[:-1], outs[-1]
-    rows, split = outs[0].shape[0], qg.shape[1]
-    ones = jnp.ones((8, n.shape[0]), BF16)
-    sums[:, :split] = mm(ones, qg[...])
-    sums[:, split:] = mm(ones, ug[...])
-    for k in list(range(1, len(outs))) + [0]:
-        if cut:
-            block = n[:, pl.ds(pl.multiple_of(order[k] * rows, rows), rows)]
-        else:
-            block = n[...]
-        outs[k][:, :split] = mm(block, qg[...], FIRST).astype(outs[k].dtype)
-        outs[k][:, split:] = mm(block, ug[...], FIRST).astype(outs[k].dtype)
-
-
-def down_kernel(act, mixed, g, dw, pw):
-    dw[...] = mm(act[...], g[...], FIRST).astype(BF16)
-    pw[...] = mm(mixed[...], g[...], FIRST).astype(BF16)
-
-
-def sums_kernel(x, back, gain_sum, shift_sum):
-    @pl.when(pl.program_id(0) == 0)
-    def _():
-        for ref in (gain_sum, shift_sum):
-            ref[...] = jnp.zeros_like(ref)
-
-    standard, _ = standardize(x[...].astype(F32))
-    terms = back[...].astype(F32)
-    gain_sum[...] += jnp.sum(terms * standard, axis=0, keepdims=True)
-    shift_sum[...] += jnp.sum(terms, axis=0, keepdims=True)
 
 
 def loss_kernel(branch, x, teacher, valid, bias, factor, out, grad, low, column, square):
@@ -425,6 +416,12 @@
         pairs = [(i, i ^ k) for i in range(n_dp)]
         total = total + lax.ppermute(terms[k], "dp", pairs).astype(F32)
     return total
+
+
+def reduce_blocks(terms, cut, n_dp, me_dp):
+    if cut:
+        return exchange_dp(terms, n_dp)
+    return reduce_dp(terms[0], n_dp, me_dp)
 
 
 def reduce_dp(terms, n_dp, me_dp):
@@ -495,7 +492,8 @@
             ],
             axis=2,
         )
-    cols, down_weight, proj_weight = lax.optimization_barrier((cols, down_weight, proj_weight))
+    tied = jnp.concatenate([down_weight, proj_weight], axis=0) if paired else down_weight
+    cols, tied = lax.optimization_barrier((cols, tied))
     x_rows = lax.all_gather(tokens, "ctx", axis=1, tiled=True).reshape(all_rows, width)
     cols = lax.all_to_all(cols, "ctx", 0, 0, tiled=True).reshape(n_ctx * own, total_cols)
     cols, segments = lax.optimization_barrier((cols, segments))
@@ -535,9 +533,10 @@
     cosine = jnp.cos(angles)
     sine = jnp.sin(angles) * jnp.where(lane < half, -1.0, 1.0)
 
-    w_down = gather_dp(down_weight, n_dp, me_dp)
+    tied = gather_dp(tied, n_dp, me_dp).reshape(n_dp, -1, width)
+    w_down = tied[:, :unit_rows].reshape(units, width)
     if paired:
-        halves = gather_dp(proj_weight, n_dp, me_dp).reshape(2, heads, own, width)
+        halves = tied[:, unit_rows:].reshape(2, heads, own, width)
         keep = lax.dynamic_index_in_dim(halves, me_core, 0, keepdims=False)
         got = lax.ppermute(
             lax.dynamic_index_in_dim(halves, 1 - me_core, 0, keepdims=False), "ctx", swap
@@ -562,12 +561,12 @@
         "forward_kernel",
         [LOCAL] * 5 + [HBM] * (5 + len(w_split)),
         [
-            store(width), store(part), store(part), store(part), store(units), store(units, F32),
+            store(width), store(part), store(part), store(part), store(units), store(units),
             store(part), store(part, F32), store(width),
         ],
         [
             *w_scratch, wide(width), wide(part, F32), wide(part, F32), *weights,
-            wide(width), wide(part), wide(part), wide(part), wide(units), wide(units, F32),
+            wide(width), wide(part), wide(part), wide(part), wide(units), wide(units),
             wide(part), wide(part, F32), wide(width), sems,
         ],
         flops=10 * 10**9, moved=2 * 10**7,
@@ -595,47 +594,43 @@
     grads = lax.all_gather(
         low.reshape(tokens.shape), "ctx", axis=1, tiled=True
     ).reshape(all_rows, width)
-    up_grad, qkv_grad, back = kernel_call(
-        functools.partial(backward_kernel, first_len, heads, size, scale, length, STEP),
+    order = jnp.stack([me_dp ^ k for k in range(n_dp)]).astype(jnp.int32)
+    cut = (width // n_dp) % 128 == 0 and unit_rows % 128 == 0
+
+    def blocks_of(rows_out, columns):
+        if not cut:
+            return [(LOCAL, shape_of((rows_out, columns), BF16))]
+        block = (rows_out // n_dp, columns)
+        return [(LOCAL, shape_of(block, BF16 if k else F32)) for k in range(n_dp)]
+
+    back, gain_sum, shift_sum, up_bsum, qkv_bsum, proj_wgrad, *terms = kernel_call(
+        functools.partial(backward_kernel, first_len, heads, size, scale, length, STEP, cut),
         "backward_kernel",
-        [LOCAL] + [HBM] * (10 + len(w_split)),
-        [store(units), store(3 * part), store(width)],
+        [SCALAR, LOCAL] + [HBM] * (14 + len(w_split)),
         [
-            *w_scratch, wide(width), wide(units, F32), wide(part), wide(part), wide(part),
-            wide(part, F32), wide(part, F32), wide(part, F32), *weights, wide(part), wide(units), wide(3 * part),
-            pltpu.VMEM((length, part), F32), pltpu.VMEM((length, part), F32), wide(width), sems,
+            store(width),
+            *[(LOCAL, shape_of((1, a), F32)) for a in (width, width, units, 3 * part)],
+            (LOCAL, shape_of((part, width), BF16)), *blocks_of(width, 3 * part + units),
+            *blocks_of(units, width),
+        ],
+        [
+            *w_scratch, wide(width), wide(units), wide(part), wide(part), wide(part),
+            wide(part, F32), wide(part, F32), wide(part, F32), wide(width), wide(width),
+            wide(units), wide(part), *weights, wide(part), wide(units), wide(3 * part), pltpu.VMEM((length, part), F32),
+            pltpu.VMEM((length, part), F32), sems,
         ],
         flops=12 * 10**9, moved=2 * 10**7,
     )(
-        segments, grads, slope, query, key, value, stat, cosine, sine, w_down, w_proj, *w_split
-    )
+        order, segments, grads, slope, query, key, value, stat, cosine, sine, x_rows, normed,
+        act, mixed, w_down, w_proj, *w_split,
+    )
+    col_terms, down_terms = terms[: len(terms) // 2], terms[len(terms) // 2 :]
     normed_grad = lax.psum_scatter(
         back.reshape(seqs, length, width), "ctx", scatter_dimension=1, tiled=True
     ).reshape(rows, width)
 
-    order = jnp.stack([me_dp ^ k for k in range(n_dp)]).astype(jnp.int32)
-    cut = (width // n_dp) % 128 == 0
-    block = (width // n_dp if cut else width, 3 * part + units)
-    *col_terms, col_sums = kernel_call(
-        functools.partial(column_kernel, cut), "column_kernel",
-        [SCALAR] + [LOCAL] * 3,
-        [(LOCAL, shape_of(block, BF16 if k else F32)) for k in range(n_dp if cut else 1)]
-        + [(LOCAL, shape_of((8, block[1]), F32))],
-        flops=4 * 10**9, moved=10**7,
-    )(order, normed, qkv_grad, up_grad)
-    col_terms, x_rows = lax.optimization_barrier((col_terms, x_rows))
-    if cut:
-        col_wgrad = exchange_dp(col_terms, n_dp).astype(BF16)
-    else:
-        col_wgrad = reduce_dp(col_terms[0].astype(BF16), n_dp, me_dp).astype(BF16)
-    sum_rows = 512
-    gain_sum, shift_sum = kernel_call(
-        sums_kernel, "sums_kernel",
-        [row_spec(sum_rows, width)] * 2,
-        [(whole_spec(1, width), shape_of((1, width), F32))] * 2,
-        flops=10**6, moved=10**5, grid=(all_rows // sum_rows,),
-    )(x_rows, back)
-    qkv_bsum, up_bsum = col_sums[:1, : 3 * part], col_sums[:1, 3 * part :]
+    col_wgrad = reduce_blocks(col_terms, cut, n_dp, me_dp).astype(BF16)
+
     if paired:
         qkv_bsum = lax.dynamic_update_slice(
             jnp.zeros((3, 2, heads, n_ctx // 2, size), F32),
@@ -659,7 +654,6 @@
     sums = jnp.pad(sums, ((0, 0), (0, -sums.shape[1] % 128)))
     sums = lax.all_to_all(sums, both, 0, 0, tiled=True)
     col_wgrad, sums = lax.optimization_barrier((col_wgrad, sums))
-    col_wgrad, act = lax.optimization_barrier((col_wgrad, act))
     col_wgrad = lax.all_to_all(
         col_wgrad.reshape(n_ctx, own, 3 * part + units), "ctx", 0, 0, tiled=True
     )
@@ -671,12 +665,7 @@
     up_bgrad = sums[6 * own : 6 * own + unit_rows]
     loss = sums[6 * own + unit_rows] / (valid_count * width)
 
-    down_wgrad, proj_wgrad = kernel_call(
-        down_kernel, "down_kernel", [LOCAL] * 3,
-        [(LOCAL, shape_of((units, width), BF16)), (LOCAL, shape_of((part, width), BF16))],
-        flops=10**6, moved=10**5,
-    )(act, mixed, grads)
-    down_wgrad = reduce_dp(down_wgrad, n_dp, me_dp)
+    down_wgrad = reduce_blocks(down_terms, cut, n_dp, me_dp)
     if paired:
         halves = proj_wgrad.reshape(heads, 2, own, width)
         keep = lax.dynamic_index_in_dim(halves, me_core, 1, keepdims=False)
@@ -695,7 +684,6 @@
         norm_back_kernel, "norm_back_kernel", [LOCAL] * 4, [(LOCAL, shape_of(own_block, BF16))],
         flops=10**6, moved=3 * 10**6,
     )(normed_grad, tokens_rows, out_grad, gain)
-    input_grad, col_wgrad = lax.optimization_barrier((input_grad, col_wgrad))
     if aligned:
         qkv_wgrad, up_wgrad = pl.pallas_call(
             functools.partial(unpack_columns, heads, size, paired, units, n_dp, n_ctx),

time: 315 us -> 306 us (0.971)
  Pallas kernels: 79.8 us -> 65.8 us
  blocking collectives: 10.8 us -> 20.1 us
  waiting for transfers between devices: 128 us -> 134 us
  starting transfers between devices: 33.5 us -> 28 us
    pallas_call x3 -> x0, Pallas kernels: 23.6 us -> none  [the longest x1 9.54 us: body(): kernel_call(functools.partial(column_kernel, cut), 'column_kernel', [SCAL...]
    ppermute x3 -> x6, waiting for transfers between devices: 0.01 us -> 10.2 us  [exchange_dp(): total = total + lax.ppermute(terms[k], 'dp', pairs).astype(F32)]
    pallas_call x1, Pallas kernels: 23 us -> 32.6 us  [body(): kernel_call(functools.partial(backward_kernel, first_len, heads, size, sc...]
    all_to_all x1, blocking collectives: 10.8 us -> 20.1 us  [body(): sums = lax.all_to_all(sums, both, 0, 0, tiled=True)]
    ppermute x6 -> x3, waiting for transfers between devices: 8.25 us -> 0.53 us  [reduce_dp(): total = total + lax.ppermute(block, 'dp', pairs).astype(F32)]
    ppermute x9 -> x6, starting transfers between devices: 14.1 us -> 8.03 us  [gather_dp(): other = lax.ppermute(block, 'dp', pairs)]
    ppermute x9 -> x6, waiting for transfers between devices: 17.7 us -> 22.3 us  [gather_dp(): other = lax.ppermute(block, 'dp', pairs)]
    ppermute x3 -> x6, starting transfers between devices: 3.49 us -> 6.98 us  [exchange_dp(): total = total + lax.ppermute(terms[k], 'dp', pairs).astype(F32)]
  transfers between devices with their start and end apart: 26 -> 23, of which waited for: 9 -> 12; matrix products, arithmetic and copies ran while one was open for 12% -> 11% of each run, Pallas kernels for 9% -> 1%
where the time goes in v3:
time: 306 us; the launch traced here: 302 us
  waiting for transfers between devices  134 us (44%)
  Pallas kernels  65.8 us (22%)
  starting transfers between devices  28 us (9%)
  other arithmetic  20.7 us (7%)
  blocking collectives  20.1 us (7%)
  between operations  17.6 us (6%)
  local copies, waits for them, and re-layouts  15.6 us (5%)
    all_gather x1, waiting for transfers between devices, body(): lax.all_gather(low.reshape(tokens.shape), 'ctx', axis=1, tiled=True)  44.8 us
    reduce_scatter x1, waiting for transfers between devices, body(): lax.psum_scatter(terms.reshape(seqs, length, width), 'ctx', scatter_dimen...  44.3 us
    pallas_call x1, Pallas kernels, body(): kernel_call(functools.partial(backward_kernel, first_len, heads, size, sc...  32.6 us
    pallas_call x1, Pallas kernels, body(): kernel_call(functools.partial(forward_kernel, first_len, heads, size, sca...  23 us
    ppermute x6, waiting for transfers between devices, gather_dp(): other = lax.ppermute(block, 'dp', pairs)  22.3 us
    all_to_all x1, blocking collectives, body(): sums = lax.all_to_all(sums, both, 0, 0, tiled=True)  20.1 us
    all_to_all x1, waiting for transfers between devices, body(): lax.all_to_all(cols, 'ctx', 0, 0, tiled=True)  10.7 us
    ppermute x6, waiting for transfers between devices, exchange_dp(): total = total + lax.ppermute(terms[k], 'dp', pairs).astype(F32)  10.2 us
  transfers between devices with their start and end apart: 23, of which 12 were waited for; matrix products, arithmetic and copies ran while one was open for 11% of the time, Pallas kernels for 1%

profile of v3, /device:TPU:0, one launch (start us, length us, event | category | flops | bytes accessed | tf_op | source)
XLA Modules:
  0.0 301.9 jit_solution(11422698600495963288)
XLA Ops:
  7.2 0.7 all-gather.3.cloned.1.call-update
  7.9 2.0 pack_columns.1
  9.9 1.0 pad_maximum_fusion
  10.9 3.0 collective-permute-start.3
  13.9 1.5 collective-permute-start.4
  15.5 5.3 %all-to-all-start = ((bf16[8,32,1024]{2,1,0:T(8,128)(2,1)}), bf16[8,32,1024]{2,1,0:T(8,128)(2,1)S(1)}, u32[]{:S(2)}, u32[]{:S(2)}) async-start(bf16[8,32,1024]{2,1,0:T(8,128)(2,1)} %pack_columns.1), calls=%async_computation | async-start | bytes 1048576 | tf_op jit(solution)/shard_map/all_to_all | solution.py:498
  21.4 1.1 collective-permute-done.3
  22.6 1.0 bitcast_dynamic-update-slice_fusion.6
  23.6 6.7 %collective-permute-done.4 = bf16[160,1024]{1,0:T(8,128)(2,1)} collective-permute-done((bf16[160,1024]{1,0:T(8,128)(2,1)S(1)}, bf16[160,1024]{1,0:T(8,128)(2,1)}, u32[]{:S(2)}, u32[]{:S(2)}) %collective-permute-start.4) | collective-permute-done | bytes 327712 | tf_op jit(solution)/shard_map/ppermute | solution.py:408
  30.2 1.0 bitcast_dynamic-update-slice_fusion.5
  32.0 5.2 %compare_select_fusion.9 = (f32[128]{0:T(128)S(1)}, f32[128]{0:T(128)S(1)}) fusion(f32[]{:T(128)} %bitcast.17, f32[]{:T(128)} %bitcast.16, f32[]{:T(128)} %bitcast.15, f32[]{:T(128)} %bitcast.14, f32[]{:T(128)} %bitcast.13, f32[]{:T(128)} %bitcast.12, f32[]{:T(128)} %bitcast.11, f32[]{:T(128)} %bitcast.10), kind=kLoop, calls=%fused_computation.68 | loop fusion | flops 5632 | bytes 1056 | tf_op jit(solution)/shard_map/jit(_where)/select_n | solution.py:534
  37.2 1.0 slice.99
  38.3 0.7 copy.46
  39.0 10.7 %all-to-all-done = bf16[8,32,1024]{2,1,0:T(8,128)(2,1)S(1)} async-done(((bf16[8,32,1024]{2,1,0:T(8,128)(2,1)}), bf16[8,32,1024]{2,1,0:T(8,128)(2,1)S(1)}, u32[]{:S(2)}, u32[]{:S(2)}) %all-to-all-start) | async-done | bytes 524320 | tf_op jit(solution)/shard_map/all_to_all | solution.py:498
  49.8 1.5 collective-permute-start
  51.2 1.5 collective-permute-start.1
  53.3 2.2 convert_reduce_fusion
  55.5 5.8 %fusion = (f32[2048,128]{1,0:T(8,128)}, f32[2048,128]{1,0:T(8,128)}) fusion(f32[128]{0:T(128)S(1)} %get-tuple-element.112, f32[128]{0:T(128)S(1)} %get-tuple-element.113, f32[2048]{0:T(1024)S(1)} %bitcast.146), kind=kLoop, calls=%fused_computation.4 | loop fusion | flops 524288 | bytes 2106368 | tf_op jit(solution)/shard_map/mul | solution.py:534
  61.6 3.0 collective-permute-done
  64.6 11.6 %collective-permute-done.1 = bf16[256,1024]{1,0:T(8,128)(2,1)S(1)} collective-permute-done((bf16[256,1024]{1,0:T(8,128)(2,1)S(1)}, bf16[256,1024]{1,0:T(8,128)(2,1)S(1)}, u32[]{:S(2)}, u32[]{:S(2)}) %collective-permute-start.1) | collective-permute-done | bytes 524320 | tf_op jit(solution)/shard_map/ppermute | solution.py:408
  76.7 0.8 reshape.250.bqkv
  77.6 0.7 reshape_squeeze.15.gain
  78.3 0.7 reshape_squeeze.16.shift
  79.6 23.0 %forward_kernel.1 = (bf16[2048,1024]{1,0:T(8,128)(2,1)}, bf16[2048,128]{1,0:T(8,128)(2,1)}, bf16[2048,128]{1,0:T(8,128)(2,1)}, bf16[2048,128]{1,0:T(8,128)(2,1)}...) custom-call(f32[1,1024]{1,0:T(1,128)} %reshape_squeeze.15.gain, ...), custom_call_target="tpu_custom_call" | custom-call | flops 10000000000 | bytes 20000000 | tf_op jit(solution)/shard_map/forward_kernel/pallas_call | solution.py:559
  103.3 0.8 copy.47.valid
  104.1 0.7 add.158.bias
  106.8 44.3 %reduce-scatter.3.cloned.1.call-done = bf16[2,128,1024]{2,1,0:T(8,128)(2,1)} async-done(((bf16[2,1024,1024]{2,1,0:T(8,128)(2,1)}), bf16[2,128,1024]{2,1,0:T(8,128)(2,1)}) %reduce-scatter.3.cloned.1.call-update) | async-done | bytes 524304 | tf_op jit(solution)/shard_map/reduce_scatter | solution.py:576
  151.1 3.2 %loss_kernel.1 = (bf16[256,1024]{1,0:T(8,128)(2,1)}, f32[256,1024]{1,0:T(8,128)}, bf16[256,1024]{1,0:T(8,128)(2,1)}, f32[1,1024]{1,0:T(1,128)}, f32[1,1]{1,0:T(1,128)}) custom-call(bf16[256,1024]{1,0:T(8,128)(2,1)} %bitcast.137, bf16[256,1024]{1,0:T(8,128)(2,1)} %bitcast.115, bf16[256,1024]{1,0:T(8,128)(2,1)} %bitcast.136, f32[256,1]{1,0:T(8,128)} %copy.47.valid, ...), custom_call_target="tpu_custom_call" | custom-call | flops 1000000 | bytes 3000000 | tf_op jit(solution)/shard_map/loss_kernel/pallas_call | solution.py:584
  154.9 44.8 %all-gather.5.cloned.1.call-done = bf16[2,1024,1024]{2,1,0:T(8,128)(2,1)} async-done(((bf16[2,128,1024]{2,1,0:T(8,128)(2,1)}), bf16[2,1024,1024]{2,1,0:T(8,128)(2,1)}) %all-gather.5.cloned.1.call-update) | async-done | bytes 4194320 | tf_op jit(solution)/shard_map/all_gather | solution.py:594
  199.8 32.6 %backward_kernel.1 = (bf16[2048,1024]{1,0:T(8,128)(2,1)}, f32[1,1024]{1,0:T(1,128)}, f32[1,1024]{1,0:T(1,128)}, f32[1,512]{1,0:T(1,128)}, f32[1,384]{1,0:T(1,128...) custom-call(s32[4]{0:T(128)} %pad_add_fusion.order, ...), custom_call_target="tpu_custom_call" | custom-call | flops 12000000000 | bytes 20000000 | tf_op jit(solution)/shard_map/backward_kernel/pallas_call | solution.py:606
  235.8 1.5 collective-permute-start.7
  237.3 1.5 collective-permute-start.8
  240.2 20.1 %all_to_all.22 = f32[32,1,384]{2,1,0:T(1,128)S(1)} all-to-all(f32[32,1,384]{2,1,0:T(1,128)S(1)} %copy.50), channel_id=1, replica_groups=mesh['dp'=4,'ctx'=8] {'dp','ctx'}, dimensions={0} | all-to-all | bytes 98304 | tf_op jit(solution)/shard_map/all_to_all | solution.py:655
  260.4 1.2 collective-permute-start.11
  261.7 1.0 add_convert_fusion
  262.7 3.5 %all-to-all-start.2 = ((bf16[8,32,896]{2,1,0:T(8,128)(2,1)}), bf16[8,32,896]{2,1,0:T(8,128)(2,1)S(1)}, u32[]{:S(2)}, u32[]{:S(2)}) async-start(bf16[8,32,896]{2,1,0:T(8,128)(2,1)} %bitcast.54), calls=%async_computation.4 | async-start | bytes 917504 | tf_op jit(solution)/shard_map/all_to_all | solution.py:657
  266.2 0.9 collective-permute-start.12
  267.1 1.4 collective-permute-start.13
  268.5 1.2 collective-permute-start.14
  269.7 0.9 collective-permute-start.15
  270.6 1.4 collective-permute-start.16
  272.6 0.7 fusion.2
  273.3 5.0 %collective-permute-done.14 = bf16[128,1024]{1,0:T(8,128)(2,1)S(1)} collective-permute-done((bf16[128,1024]{1,0:T(8,128)(2,1)}, bf16[128,1024]{1,0:T(8,128)(2,1)S(1)}, u32[]{:S(2)}, u32[]{:S(2)}) %collective-permute-start.14) | collective-permute-done | bytes 262176 | tf_op jit(solution)/shard_map/ppermute | solution.py:417
  278.9 4.6 %collective-permute-done.16 = bf16[128,1024]{1,0:T(8,128)(2,1)S(1)} collective-permute-done((bf16[128,1024]{1,0:T(8,128)(2,1)}, bf16[128,1024]{1,0:T(8,128)(2,1)S(1)}, u32[]{:S(2)}, u32[]{:S(2)}) %collective-permute-start.16) | collective-permute-done | bytes 262176 | tf_op jit(solution)/shard_map/ppermute | solution.py:417
  283.5 0.9 convert_add_fusion
  287.8 0.8 copy-done.1
  288.5 2.0 unpack_columns.1
  290.5 3.0 %norm_back_kernel.1 = bf16[256,1024]{1,0:T(8,128)(2,1)} custom-call(bf16[256,1024]{1,0:T(8,128)(2,1)} %bitcast.130, bf16[256,1024]{1,0:T(8,128)(2,1)} %bitcast.116, f32[256,1024]{1,0:T(8,128)} %get-tuple-element.77.og, f32[1,1024]{1,0:T(1,128)} %reshape_squeeze.15.gain), custom_call_target="tpu_custom_call" | custom-call | flops 1000000 | bytes 3000000 | tf_op jit(solution)/shard_map/norm_back_kernel/pallas_call | solution.py:683
  (110 shorter events, 14.6 us)
Async XLA Ops:
  7.2 72.4 %all-gather.3.cloned.1.call-start = ((), (), s32[]{:S(2)}) async-start(), calls=%async_computation.5 | async-start | bytes 4718592 | tf_op jit(solution)/shard_map/all_gather | solution.py:497
  10.9 11.6 %collective-permute-start.3 = (bf16[160,1024]{1,0:T(8,128)(2,1)S(1)}, bf16[160,1024]{1,0:T(8,128)(2,1)}, u32[]{:S(2)}, u32[]{:S(2)}) collective-permute-start(bf16[160,1024]{1,0:T(8,128)(2,1)S(1)} %pad_maximum_fusion), channel_id=1, source_target_pairs={{0,8},{8,0},{16,24},{24,16},{1,9},{9,1},{17,25},{25,17},{2,10},{10... | collective-permute-start | bytes 983048 | tf_op jit(solution)/shard_map/ppermute | solution.py:408
  13.9 16.3 %collective-permute-start.4 = (bf16[160,1024]{1,0:T(8,128)(2,1)S(1)}, bf16[160,1024]{1,0:T(8,128)(2,1)}, u32[]{:S(2)}, u32[]{:S(2)}) collective-permute-start(bf16[160,1024]{1,0:T(8,128)(2,1)S(1)} %pad_maximum_fusion), channel_id=1, source_target_pairs={{0,16},{8,24},{16,0},{24,8},{1,17},{9,25},{17,1},{25,9},{2,18},{10... | collective-permute-start | bytes 983048 | tf_op jit(solution)/shard_map/ppermute | solution.py:408
  15.4 15.8 %collective-permute-start.5 = (bf16[160,1024]{1,0:T(8,128)(2,1)S(1)}, bf16[160,1024]{1,0:T(8,128)(2,1)S(1)}, u32[]{:S(2)}, u32[]{:S(2)}) collective-permute-start(bf16[160,1024]{1,0:T(8,128)(2,1)S(1)} %pad_maximum_fusion), channel_id=1, source_target_pairs={{0,24},{8,16},{16,8},{24,0},{1,25},{9,17},{17,9},{25,1},{2,26},{10... | collective-permute-start | bytes 983048 | tf_op jit(solution)/shard_map/ppermute | solution.py:408
  15.5 34.3 %all-to-all-start = ((bf16[8,32,1024]{2,1,0:T(8,128)(2,1)}), bf16[8,32,1024]{2,1,0:T(8,128)(2,1)S(1)}, u32[]{:S(2)}, u32[]{:S(2)}) async-start(bf16[8,32,1024]{2,1,0:T(8,128)(2,1)} %pack_columns.1), calls=%async_computation | async-start | bytes 1048576 | tf_op jit(solution)/shard_map/all_to_all | solution.py:498
  20.8 130.3 %reduce-scatter.3.cloned.1.call-start = ((), (), s32[]{:S(2)}) async-start(), calls=%async_computation.6 | async-start | bytes 4718592 | tf_op jit(solution)/shard_map/reduce_scatter | solution.py:576
  31.3 22.0 %copy-start.5 = (s32[2,1024]{1,0:T(2,128)S(1)}, s32[2,1024]{1,0:T(2,128)}, u32[]{:S(2)}) copy-start(s32[2,1024]{1,0:T(2,128)} %seg_row.1) | copy-start | bytes 24580
  31.3 6.9 %collective-permute-start.6 = (bf16[2,32,1024]{2,1,0:T(8,128)(2,1)S(1)}, bf16[2,32,1024]{2,1,0:T(8,128)(2,1)S(1)}, u32[]{:S(2)}, u32[]{:S(2)}) collective-permute-start(bf16[2,32,1024]{2,1,0:T(8,128)(2,1)S(1)} %dynamic-slice_bitcast_fusion.1), channel_id=1, source_target_pairs={{0,1},{1,0},{2,3},{3,2},{4,5},{5,4},{6,7},{7,6},{8,9},{9,8},{10,11... | collective-permute-start | bytes 393224 | tf_op jit(solution)/shard_map/ppermute | solution.py:541
  49.8 14.8 %collective-permute-start = (bf16[256,1024]{1,0:T(8,128)(2,1)S(1)}, bf16[256,1024]{1,0:T(8,128)(2,1)S(1)}, u32[]{:S(2)}, u32[]{:S(2)}) collective-permute-start(bf16[256,1024]{1,0:T(8,128)(2,1)S(1)} %bitcast.122), channel_id=1, source_target_pairs={{0,8},{8,0},{16,24},{24,16},{1,9},{9,1},{17,25},{25,17},{2,10},{10... | collective-permute-start | bytes 1572872 | tf_op jit(solution)/shard_map/ppermute | solution.py:408
  51.2 24.9 %collective-permute-start.1 = (bf16[256,1024]{1,0:T(8,128)(2,1)S(1)}, bf16[256,1024]{1,0:T(8,128)(2,1)S(1)}, u32[]{:S(2)}, u32[]{:S(2)}) collective-permute-start(bf16[256,1024]{1,0:T(8,128)(2,1)S(1)} %bitcast.123), channel_id=1, source_target_pairs={{0,16},{8,24},{16,0},{24,8},{1,17},{9,25},{17,1},{25,9},{2,18},{10... | collective-permute-start | bytes 1572872 | tf_op jit(solution)/shard_map/ppermute | solution.py:408
  52.7 23.5 %collective-permute-start.2 = (bf16[256,1024]{1,0:T(8,128)(2,1)S(1)}, bf16[256,1024]{1,0:T(8,128)(2,1)S(1)}, u32[]{:S(2)}, u32[]{:S(2)}) collective-permute-start(bf16[256,1024]{1,0:T(8,128)(2,1)S(1)} %bitcast.124), channel_id=1, source_target_pairs={{0,24},{8,16},{16,8},{24,0},{1,25},{9,17},{17,9},{25,1},{2,26},{10... | collective-permute-start | bytes 1572872 | tf_op jit(solution)/shard_map/ppermute | solution.py:408
  76.3 3.3 %copy-start = (bf16[4,256,1024]{2,1,0:T(8,128)(2,1)}, bf16[4,256,1024]{2,1,0:T(8,128)(2,1)S(1)}, u32[]{:S(2)}) copy-start(bf16[4,256,1024]{2,1,0:T(8,128)(2,1)S(1)} %bitcast_dynamic-update-slice_fusion) | copy-start | bytes 6291460
  102.6 0.7 copy-start.9
  102.7 97.1 %all-gather.5.cloned.1.call-start = ((), (), s32[]{:S(2)}) async-start(), calls=%async_computation.7 | async-start | bytes 4718592 | tf_op jit(solution)/shard_map/all_gather | solution.py:594
  154.3 136.3 %reduce-scatter.5.cloned.1.call-start = ((), (), s32[]{:S(2)}) async-start(), calls=%async_computation.8 | async-start | bytes 4718592 | tf_op jit(solution)/shard_map/reduce_scatter | solution.py:628
  232.3 0.7 copy-start.6
  232.4 1.4 copy-start.11
  232.4 1.6 copy-start.4
  232.4 2.0 copy-start.8
  232.4 2.7 copy-start.7
  232.4 6.9 %copy-start.10 = (f32[1,512]{1,0:T(1,128)S(1)}, f32[1,512]{1,0:T(1,128)}, u32[]{:S(2)}) copy-start(f32[1,512]{1,0:T(1,128)} %get-tuple-element.73) | copy-start | bytes 6148
  232.4 29.3 %copy-start.2 = (f32[256,896]{1,0:T(8,128)S(1)}, f32[256,896]{1,0:T(8,128)}, u32[]{:S(2)}) copy-start(f32[256,896]{1,0:T(8,128)} %get-tuple-element.65) | copy-start | bytes 2752516
  234.0 26.3 %collective-permute-start.10 = (bf16[2,32,1024]{2,1,0:T(8,128)(2,1)S(1)}, bf16[2,32,1024]{2,1,0:T(8,128)(2,1)S(1)}, u32[]{:S(2)}, u32[]{:S(2)}) collective-permute-start(bf16[2,32,1024]{2,1,0:T(8,128)(2,1)S(1)} %dynamic-slice_bitcast_fusion), channel_id=1, source_target_pairs={{0,1},{1,0},{2,3},{3,2},{4,5},{5,4},{6,7},{7,6},{8,9},{9,8},{10,11... | collective-permute-start | bytes 393224 | tf_op jit(solution)/shard_map/ppermute | solution.py:672
  235.8 25.8 %collective-permute-start.7 = (bf16[256,896]{1,0:T(8,128)(2,1)}, bf16[256,896]{1,0:T(8,128)(2,1)S(1)}, u32[]{:S(2)}, u32[]{:S(2)}) collective-permute-start(bf16[256,896]{1,0:T(8,128)(2,1)} %get-tuple-element.66), channel_id=1, source_target_pairs={{0,8},{8,0},{16,24},{24,16},{1,9},{9,1},{17,25},{25,17},{2,10},{10... | collective-permute-start | bytes 1376264 | tf_op jit(solution)/shard_map/ppermute | solution.py:417
  237.3 24.4 %collective-permute-start.8 = (bf16[256,896]{1,0:T(8,128)(2,1)}, bf16[256,896]{1,0:T(8,128)(2,1)S(1)}, u32[]{:S(2)}, u32[]{:S(2)}) collective-permute-start(bf16[256,896]{1,0:T(8,128)(2,1)} %get-tuple-element.67), channel_id=1, source_target_pairs={{0,16},{8,24},{16,0},{24,8},{1,17},{9,25},{17,1},{25,9},{2,18},{10... | collective-permute-start | bytes 1376264 | tf_op jit(solution)/shard_map/ppermute | solution.py:417
  238.8 22.9 %collective-permute-start.9 = (bf16[256,896]{1,0:T(8,128)(2,1)}, bf16[256,896]{1,0:T(8,128)(2,1)S(1)}, u32[]{:S(2)}, u32[]{:S(2)}) collective-permute-start(bf16[256,896]{1,0:T(8,128)(2,1)} %get-tuple-element.68), channel_id=1, source_target_pairs={{0,24},{8,16},{16,8},{24,0},{1,25},{9,17},{17,9},{25,1},{2,26},{10... | collective-permute-start | bytes 1376264 | tf_op jit(solution)/shard_map/ppermute | solution.py:417
  260.4 10.2 %collective-permute-start.11 = (bf16[32,1024]{1,0:T(8,128)(2,1)S(1)}, bf16[32,1024]{1,0:T(8,128)(2,1)S(1)}, u32[]{:S(2)}, u32[]{:S(2)}) collective-permute-start(bf16[32,1024]{1,0:T(8,128)(2,1)S(1)} %get-tuple-element.95), channel_id=1, source_target_pairs={{0,8},{8,0},{16,24},{24,16},{1,9},{9,1},{17,25},{25,17},{2,10},{10... | collective-permute-start | bytes 196616 | tf_op jit(solution)/shard_map/ppermute | solution.py:434
  261.7 21.8 %copy-start.3 = (f32[128,1024]{1,0:T(8,128)S(1)}, f32[128,1024]{1,0:T(8,128)}, u32[]{:S(2)}) copy-start(f32[128,1024]{1,0:T(8,128)} %get-tuple-element.82) | copy-start | bytes 1572868
  262.7 25.1 %all-to-all-start.2 = ((bf16[8,32,896]{2,1,0:T(8,128)(2,1)}), bf16[8,32,896]{2,1,0:T(8,128)(2,1)S(1)}, u32[]{:S(2)}, u32[]{:S(2)}) async-start(bf16[8,32,896]{2,1,0:T(8,128)(2,1)} %bitcast.54), calls=%async_computation.4 | async-start | bytes 917504 | tf_op jit(solution)/shard_map/all_to_all | solution.py:657
  266.2 5.9 %collective-permute-start.12 = (bf16[32,1024]{1,0:T(8,128)(2,1)S(1)}, bf16[32,1024]{1,0:T(8,128)(2,1)S(1)}, u32[]{:S(2)}, u32[]{:S(2)}) collective-permute-start(bf16[32,1024]{1,0:T(8,128)(2,1)S(1)} %get-tuple-element.96), channel_id=1, source_target_pairs={{0,16},{8,24},{16,0},{24,8},{1,17},{9,25},{17,1},{25,9},{2,18},{10... | collective-permute-start | bytes 196616 | tf_op jit(solution)/shard_map/ppermute | solution.py:434
  267.1 5.5 %collective-permute-start.13 = (bf16[32,1024]{1,0:T(8,128)(2,1)S(1)}, bf16[32,1024]{1,0:T(8,128)(2,1)S(1)}, u32[]{:S(2)}, u32[]{:S(2)}) collective-permute-start(bf16[32,1024]{1,0:T(8,128)(2,1)S(1)} %get-tuple-element.97), channel_id=1, source_target_pairs={{0,24},{8,16},{16,8},{24,0},{1,25},{9,17},{17,9},{25,1},{2,26},{10... | collective-permute-start | bytes 196616 | tf_op jit(solution)/shard_map/ppermute | solution.py:434
  268.5 9.7 %collective-permute-start.14 = (bf16[128,1024]{1,0:T(8,128)(2,1)}, bf16[128,1024]{1,0:T(8,128)(2,1)S(1)}, u32[]{:S(2)}, u32[]{:S(2)}) collective-permute-start(bf16[128,1024]{1,0:T(8,128)(2,1)} %get-tuple-element.83), channel_id=1, source_target_pairs={{0,8},{8,0},{16,24},{24,16},{1,9},{9,1},{17,25},{25,17},{2,10},{10... | collective-permute-start | bytes 786440 | tf_op jit(solution)/shard_map/ppermute | solution.py:417
  269.7 9.2 %collective-permute-start.15 = (bf16[128,1024]{1,0:T(8,128)(2,1)}, bf16[128,1024]{1,0:T(8,128)(2,1)S(1)}, u32[]{:S(2)}, u32[]{:S(2)}) collective-permute-start(bf16[128,1024]{1,0:T(8,128)(2,1)} %get-tuple-element.84), channel_id=1, source_target_pairs={{0,16},{8,24},{16,0},{24,8},{1,17},{9,25},{17,1},{25,9},{2,18},{10... | collective-permute-start | bytes 786440 | tf_op jit(solution)/shard_map/ppermute | solution.py:417
  270.6 12.9 %collective-permute-start.16 = (bf16[128,1024]{1,0:T(8,128)(2,1)}, bf16[128,1024]{1,0:T(8,128)(2,1)S(1)}, u32[]{:S(2)}, u32[]{:S(2)}) collective-permute-start(bf16[128,1024]{1,0:T(8,128)(2,1)} %get-tuple-element.85), channel_id=1, source_target_pairs={{0,24},{8,16},{16,8},{24,0},{1,25},{9,17},{17,9},{25,1},{2,26},{10... | collective-permute-start | bytes 786440 | tf_op jit(solution)/shard_map/ppermute | solution.py:417
  286.7 7.4 %copy-start.12 = (f32[32]{0:T(128)}, f32[32]{0:T(128)S(1)}, u32[]{:S(2)}) copy-start(f32[32]{0:T(128)S(1)} %get-tuple-element.141) | copy-start | bytes 388
  287.8 0.8 copy-start.1
Sparse Core Ops, SparseCore 0:
  9.6 60.9 all-gather.2
  102.8 48.2 reduce-scatter.2
  154.4 45.3 all-gather.4
  232.6 56.8 reduce-scatter.4

commit v4 on v3

--- a/solution.py
+++ b/solution.py
@@ -17,6 +17,7 @@
 PARAMS = pltpu.CompilerParams(vmem_limit_bytes=56 * 1024 * 1024)
 COPIES = 128
 STEP = 512
+TOGETHER = 2
 LAST = ((1,), (1,))
 FIRST = ((0,), (0,))
 
@@ -56,17 +57,32 @@
     return values * cosine + partner * sine
 
 
-def span_mask(start, low, first_len, seg_row, heads):
-    stop = start + BLK
-    shape = (heads * BLK, stop - low)
-    row = lax.rem(lax.broadcasted_iota(jnp.int32, shape, 0), BLK) + start
-    col = lax.broadcasted_iota(jnp.int32, shape, 1) + low
-    allowed = col <= row
-    if low >= first_len:
-        turned = jnp.transpose(jnp.broadcast_to(seg_row[:, start:stop], (BLK, BLK)))[:, :1]
-        turned = jnp.concatenate([turned] * heads, axis=0)
-        allowed = allowed & (turned == seg_row[:, low:stop])
-    return allowed
+def mask_scores(scores, start, low, first_len, seg_row, heads):
+    shape = (heads * BLK, BLK)
+    row = lax.rem(lax.broadcasted_iota(jnp.int32, shape, 0), BLK)
+    causal = lax.broadcasted_iota(jnp.int32, shape, 1) <= row
+    if low < first_len:
+        last = jnp.where(causal, scores[:, start - low :], NEG_FILL)
+        return last if start == low else jnp.concatenate([scores[:, : start - low], last], axis=1)
+    own = jnp.transpose(jnp.broadcast_to(seg_row[:, start : start + BLK], (BLK, BLK)))
+    own = jnp.concatenate([own] * heads, axis=0)
+    parts = []
+    for at in range(low, start + BLK, BLK):
+        allowed = own == seg_row[:, at : at + BLK]
+        if at == start:
+            allowed = allowed & causal
+        parts.append(jnp.where(allowed, scores[:, at - low : at - low + BLK], NEG_FILL))
+    return jnp.concatenate(parts, axis=1)
+
+
+def in_step(chains):
+    chains = list(chains)
+    while chains:
+        chains = [chain for chain in chains if next(chain, "over") != "over"]
+
+
+def grouped(items, count):
+    return [items[at : at + count] for at in range(0, len(items), count)]
 
 
 def standardize(rows):
@@ -126,8 +142,8 @@
         t_copies[at] = copier.rows(tables, at, step)
     w_copies += [copier.start(wdown_in, wdown), copier.start(wproj_in, wproj)]
     out = []
-    for seq in range(total // length):
-        origin = seq * length
+    seqs = total // length
+    for origin in range(0, total, length):
         for at in range(origin, origin + length, step):
             rows = slice(at, at + step)
             wait_all(x_copies[at])
@@ -153,46 +169,54 @@
                 cdf + up * jnp.exp(-0.5 * up * up) * (1.0 / math.sqrt(2.0 * math.pi))
             ).astype(BF16)
             out += copier.rows(((act, act_out), (slope, slope_out)), at, step)
-        for start, low in block_spans(length, first_len):
-            rows, cols = slice(origin + start, origin + start + BLK), slice(
-                origin + low, origin + start + BLK
-            )
-            query = head_stack(q[rows, :], heads, size)
-            allowed = span_mask(start, low, first_len, seg_row[seq : seq + 1, :], heads)
-            scores = jnp.where(allowed, mm(query, k[cols, :], LAST), NEG_FILL)
-            peak = jnp.max(scores, axis=1, keepdims=True)
-            grown = jnp.exp(scores - peak)
-            summed = jnp.sum(grown, axis=1, keepdims=True)
-            probs = (grown * (1.0 / summed)).astype(BF16)
-            result = mm(probs, v[cols, :])
-            mixed[rows, :] = head_pick(result, heads, size).astype(BF16)
-            stat[rows, :] = head_pick(
-                jnp.broadcast_to(peak + jnp.log(summed), result.shape), heads, size
-            )
-        out += copier.rows(((mixed, mixed_out), (stat, stat_out)), origin, length)
-        if seq == 0:
-            wait_all(w_copies[split:])
-        for at in range(origin, origin + length, step):
-            rows = slice(at, at + step)
-            terms[rows, :] = (mm(act[rows, :], wdown[...]) + mm(mixed[rows, :], wproj[...])).astype(
-                BF16
-            )
-            out += copier.rows([(terms, terms_out)], at, step)
+
+    def attend(seq, start, low):
+        origin = seq * length
+        rows = slice(origin + start, origin + start + BLK)
+        cols = slice(origin + low, origin + start + BLK)
+        query = head_stack(q[rows, :], heads, size)
+        yield
+        scores = mm(query, k[cols, :], LAST)
+        yield
+        scores = mask_scores(scores, start, low, first_len, seg_row[seq : seq + 1, :], heads)
+        peak = jnp.max(scores, axis=1, keepdims=True)
+        yield
+        grown = jnp.exp(scores - peak)
+        summed = jnp.sum(grown, axis=1, keepdims=True)
+        yield
+        probs = (grown * (1.0 / summed)).astype(BF16)
+        yield
+        result = mm(probs, v[cols, :])
+        yield
+        mixed[rows, :] = head_pick(result, heads, size).astype(BF16)
+        stat[rows, :] = head_pick(
+            jnp.broadcast_to(peak + jnp.log(summed), result.shape), heads, size
+        )
+
+    for spans in grouped(block_spans(length, first_len), TOGETHER):
+        in_step(attend(seq, start, low) for start, low in spans for seq in range(seqs))
+    out += copier.rows(((mixed, mixed_out), (stat, stat_out)), 0, total)
+    wait_all(w_copies[split:])
+    for at in range(0, total, step):
+        rows = slice(at, at + step)
+        terms[rows, :] = (mm(act[rows, :], wdown[...]) + mm(mixed[rows, :], wproj[...])).astype(
+            BF16
+        )
+        out += copier.rows([(terms, terms_out)], at, step)
     wait_all(out)
 
 
 def backward_kernel(
     first_len, heads, size, scale, length, step, cut,
     order, seg_row, g_in, slope_in, q_in, k_in, v_in, stat_in, cos_in, sin_in, x_in, n_in,
-    act_in, mixed_in, wdown_in, wproj_in, *refs,
+    wdown_in, wproj_in, *refs,
 ):
-    (g, slope, q, k, v, stat, cosine, sine, x, normed, act, mixed, wdown, wproj,
-     mg, ug, qg, dk, dv, sems) = refs[-20:]
+    (g, slope, q, k, v, stat, cosine, sine, x, normed, wdown, wproj,
+     mg, ug, qg, dk, dv, sems) = refs[-18:]
     split = 1 if refs[0].shape[1] > 3 * heads * size else 2
-    w_in, refs = refs[:split], refs[split:-20]
-    back_out, gain_sum, shift_sum, up_sum, qkv_sum, pw = refs[:6]
-    outs, w = refs[6 : len(refs) - split], refs[len(refs) - split :]
-    col_out, down_out = outs[: len(outs) // 2], outs[len(outs) // 2 :]
+    w_in, refs = refs[:split], refs[split:-18]
+    back_out, gain_sum, shift_sum, up_sum, qkv_sum = refs[:5]
+    col_out, w = refs[5 : len(refs) - split], refs[len(refs) - split :]
     for ref in (gain_sum, shift_sum, up_sum, qkv_sum):
         ref[...] = jnp.zeros_like(ref)
     copier = Copier(sems)
@@ -217,7 +241,7 @@
             if origin == 0:
                 w_copies += [copier.start(a, b) for a, b in zip(w_in, w)]
             x_copies[origin] = copier.rows([(x_in, x)], origin, length)
-    late = [copier.start(a, b) for a, b in ((act_in, act), (mixed_in, mixed), (n_in, normed))]
+    late = [copier.start(n_in, normed)]
     out = []
     for seq in range(total // length):
         origin = seq * length
@@ -231,60 +255,84 @@
             ug[rows, :] = up_grad
             up_sum[...] += jnp.sum(up_grad.astype(F32), axis=0, keepdims=True)
             mg[rows, :] = mm(grad, wproj[...], LAST).astype(BF16)
-        dk[...] = jnp.zeros_like(dk)
-        dv[...] = jnp.zeros_like(dv)
+    dk[...] = jnp.zeros_like(dk)
+    dv[...] = jnp.zeros_like(dv)
+    for origin in s_copies:
         wait_all(s_copies[origin])
-        for start, low in block_spans(length, first_len):
-            stop = start + BLK
-            rows, cols = slice(origin + start, origin + stop), slice(origin + low, origin + stop)
-            query = head_stack(q[rows, :], heads, size)
-            grad = head_stack(mg[rows, :], heads, size)
-            key, value = k[cols, :], v[cols, :]
-            allowed = span_mask(start, low, first_len, seg_row[seq : seq + 1, :], heads)
-            peak = stat[rows, :]
-            peak = jnp.concatenate(
-                [peak[:, h * size : h * size + 1] for h in range(heads)], axis=0
-            )
-            scores = jnp.where(allowed, mm(query, key, LAST), NEG_FILL)
-            probs = jnp.exp(scores - peak)
-            prob_grad = mm(grad, value, LAST)
-            delta = jnp.sum(probs * prob_grad, axis=1, keepdims=True)
-            score_grad = (probs * (prob_grad - delta)).astype(BF16)
-            dq = head_pick(mm(score_grad, key), heads, size) * scale
-            qg[rows, :width] = turn(dq, cosine[rows, :], -sine[rows, :], size).astype(BF16)
-            dk[low:stop, :] += mm(score_grad, query, FIRST)
-            dv[low:stop, :] += mm(probs.astype(BF16), grad, FIRST)
-        rows = slice(origin, origin + length)
+
+    def attend(seq, start, low):
+        origin = seq * length
+        stop = start + BLK
+        rows, cols = slice(origin + start, origin + stop), slice(origin + low, origin + stop)
+        query = head_stack(q[rows, :], heads, size)
+        grad = head_stack(mg[rows, :], heads, size)
+        key, value = k[cols, :], v[cols, :]
+        yield
+        scores = mm(query, key, LAST)
+        yield
+        prob_grad = mm(grad, value, LAST)
+        yield
+        peak = stat[rows, :]
+        peak = jnp.concatenate([peak[:, h * size : h * size + 1] for h in range(heads)], axis=0)
+        scores = mask_scores(scores, start, low, first_len, seg_row[seq : seq + 1, :], heads)
+        probs = jnp.exp(scores - peak)
+        yield
+        delta = jnp.sum(probs * prob_grad, axis=1, keepdims=True)
+        yield
+        score_grad = (probs * (prob_grad - delta)).astype(BF16)
+        yield
+        dq = mm(score_grad, key)
+        yield
+        dk[cols, :] += mm(score_grad, query, FIRST)
+        yield
+        dv[cols, :] += mm(probs.astype(BF16), grad, FIRST)
+        yield
+        dq = head_pick(dq, heads, size) * scale
+        qg[rows, :width] = turn(dq, cosine[rows, :], -sine[rows, :], size).astype(BF16)
+
+    for spans in grouped(block_spans(length, first_len), 1):
+        in_step(
+            attend(seq, start, low) for start, low in spans for seq in range(total // length)
+        )
+    for at in range(0, total, step):
+        rows = slice(at, at + step)
         qg[rows, width : 2 * width] = turn(
-            dk[...], cosine[rows, :], -sine[rows, :], size
+            dk[rows, :], cosine[rows, :], -sine[rows, :], size
         ).astype(BF16)
-        qg[rows, 2 * width :] = dv[...].astype(BF16)
+        qg[rows, 2 * width :] = dv[rows, :].astype(BF16)
+    for origin in x_copies:
         wait_all(x_copies[origin])
-        if seq == 0:
-            wait_all(w_copies[2:])
-        for at in range(origin, origin + length, step):
-            rows = slice(at, at + step)
-            terms = mm(ug[rows, :], wup[...], LAST) + mm(qg[rows, :], wqkv[...], LAST)
-            standard, _ = standardize(x[rows, :].astype(F32))
-            x[rows, :] = terms.astype(BF16)
-            out += copier.rows([(x, back_out)], at, step)
-            gain_sum[...] += jnp.sum(terms * standard, axis=0, keepdims=True)
-            shift_sum[...] += jnp.sum(terms, axis=0, keepdims=True)
-            qkv_sum[...] += jnp.sum(qg[rows, :].astype(F32), axis=0, keepdims=True)
+    wait_all(w_copies[2:])
+    for at in range(0, total, step):
+        rows = slice(at, at + step)
+        terms = mm(ug[rows, :], wup[...], LAST) + mm(qg[rows, :], wqkv[...], LAST)
+        standard, _ = standardize(x[rows, :].astype(F32))
+        x[rows, :] = terms.astype(BF16)
+        out += copier.rows([(x, back_out)], at, step)
+        gain_sum[...] += jnp.sum(terms * standard, axis=0, keepdims=True)
+        shift_sum[...] += jnp.sum(terms, axis=0, keepdims=True)
+        qkv_sum[...] += jnp.sum(qg[rows, :].astype(F32), axis=0, keepdims=True)
     wait_all(late)
-    for left, rights, parts in ((act, (g,), down_out), (normed, (qg, ug), col_out)):
-        rows = parts[0].shape[0]
-        for i, part in enumerate(parts):
-            block = left[...]
-            if cut:
-                block = left[:, pl.ds(pl.multiple_of(order[i] * rows, rows), rows)]
-            column = 0
-            for right in rights:
-                stop = column + right.shape[1]
-                part[:, column:stop] = mm(block, right[...], FIRST).astype(part.dtype)
-                column = stop
+    weight_blocks(cut, order, normed, (qg, ug), col_out)
+    wait_all(out)
+
+
+def weight_blocks(cut, order, left, rights, outs):
+    rows = outs[0].shape[0]
+    for i, part in enumerate(outs):
+        block = left[...]
+        if cut:
+            block = left[:, pl.ds(pl.multiple_of(order[i] * rows, rows), rows)]
+        column = 0
+        for right in rights:
+            stop = column + right.shape[1]
+            part[:, column:stop] = mm(block, right[...], FIRST).astype(part.dtype)
+            column = stop
+
+
+def down_kernel(cut, order, act, mixed, g, pw, *outs):
+    weight_blocks(cut, order, act, (g,), outs)
     pw[...] = mm(mixed[...], g[...], FIRST).astype(BF16)
-    wait_all(out)
 
 
 def loss_kernel(branch, x, teacher, valid, bias, factor, out, grad, low, column, square):
@@ -320,7 +368,7 @@
 
 
 def pack_columns(heads, size, paired, units, n_dp, n_ctx, qkv_ref, up_ref, valid_ref, *refs):
-    vectors, out_ref = refs[:-1], refs[-1]
+    vectors, out_ref, small_ref = refs[:-2], refs[-2], refs[-1]
     part = heads * size
     width, unit_rows = n_ctx * part, units // n_dp
     count = jnp.sum(jnp.sum(valid_ref[...].astype(F32), axis=1, keepdims=True), axis=0, keepdims=True)
@@ -331,9 +379,9 @@
     ]
     small += [jnp.broadcast_to(a, (1, 128)) for a in (high, count - 128.0 * high)]
     small = jnp.concatenate(small, axis=0).astype(BF16)
-    small = jnp.concatenate([small, jnp.zeros((out_ref.shape[1] - 8, 128), BF16)], axis=0)
+    for j in range(small_ref.shape[0]):
+        small_ref[j] = small
     for j in range(n_ctx):
-        out_ref[j, :, 3 * part + units :] = small
         for p in range(3):
             at = [p * width + head_of(h, j, heads, n_ctx, paired) * size for h in range(heads)]
             out_ref[j, :, p * part : (p + 1) * part] = jnp.concatenate(
@@ -410,18 +458,18 @@
     return out.reshape((n_dp * block.shape[0],) + block.shape[1:])
 
 
-def exchange_dp(terms, n_dp):
+def reduce_blocks(terms, cut, n_dp, me_dp, later=None):
+    if not cut:
+        return reduce_dp(terms[0], n_dp, me_dp), later
+    parts = [
+        lax.ppermute(terms[k], "dp", [(i, i ^ k) for i in range(n_dp)]) for k in range(1, n_dp)
+    ]
+    if later is not None:
+        parts[0], later = lax.optimization_barrier((parts[0], later))
     total = terms[0]
-    for k in range(1, n_dp):
-        pairs = [(i, i ^ k) for i in range(n_dp)]
-        total = total + lax.ppermute(terms[k], "dp", pairs).astype(F32)
-    return total
-
-
-def reduce_blocks(terms, cut, n_dp, me_dp):
-    if cut:
-        return exchange_dp(terms, n_dp)
-    return reduce_dp(terms[0], n_dp, me_dp)
+    for part in parts:
+        total = total + part.astype(F32)
+    return total, later
 
 
 def reduce_dp(terms, n_dp, me_dp):
@@ -467,12 +515,13 @@
     from_plan = [(b, a) for a, b in to_plan]
     valid = valid_mask.astype(F32).reshape(rows, 1)
     vectors = [norm_gain, norm_bias, proj_bias, down_bias, qkv_bias, up_bias]
-    extra = 128 * max(1, 8 // own)
-    total_cols = 3 * part + units + extra
+    total_cols = 3 * part + units
     if aligned:
-        cols = pl.pallas_call(
+        cols, small = pl.pallas_call(
             functools.partial(pack_columns, heads, size, paired, units, n_dp, n_ctx),
-            out_shape=shape_of((n_ctx, own, total_cols), BF16),
+            out_shape=[
+                shape_of((n_ctx, own, total_cols), BF16), shape_of((n_all, 8, 128), BF16)
+            ],
             compiler_params=PARAMS,
             name="pack_columns",
         )(qkv_weight, up_weight, valid_mask, *vectors)
@@ -481,14 +530,13 @@
         small = jnp.stack(
             [jnp.pad(a, (0, 128 - a.shape[0])) for a in vectors]
             + [jnp.broadcast_to(a.astype(BF16), (128,)) for a in (count // 128, count % 128)]
-        ).reshape(8 * 128)
-        small = jnp.pad(small, (0, own * extra - 8 * 128)).reshape(own, extra)
+        )
+        small = jnp.broadcast_to(small[None], (n_all, 8, 128))
         qkv_cols = qkv_weight.reshape(own, 3, n_ctx, part).transpose(2, 0, 1, 3)
         up_cols = up_weight.reshape(own, n_dp, n_ctx, unit_rows).transpose(2, 0, 1, 3)
         cols = jnp.concatenate(
             [
                 qkv_cols.reshape(n_ctx, own, 3 * part), up_cols.reshape(n_ctx, own, units),
-                jnp.broadcast_to(small[None], (n_ctx, own, extra)),
             ],
             axis=2,
         )
@@ -496,10 +544,9 @@
     cols, tied = lax.optimization_barrier((cols, tied))
     x_rows = lax.all_gather(tokens, "ctx", axis=1, tiled=True).reshape(all_rows, width)
     cols = lax.all_to_all(cols, "ctx", 0, 0, tiled=True).reshape(n_ctx * own, total_cols)
-    cols, segments = lax.optimization_barrier((cols, segments))
+    cols, segments, small = lax.optimization_barrier((cols, segments, small))
     w_cols = gather_dp(cols, n_dp, me_dp)
-    small = w_cols[:, 3 * part + units :].reshape(n_all, own * extra)[:, : 8 * 128]
-    small = small.reshape(n_all, 8, 128).astype(F32)
+    small = lax.all_to_all(small, both, 0, 0, tiled=True).astype(F32)
     gain = small[:, 0, :own].reshape(1, width)
     shift = small[:, 1, :own].reshape(1, width)
     out_bias = (small[:, 2, :own] + small[:, 3, :own]).reshape(1, width)
@@ -603,33 +650,32 @@
         block = (rows_out // n_dp, columns)
         return [(LOCAL, shape_of(block, BF16 if k else F32)) for k in range(n_dp)]
 
-    back, gain_sum, shift_sum, up_bsum, qkv_bsum, proj_wgrad, *terms = kernel_call(
+    back, gain_sum, shift_sum, up_bsum, qkv_bsum, *col_terms = kernel_call(
         functools.partial(backward_kernel, first_len, heads, size, scale, length, STEP, cut),
         "backward_kernel",
-        [SCALAR, LOCAL] + [HBM] * (14 + len(w_split)),
+        [SCALAR, LOCAL] + [HBM] * (12 + len(w_split)),
         [
             store(width),
             *[(LOCAL, shape_of((1, a), F32)) for a in (width, width, units, 3 * part)],
-            (LOCAL, shape_of((part, width), BF16)), *blocks_of(width, 3 * part + units),
-            *blocks_of(units, width),
+            *blocks_of(width, 3 * part + units),
         ],
         [
             *w_scratch, wide(width), wide(units), wide(part), wide(part), wide(part),
             wide(part, F32), wide(part, F32), wide(part, F32), wide(width), wide(width),
-            wide(units), wide(part), *weights, wide(part), wide(units), wide(3 * part), pltpu.VMEM((length, part), F32),
-            pltpu.VMEM((length, part), F32), sems,
+            *weights, wide(part), wide(units), wide(3 * part), wide(part, F32),
+            wide(part, F32), sems,
         ],
         flops=12 * 10**9, moved=2 * 10**7,
     )(
         order, segments, grads, slope, query, key, value, stat, cosine, sine, x_rows, normed,
-        act, mixed, w_down, w_proj, *w_split,
-    )
-    col_terms, down_terms = terms[: len(terms) // 2], terms[len(terms) // 2 :]
+        w_down, w_proj, *w_split,
+    )
     normed_grad = lax.psum_scatter(
         back.reshape(seqs, length, width), "ctx", scatter_dimension=1, tiled=True
     ).reshape(rows, width)
 
-    col_wgrad = reduce_blocks(col_terms, cut, n_dp, me_dp).astype(BF16)
+    col_wgrad, act = reduce_blocks(col_terms, cut, n_dp, me_dp, act)
+    col_wgrad = col_wgrad.astype(BF16)
 
     if paired:
         qkv_bsum = lax.dynamic_update_slice(
@@ -652,6 +698,7 @@
     ]
     sums = jnp.concatenate(parts, axis=1)
     sums = jnp.pad(sums, ((0, 0), (0, -sums.shape[1] % 128)))
+    sums, act = lax.optimization_barrier((sums, act))
     sums = lax.all_to_all(sums, both, 0, 0, tiled=True)
     col_wgrad, sums = lax.optimization_barrier((col_wgrad, sums))
     col_wgrad = lax.all_to_all(
@@ -665,7 +712,12 @@
     up_bgrad = sums[6 * own : 6 * own + unit_rows]
     loss = sums[6 * own + unit_rows] / (valid_count * width)
 
-    down_wgrad = reduce_blocks(down_terms, cut, n_dp, me_dp)
+    proj_wgrad, *down_terms = kernel_call(
+        functools.partial(down_kernel, cut), "down_kernel", [SCALAR] + [LOCAL] * 3,
+        [(LOCAL, shape_of((part, width), BF16)), *blocks_of(units, width)],
+        flops=10**6, moved=10**5,
+    )(order, act, mixed, grads)
+    down_wgrad, _ = reduce_blocks(down_terms, cut, n_dp, me_dp)
     if paired:
         halves = proj_wgrad.reshape(heads, 2, own, width)
         keep = lax.dynamic_index_in_dim(halves, me_core, 1, keepdims=False)

time: 306 us -> 297 us (0.971)
  blocking collectives: 20.1 us -> 0 us
  starting transfers between devices: 28 us -> 34.4 us
  local copies, waits for them, and re-layouts: 15.6 us -> 19.9 us
    all_to_all x1 -> x0, blocking collectives: 20.1 us -> none  [body(): sums = lax.all_to_all(sums, both, 0, 0, tiled=True)]
    all_to_all x0 -> x2, waiting for transfers between devices: none -> 16.3 us  [the longest x1 9.37 us: body(): small = lax.all_to_all(small, both, 0, 0, tiled=True).astype(F32)]
    ppermute x6, waiting for transfers between devices: 22.3 us -> 7.91 us  [gather_dp(): other = lax.ppermute(block, 'dp', pairs)]
    ppermute x3, waiting for transfers between devices: 0.53 us -> 8.48 us  [reduce_dp(): total = total + lax.ppermute(block, 'dp', pairs).astype(F32)]
    pallas_call x0 -> x1, Pallas kernels: none -> 6.84 us  [body(): kernel_call(functools.partial(down_kernel, cut), 'down_kernel', [SCALAR]...]
    all_to_all x0 -> x2, starting transfers between devices: none -> 6.62 us  [the longest x1 3.4 us: body(): sums = lax.all_to_all(sums, both, 0, 0, tiled=True)]
    pallas_call x1, Pallas kernels: 32.6 us -> 26.9 us  [body(): kernel_call(functools.partial(backward_kernel, first_len, heads, size, sc...]
    ppermute x6, waiting for transfers between devices: 10.2 us -> 6.09 us  [reduce_blocks(): lax.ppermute(terms[k], 'dp', [(i, i ^ k) for i in range(n_dp)])]
  transfers between devices with their start and end apart: 23 -> 25, of which waited for: 12 -> 9; matrix products, arithmetic and copies ran while one was open for 11% -> 12% of each run, Pallas kernels for 1% -> 4%
where the time goes in v4:
time: 297 us; the launch traced here: 293 us
  waiting for transfers between devices  136 us (46%)
  Pallas kernels  64.1 us (22%)
  starting transfers between devices  34.4 us (12%)
  other arithmetic  20.7 us (7%)
  local copies, waits for them, and re-layouts  19.9 us (7%)
  between operations  17.6 us (6%)
    all_gather x1, waiting for transfers between devices, body(): lax.all_gather(low.reshape(tokens.shape), 'ctx', axis=1, tiled=True)  44.8 us
    reduce_scatter x1, waiting for transfers between devices, body(): lax.psum_scatter(terms.reshape(seqs, length, width), 'ctx', scatter_dimen...  43.7 us
    pallas_call x1, Pallas kernels, body(): kernel_call(functools.partial(backward_kernel, first_len, heads, size, sc...  26.9 us
    pallas_call x1, Pallas kernels, body(): kernel_call(functools.partial(forward_kernel, first_len, heads, size, sca...  20.2 us
    all_to_all x1, waiting for transfers between devices, body(): small = lax.all_to_all(small, both, 0, 0, tiled=True).astype(F32)  9.37 us
    ppermute x3, waiting for transfers between devices, reduce_dp(): total = total + lax.ppermute(block, 'dp', pairs).astype(F32)  8.48 us
    all_to_all x1, waiting for transfers between devices, body(): lax.all_to_all(cols, 'ctx', 0, 0, tiled=True)  8.29 us
    ppermute x6, starting transfers between devices, gather_dp(): other = lax.ppermute(block, 'dp', pairs)  8.03 us
  transfers between devices with their start and end apart: 25, of which 9 were waited for; matrix products, arithmetic and copies ran while one was open for 12% of the time, Pallas kernels for 4%

profile of v4, /device:TPU:0, one launch (start us, length us, event | category | flops | bytes accessed | tf_op | source)
XLA Modules:
  0.0 293.0 jit_solution(4003938762199759900)
XLA Ops:
  7.9 2.0 pack_columns.1
  9.9 1.0 pad_maximum_fusion
  10.9 3.0 %collective-permute-start = (bf16[160,1024]{1,0:T(8,128)(2,1)S(1)}, bf16[160,1024]{1,0:T(8,128)(2,1)}, u32[]{:S(2)}, u32[]{:S(2)}) collective-permute-start(bf16[160,1024]{1,0:T(8,128)(2,1)S(1)} %pad_maximum_fusion), channel_id=1, source_target_pairs={{0,8},{8,0},{16,24},{24,16},{1,9},{9,1},{17,25},{25,17},{2,10},{10... | collective-permute-start | bytes 983048 | tf_op jit(solution)/shard_map/ppermute | solution.py:456
  13.9 1.5 collective-permute-start.1
  15.4 5.3 %all-to-all-start = ((bf16[8,32,896]{2,1,0:T(8,128)(2,1)}), bf16[8,32,896]{2,1,0:T(8,128)(2,1)S(1)}, u32[]{:S(2)}, u32[]{:S(2)}) async-start(bf16[8,32,896]{2,1,0:T(8,128)(2,1)} %get-tuple-element.58), calls=%async_computation | async-start | bytes 917504 | tf_op jit(solution)/shard_map/all_to_all | solution.py:546
  21.3 1.2 collective-permute-done
  22.5 1.0 bitcast_dynamic-update-slice_fusion.6
  23.5 6.7 %collective-permute-done.1 = bf16[160,1024]{1,0:T(8,128)(2,1)} collective-permute-done((bf16[160,1024]{1,0:T(8,128)(2,1)S(1)}, bf16[160,1024]{1,0:T(8,128)(2,1)}, u32[]{:S(2)}, u32[]{:S(2)}) %collective-permute-start.1) | collective-permute-done | bytes 327712 | tf_op jit(solution)/shard_map/ppermute | solution.py:456
  30.2 1.0 bitcast_dynamic-update-slice_fusion.5
  32.0 5.2 %compare_select_fusion.9 = (f32[128]{0:T(128)S(1)}, f32[128]{0:T(128)S(1)}) fusion(f32[]{:T(128)} %bitcast.12, f32[]{:T(128)} %bitcast.11, f32[]{:T(128)} %bitcast.10, f32[]{:T(128)} %bitcast.9, f32[]{:T(128)} %bitcast.8, f32[]{:T(128)} %bitcast.7, f32[]{:T(128)} %bitcast.6, f32[]{:T(128)} %bitcast.5), kind=kLoop, calls=%fused_computation.66 | loop fusion | flops 5632 | bytes 1056 | tf_op jit(solution)/shard_map/jit(_where)/select_n | solution.py:581
  37.2 1.1 slice.89
  38.3 0.7 copy.46
  39.1 8.3 %all-to-all-done = bf16[8,32,896]{2,1,0:T(8,128)(2,1)S(1)} async-done(((bf16[8,32,896]{2,1,0:T(8,128)(2,1)}), bf16[8,32,896]{2,1,0:T(8,128)(2,1)S(1)}, u32[]{:S(2)}, u32[]{:S(2)}) %all-to-all-start) | async-done | bytes 458784 | tf_op jit(solution)/shard_map/all_to_all | solution.py:546
  47.8 2.5 collective-permute-start.5
  50.8 3.2 %all-to-all-start.1 = ((bf16[32,8,128]{2,1,0:T(8,128)(2,1)}), bf16[32,8,128]{2,1,0:T(8,128)(2,1)S(1)}, u32[]{:S(2)}, u32[]{:S(2)}) async-start(bf16[32,8,128]{2,1,0:T(8,128)(2,1)} %get-tuple-element.60), calls=%async_computation.1 | async-start | bytes 131072 | tf_op jit(solution)/shard_map/all_to_all | solution.py:549
  54.1 2.2 convert_reduce_fusion
  56.4 5.8 %fusion = (f32[2048,128]{1,0:T(8,128)}, f32[2048,128]{1,0:T(8,128)}) fusion(f32[128]{0:T(128)S(1)} %get-tuple-element.126, f32[128]{0:T(128)S(1)} %get-tuple-element.127, f32[2048]{0:T(1024)S(1)} %bitcast.140), kind=kLoop, calls=%fused_computation.4 | loop fusion | flops 524288 | bytes 2106368 | tf_op jit(solution)/shard_map/mul | solution.py:581
  62.3 9.4 %all-to-all-done.1 = bf16[32,8,128]{2,1,0:T(8,128)(2,1)S(1)} async-done(((bf16[32,8,128]{2,1,0:T(8,128)(2,1)}), bf16[32,8,128]{2,1,0:T(8,128)(2,1)S(1)}, u32[]{:S(2)}, u32[]{:S(2)}) %all-to-all-start.1) | async-done | bytes 65568 | tf_op jit(solution)/shard_map/all_to_all | solution.py:549
  74.7 1.1 bitcast_dynamic-update-slice_fusion.2
  75.9 1.2 copy-done.1
  77.1 20.2 %forward_kernel.1 = (bf16[2048,1024]{1,0:T(8,128)(2,1)}, bf16[2048,128]{1,0:T(8,128)(2,1)}, bf16[2048,128]{1,0:T(8,128)(2,1)}, bf16[2048,128]{1,0:T(8,128)(2,1)}...) custom-call(f32[1,1024]{1,0:T(1,128)} %reshape_squeeze.15.gain, ...), custom_call_target="tpu_custom_call" | custom-call | flops 10000000000 | bytes 20000000 | tf_op jit(solution)/shard_map/forward_kernel/pallas_call | solution.py:606
  98.1 0.8 copy.47.valid
  101.5 43.7 %reduce-scatter.3.cloned.1.call-done = bf16[2,128,1024]{2,1,0:T(8,128)(2,1)} async-done(((bf16[2,1024,1024]{2,1,0:T(8,128)(2,1)}), bf16[2,128,1024]{2,1,0:T(8,128)(2,1)}) %reduce-scatter.3.cloned.1.call-update) | async-done | bytes 524304 | tf_op jit(solution)/shard_map/reduce_scatter | solution.py:623
  145.2 3.2 %loss_kernel.1 = (bf16[256,1024]{1,0:T(8,128)(2,1)}, f32[256,1024]{1,0:T(8,128)}, bf16[256,1024]{1,0:T(8,128)(2,1)}, f32[1,1024]{1,0:T(1,128)}, f32[1,1]{1,0:T(1,128)}) custom-call(bf16[256,1024]{1,0:T(8,128)(2,1)} %bitcast.130, bf16[256,1024]{1,0:T(8,128)(2,1)} %bitcast.111, bf16[256,1024]{1,0:T(8,128)(2,1)} %bitcast.129, f32[256,1]{1,0:T(8,128)} %copy.47.valid, ...), custom_call_target="tpu_custom_call" | custom-call | flops 1000000 | bytes 3000000 | tf_op jit(solution)/shard_map/loss_kernel/pallas_call | solution.py:631
  149.0 44.8 %all-gather.5.cloned.1.call-done = bf16[2,1024,1024]{2,1,0:T(8,128)(2,1)} async-done(((bf16[2,128,1024]{2,1,0:T(8,128)(2,1)}), bf16[2,1024,1024]{2,1,0:T(8,128)(2,1)}) %all-gather.5.cloned.1.call-update) | async-done | bytes 4194320 | tf_op jit(solution)/shard_map/all_gather | solution.py:641
  193.8 26.9 %backward_kernel.1 = (bf16[2048,1024]{1,0:T(8,128)(2,1)}, f32[1,1024]{1,0:T(1,128)}, f32[1,1024]{1,0:T(1,128)}, f32[1,512]{1,0:T(1,128)}, f32[1,384]{1,0:T(1,128...) custom-call(s32[4]{0:T(128)} %pad_add_fusion.order, ...), custom_call_target="tpu_custom_call" | custom-call | flops 12000000000 | bytes 20000000 | tf_op jit(solution)/shard_map/backward_kernel/pallas_call | solution.py:653
  220.8 0.9 copy-done.14
  221.7 1.5 collective-permute-start.7
  223.2 1.5 collective-permute-start.8
  229.0 6.1 %collective-permute-done.7 = bf16[256,896]{1,0:T(8,128)(2,1)S(1)} collective-permute-done((bf16[256,896]{1,0:T(8,128)(2,1)S(1)}, bf16[256,896]{1,0:T(8,128)(2,1)S(1)}, u32[]{:S(2)}, u32[]{:S(2)}) %collective-permute-start.7) | collective-permute-done | bytes 458784 | tf_op jit(solution)/shard_map/ppermute | solution.py:465
  235.1 6.8 %down_kernel.1 = (bf16[128,1024]{1,0:T(8,128)(2,1)}, f32[128,1024]{1,0:T(8,128)}, bf16[128,1024]{1,0:T(8,128)(2,1)}, bf16[128,1024]{1,0:T(8,128)(2,1)}, bf16[128,1024]{1,0:T(8,128)(2,1)}) custom-call(s32[4]{0:T(128)} %pad_add_fusion.order, bf16[2048,512]{1,0:T(8,128)(2,1)} %get-tuple-element.92.act, bf16[2048,128]{1,0:T(8,128)(2,1)} %get-tuple-element.93.mixed, ...), custom_call_target="tpu_custom_call" | custom-call | flops 1000000 | bytes 100000 | tf_op jit(solution)/shard_map/down_kernel/pallas_call | solution.py:715
  241.9 0.9 dynamic-slice_bitcast_fusion
  243.6 3.4 %all-to-all-start.2 = ((f32[32,1,384]{2,1,0:T(1,128)}), f32[32,1,384]{2,1,0:T(1,128)S(1)}, u32[]{:S(2)}, u32[]{:S(2)}) async-start(f32[32,1,384]{2,1,0:T(1,128)} %copy.50), calls=%async_computation.3 | async-start | bytes 98304 | tf_op jit(solution)/shard_map/all_to_all | solution.py:702
  247.1 1.0 add_convert_fusion
  248.0 6.9 %all-to-all-done.2 = f32[32,1,384]{2,1,0:T(1,128)S(1)} async-done(((f32[32,1,384]{2,1,0:T(1,128)}), f32[32,1,384]{2,1,0:T(1,128)S(1)}, u32[]{:S(2)}, u32[]{:S(2)}) %all-to-all-start.2) | async-done | bytes 49184 | tf_op jit(solution)/shard_map/all_to_all | solution.py:702
  255.0 3.5 %all-to-all-start.3 = ((bf16[8,32,896]{2,1,0:T(8,128)(2,1)}), bf16[8,32,896]{2,1,0:T(8,128)(2,1)S(1)}, u32[]{:S(2)}, u32[]{:S(2)}) async-start(bf16[8,32,896]{2,1,0:T(8,128)(2,1)} %bitcast.54), calls=%async_computation.5 | async-start | bytes 917504 | tf_op jit(solution)/shard_map/all_to_all | solution.py:704
  258.6 1.0 collective-permute-start.11
  259.6 1.1 collective-permute-start.14
  260.7 0.9 collective-permute-start.15
  261.7 1.4 collective-permute-start.16
  263.1 0.8 collective-permute-start.12
  263.9 1.9 collective-permute-start.13
  268.7 8.5 %collective-permute-done.12 = bf16[32,1024]{1,0:T(8,128)(2,1)S(1)} collective-permute-done((bf16[32,1024]{1,0:T(8,128)(2,1)S(1)}, bf16[32,1024]{1,0:T(8,128)(2,1)S(1)}, u32[]{:S(2)}, u32[]{:S(2)}) %collective-permute-start.12) | collective-permute-done | bytes 65568 | tf_op jit(solution)/shard_map/ppermute | solution.py:482
  277.2 0.7 fusion.2
  277.9 0.9 convert_add_fusion
  278.9 0.8 copy-done
  279.6 2.0 unpack_columns.1
  281.6 3.0 %norm_back_kernel.1 = bf16[256,1024]{1,0:T(8,128)(2,1)} custom-call(bf16[256,1024]{1,0:T(8,128)(2,1)} %bitcast.127, bf16[256,1024]{1,0:T(8,128)(2,1)} %bitcast.112, f32[256,1024]{1,0:T(8,128)} %get-tuple-element.89.og, f32[1,1024]{1,0:T(1,128)} %reshape_squeeze.15.gain), custom_call_target="tpu_custom_call" | custom-call | flops 1000000 | bytes 3000000 | tf_op jit(solution)/shard_map/norm_back_kernel/pallas_call | solution.py:735
  (119 shorter events, 17.0 us)
Async XLA Ops:
  7.2 68.7 %all-gather.3.cloned.1.call-start = ((), (), s32[]{:S(2)}) async-start(), calls=%async_computation.6 | async-start | bytes 4718592 | tf_op jit(solution)/shard_map/all_gather | solution.py:545
  10.9 11.6 %collective-permute-start = (bf16[160,1024]{1,0:T(8,128)(2,1)S(1)}, bf16[160,1024]{1,0:T(8,128)(2,1)}, u32[]{:S(2)}, u32[]{:S(2)}) collective-permute-start(bf16[160,1024]{1,0:T(8,128)(2,1)S(1)} %pad_maximum_fusion), channel_id=1, source_target_pairs={{0,8},{8,0},{16,24},{24,16},{1,9},{9,1},{17,25},{25,17},{2,10},{10... | collective-permute-start | bytes 983048 | tf_op jit(solution)/shard_map/ppermute | solution.py:456
  13.9 16.3 %collective-permute-start.1 = (bf16[160,1024]{1,0:T(8,128)(2,1)S(1)}, bf16[160,1024]{1,0:T(8,128)(2,1)}, u32[]{:S(2)}, u32[]{:S(2)}) collective-permute-start(bf16[160,1024]{1,0:T(8,128)(2,1)S(1)} %pad_maximum_fusion), channel_id=1, source_target_pairs={{0,16},{8,24},{16,0},{24,8},{1,17},{9,25},{17,1},{25,9},{2,18},{10... | collective-permute-start | bytes 983048 | tf_op jit(solution)/shard_map/ppermute | solution.py:456
  15.4 15.8 %collective-permute-start.2 = (bf16[160,1024]{1,0:T(8,128)(2,1)S(1)}, bf16[160,1024]{1,0:T(8,128)(2,1)S(1)}, u32[]{:S(2)}, u32[]{:S(2)}) collective-permute-start(bf16[160,1024]{1,0:T(8,128)(2,1)S(1)} %pad_maximum_fusion), channel_id=1, source_target_pairs={{0,24},{8,16},{16,8},{24,0},{1,25},{9,17},{17,9},{25,1},{2,26},{10... | collective-permute-start | bytes 983048 | tf_op jit(solution)/shard_map/ppermute | solution.py:456
  15.4 31.9 %all-to-all-start = ((bf16[8,32,896]{2,1,0:T(8,128)(2,1)}), bf16[8,32,896]{2,1,0:T(8,128)(2,1)S(1)}, u32[]{:S(2)}, u32[]{:S(2)}) async-start(bf16[8,32,896]{2,1,0:T(8,128)(2,1)} %get-tuple-element.58), calls=%async_computation | async-start | bytes 917504 | tf_op jit(solution)/shard_map/all_to_all | solution.py:546
  31.3 7.0 %collective-permute-start.3 = (bf16[2,32,1024]{2,1,0:T(8,128)(2,1)S(1)}, bf16[2,32,1024]{2,1,0:T(8,128)(2,1)S(1)}, u32[]{:S(2)}, u32[]{:S(2)}) collective-permute-start(bf16[2,32,1024]{2,1,0:T(8,128)(2,1)S(1)} %dynamic-slice_bitcast_fusion.1), channel_id=1, source_target_pairs={{0,1},{1,0},{2,3},{3,2},{4,5},{5,4},{6,7},{7,6},{8,9},{9,8},{10,11... | collective-permute-start | bytes 393224 | tf_op jit(solution)/shard_map/ppermute | solution.py:588
  37.2 16.9 %copy-start.5 = (s32[2,1024]{1,0:T(2,128)S(1)}, s32[2,1024]{1,0:T(2,128)}, u32[]{:S(2)}) copy-start(s32[2,1024]{1,0:T(2,128)} %seg_row.1) | copy-start | bytes 24580
  47.4 27.3 %collective-permute-start.4 = (bf16[256,896]{1,0:T(8,128)(2,1)S(1)}, bf16[256,896]{1,0:T(8,128)(2,1)}, u32[]{:S(2)}, u32[]{:S(2)}) collective-permute-start(bf16[256,896]{1,0:T(8,128)(2,1)S(1)} %bitcast.117), channel_id=1, source_target_pairs={{0,8},{8,0},{16,24},{24,16},{1,9},{9,1},{17,25},{25,17},{2,10},{10... | collective-permute-start | bytes 1376264 | tf_op jit(solution)/shard_map/ppermute | solution.py:456
  47.8 27.9 %collective-permute-start.5 = (bf16[256,896]{1,0:T(8,128)(2,1)S(1)}, bf16[256,896]{1,0:T(8,128)(2,1)S(1)}, u32[]{:S(2)}, u32[]{:S(2)}) collective-permute-start(bf16[256,896]{1,0:T(8,128)(2,1)S(1)} %bitcast.118), channel_id=1, source_target_pairs={{0,16},{8,24},{16,0},{24,8},{1,17},{9,25},{17,1},{25,9},{2,18},{10... | collective-permute-start | bytes 1376264 | tf_op jit(solution)/shard_map/ppermute | solution.py:456
  50.3 25.5 %collective-permute-start.6 = (bf16[256,896]{1,0:T(8,128)(2,1)S(1)}, bf16[256,896]{1,0:T(8,128)(2,1)S(1)}, u32[]{:S(2)}, u32[]{:S(2)}) collective-permute-start(bf16[256,896]{1,0:T(8,128)(2,1)S(1)} %bitcast.119), channel_id=1, source_target_pairs={{0,24},{8,16},{16,8},{24,0},{1,25},{9,17},{17,9},{25,1},{2,26},{10... | collective-permute-start | bytes 1376264 | tf_op jit(solution)/shard_map/ppermute | solution.py:456
  50.8 20.9 %all-to-all-start.1 = ((bf16[32,8,128]{2,1,0:T(8,128)(2,1)}), bf16[32,8,128]{2,1,0:T(8,128)(2,1)S(1)}, u32[]{:S(2)}, u32[]{:S(2)}) async-start(bf16[32,8,128]{2,1,0:T(8,128)(2,1)} %get-tuple-element.60), calls=%async_computation.1 | async-start | bytes 131072 | tf_op jit(solution)/shard_map/all_to_all | solution.py:549
  54.1 91.1 %reduce-scatter.3.cloned.1.call-start = ((), (), s32[]{:S(2)}) async-start(), calls=%async_computation.7 | async-start | bytes 4718592 | tf_op jit(solution)/shard_map/reduce_scatter | solution.py:623
  75.9 1.2 copy-start.1
  97.4 0.7 copy-start.6
  97.4 96.4 %all-gather.5.cloned.1.call-start = ((), (), s32[]{:S(2)}) async-start(), calls=%async_computation.8 | async-start | bytes 4718592 | tf_op jit(solution)/shard_map/all_gather | solution.py:641
  148.4 133.2 %reduce-scatter.5.cloned.1.call-start = ((), (), s32[]{:S(2)}) async-start(), calls=%async_computation.9 | async-start | bytes 4718592 | tf_op jit(solution)/shard_map/reduce_scatter | solution.py:673
  220.7 1.0 copy-start.14
  220.7 3.9 %copy-start.13 = (bf16[256,896]{1,0:T(8,128)(2,1)S(1)}, bf16[256,896]{1,0:T(8,128)(2,1)}, u32[]{:S(2)}) copy-start(bf16[256,896]{1,0:T(8,128)(2,1)} %get-tuple-element.78) | copy-start | bytes 1376260
  220.7 5.0 %copy-start.7 = (f32[1,1024]{1,0:T(1,128)S(1)}, f32[1,1024]{1,0:T(1,128)}, u32[]{:S(2)}) copy-start(f32[1,1024]{1,0:T(1,128)} %get-tuple-element.81) | copy-start | bytes 12292
  220.7 5.7 %copy-start.11 = (f32[1,384]{1,0:T(1,128)S(1)}, f32[1,384]{1,0:T(1,128)}, u32[]{:S(2)}) copy-start(f32[1,384]{1,0:T(1,128)} %get-tuple-element.82) | copy-start | bytes 4612
  220.8 6.0 %copy-start.9 = (f32[1,1024]{1,0:T(1,128)S(1)}, f32[1,1024]{1,0:T(1,128)}, u32[]{:S(2)}) copy-start(f32[1,1024]{1,0:T(1,128)} %get-tuple-element.79) | copy-start | bytes 12292
  220.8 6.7 %copy-start.8 = (f32[1,1024]{1,0:T(1,128)S(1)}, f32[1,1024]{1,0:T(1,128)}, u32[]{:S(2)}) copy-start(f32[1,1024]{1,0:T(1,128)} %get-tuple-element.80) | copy-start | bytes 12292
  220.8 7.4 %copy-start.10 = (f32[1,512]{1,0:T(1,128)S(1)}, f32[1,512]{1,0:T(1,128)}, u32[]{:S(2)}) copy-start(f32[1,512]{1,0:T(1,128)} %get-tuple-element.83) | copy-start | bytes 6148
  221.7 13.4 %collective-permute-start.7 = (bf16[256,896]{1,0:T(8,128)(2,1)S(1)}, bf16[256,896]{1,0:T(8,128)(2,1)S(1)}, u32[]{:S(2)}, u32[]{:S(2)}) collective-permute-start(bf16[256,896]{1,0:T(8,128)(2,1)S(1)} %copy-done.14), channel_id=1, source_target_pairs={{0,8},{8,0},{16,24},{24,16},{1,9},{9,1},{17,25},{25,17},{2,10},{10... | collective-permute-start | bytes 1376264 | tf_op jit(solution)/shard_map/ppermute | solution.py:465
  223.2 23.8 %collective-permute-start.8 = (bf16[256,896]{1,0:T(8,128)(2,1)}, bf16[256,896]{1,0:T(8,128)(2,1)S(1)}, u32[]{:S(2)}, u32[]{:S(2)}) collective-permute-start(bf16[256,896]{1,0:T(8,128)(2,1)} %get-tuple-element.77), channel_id=1, source_target_pairs={{0,16},{8,24},{16,0},{24,8},{1,17},{9,25},{17,1},{25,9},{2,18},{10... | collective-permute-start | bytes 1376264 | tf_op jit(solution)/shard_map/ppermute | solution.py:465
  224.7 22.4 %collective-permute-start.9 = (bf16[256,896]{1,0:T(8,128)(2,1)S(1)}, bf16[256,896]{1,0:T(8,128)(2,1)S(1)}, u32[]{:S(2)}, u32[]{:S(2)}) collective-permute-start(bf16[256,896]{1,0:T(8,128)(2,1)S(1)} %copy-done.13), channel_id=1, source_target_pairs={{0,24},{8,16},{16,8},{24,0},{1,25},{9,17},{17,9},{25,1},{2,26},{10... | collective-permute-start | bytes 1376264 | tf_op jit(solution)/shard_map/ppermute | solution.py:465
  235.1 11.9 %copy-start.2 = (f32[256,896]{1,0:T(8,128)S(1)}, f32[256,896]{1,0:T(8,128)}, u32[]{:S(2)}) copy-start(f32[256,896]{1,0:T(8,128)} %get-tuple-element.73) | copy-start | bytes 2752516
  242.9 15.6 %collective-permute-start.10 = (bf16[2,32,1024]{2,1,0:T(8,128)(2,1)S(1)}, bf16[2,32,1024]{2,1,0:T(8,128)(2,1)S(1)}, u32[]{:S(2)}, u32[]{:S(2)}) collective-permute-start(bf16[2,32,1024]{2,1,0:T(8,128)(2,1)S(1)} %dynamic-slice_bitcast_fusion), channel_id=1, source_target_pairs={{0,1},{1,0},{2,3},{3,2},{4,5},{5,4},{6,7},{7,6},{8,9},{9,8},{10,11... | collective-permute-start | bytes 393224 | tf_op jit(solution)/shard_map/ppermute | solution.py:724
  243.6 11.4 %all-to-all-start.2 = ((f32[32,1,384]{2,1,0:T(1,128)}), f32[32,1,384]{2,1,0:T(1,128)S(1)}, u32[]{:S(2)}, u32[]{:S(2)}) async-start(f32[32,1,384]{2,1,0:T(1,128)} %copy.50), calls=%async_computation.3 | async-start | bytes 98304 | tf_op jit(solution)/shard_map/all_to_all | solution.py:702
  247.0 11.4 %copy-start.4 = (bf16[128,1024]{1,0:T(8,128)(2,1)S(1)}, bf16[128,1024]{1,0:T(8,128)(2,1)}, u32[]{:S(2)}) copy-start(bf16[128,1024]{1,0:T(8,128)(2,1)} %get-tuple-element.94) | copy-start | bytes 786436
  247.1 13.7 %copy-start.16 = (bf16[128,1024]{1,0:T(8,128)(2,1)S(1)}, bf16[128,1024]{1,0:T(8,128)(2,1)}, u32[]{:S(2)}) copy-start(bf16[128,1024]{1,0:T(8,128)(2,1)} %get-tuple-element.98) | copy-start | bytes 786436
  247.1 14.6 %copy-start.15 = (bf16[128,1024]{1,0:T(8,128)(2,1)S(1)}, bf16[128,1024]{1,0:T(8,128)(2,1)}, u32[]{:S(2)}) copy-start(bf16[128,1024]{1,0:T(8,128)(2,1)} %get-tuple-element.99) | copy-start | bytes 786436
  248.0 29.9 %copy-start.3 = (f32[128,1024]{1,0:T(8,128)S(1)}, f32[128,1024]{1,0:T(8,128)}, u32[]{:S(2)}) copy-start(f32[128,1024]{1,0:T(8,128)} %get-tuple-element.96) | copy-start | bytes 1572868
  255.0 23.9 %all-to-all-start.3 = ((bf16[8,32,896]{2,1,0:T(8,128)(2,1)}), bf16[8,32,896]{2,1,0:T(8,128)(2,1)S(1)}, u32[]{:S(2)}, u32[]{:S(2)}) async-start(bf16[8,32,896]{2,1,0:T(8,128)(2,1)} %bitcast.54), calls=%async_computation.5 | async-start | bytes 917504 | tf_op jit(solution)/shard_map/all_to_all | solution.py:704
  258.6 5.3 %collective-permute-start.11 = (bf16[32,1024]{1,0:T(8,128)(2,1)S(1)}, bf16[32,1024]{1,0:T(8,128)(2,1)S(1)}, u32[]{:S(2)}, u32[]{:S(2)}) collective-permute-start(bf16[32,1024]{1,0:T(8,128)(2,1)S(1)} %get-tuple-element.109), channel_id=1, source_target_pairs={{0,8},{8,0},{16,24},{24,16},{1,9},{9,1},{17,25},{25,17},{2,10},{10... | collective-permute-start | bytes 196616 | tf_op jit(solution)/shard_map/ppermute | solution.py:482
  259.6 18.3 %collective-permute-start.14 = (bf16[128,1024]{1,0:T(8,128)(2,1)}, bf16[128,1024]{1,0:T(8,128)(2,1)S(1)}, u32[]{:S(2)}, u32[]{:S(2)}) collective-permute-start(bf16[128,1024]{1,0:T(8,128)(2,1)} %get-tuple-element.97), channel_id=1, source_target_pairs={{0,8},{8,0},{16,24},{24,16},{1,9},{9,1},{17,25},{25,17},{2,10},{10... | collective-permute-start | bytes 786440 | tf_op jit(solution)/shard_map/ppermute | solution.py:465
  260.7 17.2 %collective-permute-start.15 = (bf16[128,1024]{1,0:T(8,128)(2,1)S(1)}, bf16[128,1024]{1,0:T(8,128)(2,1)S(1)}, u32[]{:S(2)}, u32[]{:S(2)}) collective-permute-start(bf16[128,1024]{1,0:T(8,128)(2,1)S(1)} %copy-done.16), channel_id=1, source_target_pairs={{0,16},{8,24},{16,0},{24,8},{1,17},{9,25},{17,1},{25,9},{2,18},{10... | collective-permute-start | bytes 786440 | tf_op jit(solution)/shard_map/ppermute | solution.py:465
  261.7 16.2 %collective-permute-start.16 = (bf16[128,1024]{1,0:T(8,128)(2,1)S(1)}, bf16[128,1024]{1,0:T(8,128)(2,1)S(1)}, u32[]{:S(2)}, u32[]{:S(2)}) collective-permute-start(bf16[128,1024]{1,0:T(8,128)(2,1)S(1)} %copy-done.15), channel_id=1, source_target_pairs={{0,24},{8,16},{16,8},{24,0},{1,25},{9,17},{17,9},{25,1},{2,26},{10... | collective-permute-start | bytes 786440 | tf_op jit(solution)/shard_map/ppermute | solution.py:465
  263.1 14.0 %collective-permute-start.12 = (bf16[32,1024]{1,0:T(8,128)(2,1)S(1)}, bf16[32,1024]{1,0:T(8,128)(2,1)S(1)}, u32[]{:S(2)}, u32[]{:S(2)}) collective-permute-start(bf16[32,1024]{1,0:T(8,128)(2,1)S(1)} %get-tuple-element.110), channel_id=1, source_target_pairs={{0,16},{8,24},{16,0},{24,8},{1,17},{9,25},{17,1},{25,9},{2,18},{10... | collective-permute-start | bytes 196616 | tf_op jit(solution)/shard_map/ppermute | solution.py:482
  263.9 13.3 %collective-permute-start.13 = (bf16[32,1024]{1,0:T(8,128)(2,1)S(1)}, bf16[32,1024]{1,0:T(8,128)(2,1)S(1)}, u32[]{:S(2)}, u32[]{:S(2)}) collective-permute-start(bf16[32,1024]{1,0:T(8,128)(2,1)S(1)} %get-tuple-element.111), channel_id=1, source_target_pairs={{0,24},{8,16},{16,8},{24,0},{1,25},{9,17},{17,9},{25,1},{2,26},{10... | collective-permute-start | bytes 196616 | tf_op jit(solution)/shard_map/ppermute | solution.py:482
  266.4 18.3 %copy-start.12 = (f32[32]{0:T(128)}, f32[32]{0:T(128)S(1)}, u32[]{:S(2)}) copy-start(f32[32]{0:T(128)S(1)} %get-tuple-element.155) | copy-start | bytes 388
  278.9 0.8 copy-start
Sparse Core Ops, SparseCore 0:
  9.6 60.9 all-gather.2
  97.5 47.6 reduce-scatter.2
  148.5 45.2 all-gather.4
  220.9 55.1 reduce-scatter.4

commit v5 on v4

--- a/solution.py
+++ b/solution.py
@@ -17,7 +17,7 @@
 PARAMS = pltpu.CompilerParams(vmem_limit_bytes=56 * 1024 * 1024)
 COPIES = 128
 STEP = 512
-TOGETHER = 2
+TOGETHER = 4
 LAST = ((1,), (1,))
 FIRST = ((0,), (0,))
 
@@ -106,6 +106,16 @@
         return [self.start(a.at[at : at + step], b.at[at : at + step]) for a, b in pairs]
 
 
+def fetch_columns(copier, order, sources, targets):
+    if len(targets) == 2:
+        return [copier.start(a, b) for a, b in zip(sources, targets)]
+    rows = sources[0].shape[0]
+    return [
+        copier.start(a, targets[0].at[pl.ds(pl.multiple_of(order[k] * rows, rows), rows)])
+        for k, a in enumerate(sources)
+    ]
+
+
 def view_columns(refs, part, units):
     if len(refs) == 2:
         return refs
@@ -118,13 +128,12 @@
 
 
 def forward_kernel(
-    first_len, heads, size, scale, length, step,
-    gain, shift, bqkv, bup, seg_row, x_in, cos_in, sin_in, wdown_in, wproj_in, *refs,
+    first_len, heads, size, scale, length, step, split,
+    order, gain, shift, bqkv, bup, seg_row, x_in, cos_in, sin_in, wdown_in, wproj_in, *refs,
 ):
     (x, cosine, sine, wdown, wproj,
      normed, q, k, v, act, slope, mixed, stat, terms, sems) = refs[-15:]
-    split = (len(refs) - 24) // 2
-    w_in, w = refs[:split], refs[split + 9 : 2 * split + 9]
+    w_in, w = refs[:split], refs[split + 9 : -15]
     (n_out, q_out, k_out, v_out, act_out, slope_out, mixed_out, stat_out, terms_out) = refs[
         split : split + 9
     ]
@@ -135,7 +144,7 @@
     starts = range(0, total, step)
     tables = ((cos_in, cosine), (sin_in, sine))
     x_copies = {0: copier.rows([(x_in, x)], 0, step)}
-    w_copies = [copier.start(a, b) for a, b in zip(w_in, w)]
+    w_copies = fetch_columns(copier, order, w_in, w)
     t_copies = {0: copier.rows(tables, 0, step)}
     for at in starts[1:]:
         x_copies[at] = copier.rows([(x_in, x)], at, step)
@@ -207,16 +216,16 @@
 
 
 def backward_kernel(
-    first_len, heads, size, scale, length, step, cut,
+    first_len, heads, size, scale, length, step, cut, split,
     order, seg_row, g_in, slope_in, q_in, k_in, v_in, stat_in, cos_in, sin_in, x_in, n_in,
     wdown_in, wproj_in, *refs,
 ):
     (g, slope, q, k, v, stat, cosine, sine, x, normed, wdown, wproj,
      mg, ug, qg, dk, dv, sems) = refs[-18:]
-    split = 1 if refs[0].shape[1] > 3 * heads * size else 2
     w_in, refs = refs[:split], refs[split:-18]
     back_out, gain_sum, shift_sum, up_sum, qkv_sum = refs[:5]
-    col_out, w = refs[5 : len(refs) - split], refs[len(refs) - split :]
+    held = 2 if split == 2 else 1
+    col_out, w = refs[5 : len(refs) - held], refs[len(refs) - held :]
     for ref in (gain_sum, shift_sum, up_sum, qkv_sum):
         ref[...] = jnp.zeros_like(ref)
     copier = Copier(sems)
@@ -239,7 +248,7 @@
             origin = at + step - length
             s_copies[origin] = copier.rows(saved, origin, length)
             if origin == 0:
-                w_copies += [copier.start(a, b) for a, b in zip(w_in, w)]
+                w_copies += fetch_columns(copier, order, w_in, w)
             x_copies[origin] = copier.rows([(x_in, x)], origin, length)
     late = [copier.start(n_in, normed)]
     out = []
@@ -335,16 +344,22 @@
     pw[...] = mm(mixed[...], g[...], FIRST).astype(BF16)
 
 
-def loss_kernel(branch, x, teacher, valid, bias, factor, out, grad, low, column, square):
+def loss_terms(branch, x, teacher, valid, bias, factor):
     full = x[...].astype(F32) + (branch[...].astype(F32) + bias[...])
+    error = valid[...] * (full - teacher[...].astype(F32))
+    return full, error, factor[...] * error
+
+
+def loss_kernel(branch, x, teacher, valid, bias, factor, low):
+    low[...] = loss_terms(branch, x, teacher, valid, bias, factor)[2].astype(BF16)
+
+
+def output_kernel(branch, x, teacher, valid, bias, factor, out, grad, column, square):
+    full, error, scaled = loss_terms(branch, x, teacher, valid, bias, factor)
     out[...] = full.astype(BF16)
-    error = valid[...] * (full - teacher[...].astype(F32))
+    grad[...] = scaled
     square[...] = jnp.sum(jnp.sum(error * error, axis=0, keepdims=True), axis=1, keepdims=True)
-    scaled = factor[...] * error
-    grad[...] = scaled
-    rounded = scaled.astype(BF16)
-    low[...] = rounded
-    column[...] = jnp.sum(rounded.astype(F32), axis=0, keepdims=True)
+    column[...] = jnp.sum(scaled.astype(BF16).astype(F32), axis=0, keepdims=True)
 
 
 def norm_back_kernel(ng, x, og, gain, out):
@@ -545,7 +560,6 @@
     x_rows = lax.all_gather(tokens, "ctx", axis=1, tiled=True).reshape(all_rows, width)
     cols = lax.all_to_all(cols, "ctx", 0, 0, tiled=True).reshape(n_ctx * own, total_cols)
     cols, segments, small = lax.optimization_barrier((cols, segments, small))
-    w_cols = gather_dp(cols, n_dp, me_dp)
     small = lax.all_to_all(small, both, 0, 0, tiled=True).astype(F32)
     gain = small[:, 0, :own].reshape(1, width)
     shift = small[:, 1, :own].reshape(1, width)
@@ -563,10 +577,16 @@
     up_b = lax.dynamic_index_in_dim(up_b, me_ctx, 1, keepdims=False).reshape(1, units)
     valid_count = 128.0 * jnp.sum(small[:, 6, 0]) + jnp.sum(small[:, 7, 0])
     sliced = (3 * part) % 128 == 0 and units % 128 == 0
-    if sliced:
-        w_split = [w_cols]
+    order = jnp.stack([me_dp ^ k for k in range(n_dp)]).astype(jnp.int32)
+    if sliced and n_dp > 2:
+        w_split = [cols] + [
+            lax.ppermute(cols, "dp", [(i, i ^ k) for i in range(n_dp)]) for k in range(1, n_dp)
+        ]
+        w_scratch = [pltpu.VMEM((width, total_cols), BF16)]
     else:
+        w_cols = gather_dp(cols, n_dp, me_dp)
         w_split = [w_cols[:, : 3 * part], w_cols[:, 3 * part : 3 * part + units]]
+        w_scratch = [pltpu.VMEM(a.shape, BF16) for a in w_split]
     token = jnp.arange(length, dtype=jnp.int32)
     half = ROT // 2
     lane = jnp.arange(part, dtype=jnp.int32) % size
@@ -600,13 +620,14 @@
     def store(columns, dtype=BF16):
         return (HBM, shape_of((all_rows, columns), dtype))
 
-    w_scratch = [pltpu.VMEM(a.shape, BF16) for a in w_split]
     weights = [pltpu.VMEM((units, width), BF16), pltpu.VMEM((part, width), BF16)]
     sems = pltpu.SemaphoreType.DMA((COPIES,))
     normed, query, key, value, act, slope, mixed, stat, terms = kernel_call(
-        functools.partial(forward_kernel, first_len, heads, size, scale, length, STEP),
+        functools.partial(
+            forward_kernel, first_len, heads, size, scale, length, STEP, len(w_split)
+        ),
         "forward_kernel",
-        [LOCAL] * 5 + [HBM] * (5 + len(w_split)),
+        [SCALAR] + [LOCAL] * 5 + [HBM] * (5 + len(w_split)),
         [
             store(width), store(part), store(part), store(part), store(units), store(units),
             store(part), store(part, F32), store(width),
@@ -618,7 +639,7 @@
         ],
         flops=10 * 10**9, moved=2 * 10**7,
     )(
-        gain, shift, qkv_b, up_b, segments, x_rows, cosine, sine, w_down, w_proj, *w_split
+        order, gain, shift, qkv_b, up_b, segments, x_rows, cosine, sine, w_down, w_proj, *w_split
     )
     branch = lax.psum_scatter(
         terms.reshape(seqs, length, width), "ctx", scatter_dimension=1, tiled=True
@@ -628,20 +649,24 @@
     factor = (total_tokens / valid_count).reshape(1, 1)
     tokens_rows = tokens.reshape(rows, width)
     own_block = (rows, width)
-    layer_out, out_grad, low, column, square = kernel_call(
-        loss_kernel, "loss_kernel", [LOCAL] * 6,
+    loss_in = (branch, tokens_rows, teacher.reshape(rows, width), valid, out_bias, factor)
+    (low,) = kernel_call(
+        loss_kernel, "loss_kernel", [LOCAL] * 6, [(LOCAL, shape_of(own_block, BF16))],
+        flops=10**6, moved=2 * 10**6,
+    )(*loss_in)
+    low, *loss_in = lax.optimization_barrier((low, *loss_in))
+    layer_out, out_grad, column, square = kernel_call(
+        output_kernel, "output_kernel", [LOCAL] * 6,
         [
             (LOCAL, shape_of(own_block, BF16)), (LOCAL, shape_of(own_block, F32)),
-            (LOCAL, shape_of(own_block, BF16)), (LOCAL, shape_of((1, width), F32)),
-            (LOCAL, shape_of((1, 1), F32)),
+            (LOCAL, shape_of((1, width), F32)), (LOCAL, shape_of((1, 1), F32)),
         ],
         flops=10**6, moved=3 * 10**6,
-    )(branch, tokens_rows, teacher.reshape(rows, width), valid, out_bias, factor)
+    )(*loss_in)
 
     grads = lax.all_gather(
         low.reshape(tokens.shape), "ctx", axis=1, tiled=True
     ).reshape(all_rows, width)
-    order = jnp.stack([me_dp ^ k for k in range(n_dp)]).astype(jnp.int32)
     cut = (width // n_dp) % 128 == 0 and unit_rows % 128 == 0
 
     def blocks_of(rows_out, columns):
@@ -651,7 +676,9 @@
         return [(LOCAL, shape_of(block, BF16 if k else F32)) for k in range(n_dp)]
 
     back, gain_sum, shift_sum, up_bsum, qkv_bsum, *col_terms = kernel_call(
-        functools.partial(backward_kernel, first_len, heads, size, scale, length, STEP, cut),
+        functools.partial(
+            backward_kernel, first_len, heads, size, scale, length, STEP, cut, len(w_split)
+        ),
         "backward_kernel",
         [SCALAR, LOCAL] + [HBM] * (12 + len(w_split)),
         [

time: 297 us -> 295 us (level)
  waiting for transfers between devices: 136 us -> 132 us
    ppermute x6, waiting for transfers between devices: 6.09 us -> 1.6 us  [reduce_blocks(): lax.ppermute(terms[k], 'dp', [(i, i ^ k) for i in range(n_dp)])]
    ppermute x0 -> x3, starting transfers between devices: none -> 3.49 us  [body(): lax.ppermute(cols, 'dp', [(i, i ^ k) for i in range(n_dp)])]
    ppermute x6 -> x3, starting transfers between devices: 8.03 us -> 4.55 us  [gather_dp(): other = lax.ppermute(block, 'dp', pairs)]
    pallas_call x0 -> x1, Pallas kernels: none -> 3.01 us  [body(): kernel_call(output_kernel, 'output_kernel', [LOCAL] * 6, [(LOCAL, shape_o...]
    ppermute x6 -> x3, waiting for transfers between devices: 7.91 us -> 7.29 us  [gather_dp(): other = lax.ppermute(block, 'dp', pairs)]
  transfers between devices with their start and end apart: 25 -> 25, of which waited for: 9 -> 9; matrix products, arithmetic and copies ran while one was open for 12% -> 13% of each run, Pallas kernels for 4% -> 5%
where the time goes in v5:
time: 295 us; the launch traced here: 291 us
  waiting for transfers between devices  132 us (45%)
  Pallas kernels  66.3 us (22%)
  starting transfers between devices  34.4 us (12%)
  other arithmetic  21.3 us (7%)
  local copies, waits for them, and re-layouts  19.3 us (7%)
  between operations  17.6 us (6%)
    all_gather x1, waiting for transfers between devices, body(): lax.all_gather(low.reshape(tokens.shape), 'ctx', axis=1, tiled=True)  45.4 us
    reduce_scatter x1, waiting for transfers between devices, body(): lax.psum_scatter(terms.reshape(seqs, length, width), 'ctx', scatter_dimen...  43.6 us
    pallas_call x1, Pallas kernels, body(): kernel_call(functools.partial(backward_kernel, first_len, heads, size, sc...  26.9 us
    pallas_call x1, Pallas kernels, body(): kernel_call(functools.partial(forward_kernel, first_len, heads, size, sca...  20.1 us
    all_to_all x1, waiting for transfers between devices, body(): small = lax.all_to_all(small, both, 0, 0, tiled=True).astype(F32)  9.57 us
    ppermute x3, waiting for transfers between devices, reduce_dp(): total = total + lax.ppermute(block, 'dp', pairs).astype(F32)  8.69 us
    all_to_all x1, waiting for transfers between devices, body(): lax.all_to_all(cols, 'ctx', 0, 0, tiled=True)  8.45 us
    ppermute x3, waiting for transfers between devices, gather_dp(): other = lax.ppermute(block, 'dp', pairs)  7.29 us
  transfers between devices with their start and end apart: 25, of which 9 were waited for; matrix products, arithmetic and copies ran while one was open for 13% of the time, Pallas kernels for 5%

profile of v5, /device:TPU:0, one launch (start us, length us, event | category | flops | bytes accessed | tf_op | source)
XLA Modules:
  0.0 291.2 jit_solution(5789332716591333201)
XLA Ops:
  7.9 2.0 pack_columns.1
  9.9 1.0 pad_maximum_fusion
  10.9 3.0 %collective-permute-start = (bf16[160,1024]{1,0:T(8,128)(2,1)S(1)}, bf16[160,1024]{1,0:T(8,128)(2,1)}, u32[]{:S(2)}, u32[]{:S(2)}) collective-permute-start(bf16[160,1024]{1,0:T(8,128)(2,1)S(1)} %pad_maximum_fusion), channel_id=1, source_target_pairs={{0,8},{8,0},{16,24},{24,16},{1,9},{9,1},{17,25},{25,17},{2,10},{10... | collective-permute-start | bytes 983048 | tf_op jit(solution)/shard_map/ppermute | solution.py:471
  13.9 1.5 collective-permute-start.1
  15.4 5.3 %all-to-all-start = ((bf16[8,32,896]{2,1,0:T(8,128)(2,1)}), bf16[8,32,896]{2,1,0:T(8,128)(2,1)S(1)}, u32[]{:S(2)}, u32[]{:S(2)}) async-start(bf16[8,32,896]{2,1,0:T(8,128)(2,1)} %get-tuple-element.64), calls=%async_computation | async-start | bytes 917504 | tf_op jit(solution)/shard_map/all_to_all | solution.py:561
  22.5 1.0 bitcast_dynamic-update-slice_fusion.2
  23.5 6.7 %collective-permute-done.1 = bf16[160,1024]{1,0:T(8,128)(2,1)} collective-permute-done((bf16[160,1024]{1,0:T(8,128)(2,1)S(1)}, bf16[160,1024]{1,0:T(8,128)(2,1)}, u32[]{:S(2)}, u32[]{:S(2)}) %collective-permute-start.1) | collective-permute-done | bytes 327712 | tf_op jit(solution)/shard_map/ppermute | solution.py:471
  30.2 1.0 bitcast_dynamic-update-slice_fusion.1
  32.0 5.1 %compare_select_fusion.9 = (f32[128]{0:T(128)S(1)}, f32[128]{0:T(128)S(1)}) fusion(f32[]{:T(128)} %bitcast.16, f32[]{:T(128)} %bitcast.15, f32[]{:T(128)} %bitcast.14, f32[]{:T(128)} %bitcast.13, f32[]{:T(128)} %bitcast.12, f32[]{:T(128)} %bitcast.11, f32[]{:T(128)} %bitcast.10, f32[]{:T(128)} %bitcast.9), kind=kLoop, calls=%fused_computation.62 | loop fusion | flops 5632 | bytes 1056 | tf_op jit(solution)/shard_map/jit(_where)/select_n | solution.py:601
  37.1 1.0 slice.89
  38.2 0.7 copy.48
  38.9 8.4 %all-to-all-done = bf16[8,32,896]{2,1,0:T(8,128)(2,1)S(1)} async-done(((bf16[8,32,896]{2,1,0:T(8,128)(2,1)}), bf16[8,32,896]{2,1,0:T(8,128)(2,1)S(1)}, u32[]{:S(2)}, u32[]{:S(2)}) %all-to-all-start) | async-done | bytes 458784 | tf_op jit(solution)/shard_map/all_to_all | solution.py:561
  47.8 2.5 collective-permute-start.5
  50.8 3.2 %all-to-all-start.1 = ((bf16[32,8,128]{2,1,0:T(8,128)(2,1)}), bf16[32,8,128]{2,1,0:T(8,128)(2,1)S(1)}, u32[]{:S(2)}, u32[]{:S(2)}) async-start(bf16[32,8,128]{2,1,0:T(8,128)(2,1)} %get-tuple-element.66), calls=%async_computation.1 | async-start | bytes 131072 | tf_op jit(solution)/shard_map/all_to_all | solution.py:563
  54.1 2.2 convert_reduce_fusion
  56.4 5.8 %fusion = (f32[2048,128]{1,0:T(8,128)}, f32[2048,128]{1,0:T(8,128)}) fusion(f32[128]{0:T(128)S(1)} %get-tuple-element.138, f32[128]{0:T(128)S(1)} %get-tuple-element.139, f32[2048]{0:T(1024)S(1)} %bitcast.133), kind=kLoop, calls=%fused_computation.4 | loop fusion | flops 524288 | bytes 2106368 | tf_op jit(solution)/shard_map/mul | solution.py:601
  62.1 9.6 %all-to-all-done.1 = bf16[32,8,128]{2,1,0:T(8,128)(2,1)S(1)} async-done(((bf16[32,8,128]{2,1,0:T(8,128)(2,1)}), bf16[32,8,128]{2,1,0:T(8,128)(2,1)S(1)}, u32[]{:S(2)}, u32[]{:S(2)}) %all-to-all-start.1) | async-done | bytes 65568 | tf_op jit(solution)/shard_map/all_to_all | solution.py:563
  75.8 20.1 %forward_kernel.1 = (bf16[2048,1024]{1,0:T(8,128)(2,1)}, bf16[2048,128]{1,0:T(8,128)(2,1)}, bf16[2048,128]{1,0:T(8,128)(2,1)}, bf16[2048,128]{1,0:T(8,128)(2,1)}...) custom-call(s32[4]{0:T(128)} %pad_add_fusion.order, ...), custom_call_target="tpu_custom_call" | custom-call | flops 10000000000 | bytes 20000000 | tf_op jit(solution)/shard_map/forward_kernel/pallas_call | solution.py:625
  96.6 0.8 copy.49.valid
  100.1 43.6 %reduce-scatter.3.cloned.1.call-done = bf16[2,128,1024]{2,1,0:T(8,128)(2,1)} async-done(((bf16[2,1024,1024]{2,1,0:T(8,128)(2,1)}), bf16[2,128,1024]{2,1,0:T(8,128)(2,1)}) %reduce-scatter.3.cloned.1.call-update) | async-done | bytes 524304 | tf_op jit(solution)/shard_map/reduce_scatter | solution.py:644
  143.7 2.5 loss_kernel.1
  146.3 45.4 %all-gather.5.cloned.1.call-done = bf16[2,1024,1024]{2,1,0:T(8,128)(2,1)} async-done(((bf16[2,128,1024]{2,1,0:T(8,128)(2,1)}), bf16[2,1024,1024]{2,1,0:T(8,128)(2,1)}) %all-gather.5.cloned.1.call-update) | async-done | bytes 4194320 | tf_op jit(solution)/shard_map/all_gather | solution.py:667
  191.7 26.9 %backward_kernel.1 = (bf16[2048,1024]{1,0:T(8,128)(2,1)}, f32[1,1024]{1,0:T(1,128)}, f32[1,1024]{1,0:T(1,128)}, f32[1,512]{1,0:T(1,128)}, f32[1,384]{1,0:T(1,128...) custom-call(s32[4]{0:T(128)} %pad_add_fusion.order, ...), custom_call_target="tpu_custom_call" | custom-call | flops 12000000000 | bytes 20000000 | tf_op jit(solution)/shard_map/backward_kernel/pallas_call | solution.py:678
  218.7 0.9 copy-done.15
  219.6 1.5 collective-permute-start.7
  221.1 1.5 collective-permute-start.8
  223.1 0.8 copy.50.valid
  223.9 3.0 %output_kernel.1 = (bf16[256,1024]{1,0:T(8,128)(2,1)}, f32[256,1024]{1,0:T(8,128)}, f32[1,1024]{1,0:T(1,128)}, f32[1,1]{1,0:T(1,128)}) custom-call(bf16[256,1024]{1,0:T(8,128)(2,1)} %bitcast.112, bf16[256,1024]{1,0:T(8,128)(2,1)} %bitcast.103, bf16[256,1024]{1,0:T(8,128)(2,1)} %bitcast.110, f32[256,1]{1,0:T(8,128)} %copy.50.valid, f32[1,1024]{1,0:T(1,128)} %add.153.bias, ...), custom_call_target="tpu_custom_call" | custom-call | flops 1000000 | bytes 3000000 | tf_op jit(solution)/shard_map/output_kernel/pallas_call | solution.py:658
  227.4 1.3 reduce.30
  231.4 1.6 collective-permute-done.7
  233.0 6.8 %down_kernel.1 = (bf16[128,1024]{1,0:T(8,128)(2,1)}, f32[128,1024]{1,0:T(8,128)}, bf16[128,1024]{1,0:T(8,128)(2,1)}, bf16[128,1024]{1,0:T(8,128)(2,1)}, bf16[128,1024]{1,0:T(8,128)(2,1)}) custom-call(s32[4]{0:T(128)} %pad_add_fusion.order, bf16[2048,512]{1,0:T(8,128)(2,1)} %get-tuple-element.104.act, bf16[2048,128]{1,0:T(8,128)(2,1)} %get-tuple-element.105.mixed, ...), custom_call_target="tpu_custom_call" | custom-call | flops 1000000 | bytes 100000 | tf_op jit(solution)/shard_map/down_kernel/pallas_call | solution.py:742
  239.8 1.0 dynamic-slice_bitcast_fusion
  241.6 3.4 %all-to-all-start.2 = ((f32[32,1,384]{2,1,0:T(1,128)}), f32[32,1,384]{2,1,0:T(1,128)S(1)}, u32[]{:S(2)}, u32[]{:S(2)}) async-start(f32[32,1,384]{2,1,0:T(1,128)} %copy.53), calls=%async_computation.3 | async-start | bytes 98304 | tf_op jit(solution)/shard_map/all_to_all | solution.py:729
  245.0 1.0 add_convert_fusion
  246.0 6.9 %all-to-all-done.2 = f32[32,1,384]{2,1,0:T(1,128)S(1)} async-done(((f32[32,1,384]{2,1,0:T(1,128)}), f32[32,1,384]{2,1,0:T(1,128)S(1)}, u32[]{:S(2)}, u32[]{:S(2)}) %all-to-all-start.2) | async-done | bytes 49184 | tf_op jit(solution)/shard_map/all_to_all | solution.py:729
  252.9 3.5 %all-to-all-start.3 = ((bf16[8,32,896]{2,1,0:T(8,128)(2,1)}), bf16[8,32,896]{2,1,0:T(8,128)(2,1)S(1)}, u32[]{:S(2)}, u32[]{:S(2)}) async-start(bf16[8,32,896]{2,1,0:T(8,128)(2,1)} %bitcast.49), calls=%async_computation.5 | async-start | bytes 917504 | tf_op jit(solution)/shard_map/all_to_all | solution.py:731
  256.6 1.0 collective-permute-start.11
  257.6 1.1 collective-permute-start.14
  258.7 0.9 collective-permute-start.15
  259.6 1.4 collective-permute-start.16
  261.1 0.8 collective-permute-start.12
  261.9 1.9 collective-permute-start.13
  266.7 8.7 %collective-permute-done.12 = bf16[32,1024]{1,0:T(8,128)(2,1)S(1)} collective-permute-done((bf16[32,1024]{1,0:T(8,128)(2,1)S(1)}, bf16[32,1024]{1,0:T(8,128)(2,1)S(1)}, u32[]{:S(2)}, u32[]{:S(2)}) %collective-permute-start.12) | collective-permute-done | bytes 65568 | tf_op jit(solution)/shard_map/ppermute | solution.py:497
  275.4 0.7 fusion.2
  276.1 0.9 convert_add_fusion
  277.0 0.8 copy-done
  277.8 2.0 unpack_columns.1
  279.8 3.0 %norm_back_kernel.1 = bf16[256,1024]{1,0:T(8,128)(2,1)} custom-call(bf16[256,1024]{1,0:T(8,128)(2,1)} %bitcast.118, bf16[256,1024]{1,0:T(8,128)(2,1)} %bitcast.104, f32[256,1024]{1,0:T(8,128)} %get-tuple-element.101.og, f32[1,1024]{1,0:T(1,128)} %reshape_squeeze.15.gain), custom_call_target="tpu_custom_call" | custom-call | flops 1000000 | bytes 3000000 | tf_op jit(solution)/shard_map/norm_back_kernel/pallas_call | solution.py:762
  (114 shorter events, 17.8 us)
Async XLA Ops:
  7.2 67.5 %all-gather.3.cloned.1.call-start = ((), (), s32[]{:S(2)}) async-start(), calls=%async_computation.6 | async-start | bytes 4718592 | tf_op jit(solution)/shard_map/all_gather | solution.py:560
  10.9 11.6 %collective-permute-start = (bf16[160,1024]{1,0:T(8,128)(2,1)S(1)}, bf16[160,1024]{1,0:T(8,128)(2,1)}, u32[]{:S(2)}, u32[]{:S(2)}) collective-permute-start(bf16[160,1024]{1,0:T(8,128)(2,1)S(1)} %pad_maximum_fusion), channel_id=1, source_target_pairs={{0,8},{8,0},{16,24},{24,16},{1,9},{9,1},{17,25},{25,17},{2,10},{10... | collective-permute-start | bytes 983048 | tf_op jit(solution)/shard_map/ppermute | solution.py:471
  13.9 16.3 %collective-permute-start.1 = (bf16[160,1024]{1,0:T(8,128)(2,1)S(1)}, bf16[160,1024]{1,0:T(8,128)(2,1)}, u32[]{:S(2)}, u32[]{:S(2)}) collective-permute-start(bf16[160,1024]{1,0:T(8,128)(2,1)S(1)} %pad_maximum_fusion), channel_id=1, source_target_pairs={{0,16},{8,24},{16,0},{24,8},{1,17},{9,25},{17,1},{25,9},{2,18},{10... | collective-permute-start | bytes 983048 | tf_op jit(solution)/shard_map/ppermute | solution.py:471
  15.4 15.8 %collective-permute-start.2 = (bf16[160,1024]{1,0:T(8,128)(2,1)S(1)}, bf16[160,1024]{1,0:T(8,128)(2,1)S(1)}, u32[]{:S(2)}, u32[]{:S(2)}) collective-permute-start(bf16[160,1024]{1,0:T(8,128)(2,1)S(1)} %pad_maximum_fusion), channel_id=1, source_target_pairs={{0,24},{8,16},{16,8},{24,0},{1,25},{9,17},{17,9},{25,1},{2,26},{10... | collective-permute-start | bytes 983048 | tf_op jit(solution)/shard_map/ppermute | solution.py:471
  15.4 31.9 %all-to-all-start = ((bf16[8,32,896]{2,1,0:T(8,128)(2,1)}), bf16[8,32,896]{2,1,0:T(8,128)(2,1)S(1)}, u32[]{:S(2)}, u32[]{:S(2)}) async-start(bf16[8,32,896]{2,1,0:T(8,128)(2,1)} %get-tuple-element.64), calls=%async_computation | async-start | bytes 917504 | tf_op jit(solution)/shard_map/all_to_all | solution.py:561
  31.3 22.9 %copy-start.5 = (s32[2,1024]{1,0:T(2,128)S(1)}, s32[2,1024]{1,0:T(2,128)}, u32[]{:S(2)}) copy-start(s32[2,1024]{1,0:T(2,128)} %seg_row.1) | copy-start | bytes 24580
  31.3 6.8 %collective-permute-start.3 = (bf16[2,32,1024]{2,1,0:T(8,128)(2,1)S(1)}, bf16[2,32,1024]{2,1,0:T(8,128)(2,1)S(1)}, u32[]{:S(2)}, u32[]{:S(2)}) collective-permute-start(bf16[2,32,1024]{2,1,0:T(8,128)(2,1)S(1)} %dynamic-slice_bitcast_fusion.1), channel_id=1, source_target_pairs={{0,1},{1,0},{2,3},{3,2},{4,5},{5,4},{6,7},{7,6},{8,9},{9,8},{10,11... | collective-permute-start | bytes 393224 | tf_op jit(solution)/shard_map/ppermute | solution.py:608
  47.4 27.4 %copy-start.3 = (bf16[8,32,896]{2,1,0:T(8,128)(2,1)}, bf16[8,32,896]{2,1,0:T(8,128)(2,1)S(1)}, u32[]{:S(2)}) copy-start(bf16[8,32,896]{2,1,0:T(8,128)(2,1)S(1)} %all-to-all-done) | copy-start | bytes 1376260
  47.4 27.3 %collective-permute-start.4 = (bf16[256,896]{1,0:T(8,128)(2,1)S(1)}, bf16[256,896]{1,0:T(8,128)(2,1)S(1)}, u32[]{:S(2)}, u32[]{:S(2)}) collective-permute-start(bf16[256,896]{1,0:T(8,128)(2,1)S(1)} %bitcast.120), channel_id=1, source_target_pairs={{0,8},{8,0},{16,24},{24,16},{1,9},{9,1},{17,25},{25,17},{2,10},{10... | collective-permute-start | bytes 1376264 | tf_op jit(solution)/shard_map/ppermute | solution.py:583
  47.8 26.8 %collective-permute-start.5 = (bf16[256,896]{1,0:T(8,128)(2,1)S(1)}, bf16[256,896]{1,0:T(8,128)(2,1)S(1)}, u32[]{:S(2)}, u32[]{:S(2)}) collective-permute-start(bf16[256,896]{1,0:T(8,128)(2,1)S(1)} %bitcast.121), channel_id=1, source_target_pairs={{0,16},{8,24},{16,0},{24,8},{1,17},{9,25},{17,1},{25,9},{2,18},{10... | collective-permute-start | bytes 1376264 | tf_op jit(solution)/shard_map/ppermute | solution.py:583
  50.3 24.4 %collective-permute-start.6 = (bf16[256,896]{1,0:T(8,128)(2,1)S(1)}, bf16[256,896]{1,0:T(8,128)(2,1)S(1)}, u32[]{:S(2)}, u32[]{:S(2)}) collective-permute-start(bf16[256,896]{1,0:T(8,128)(2,1)S(1)} %bitcast.122), channel_id=1, source_target_pairs={{0,24},{8,16},{16,8},{24,0},{1,25},{9,17},{17,9},{25,1},{2,26},{10... | collective-permute-start | bytes 1376264 | tf_op jit(solution)/shard_map/ppermute | solution.py:583
  50.8 20.9 %all-to-all-start.1 = ((bf16[32,8,128]{2,1,0:T(8,128)(2,1)}), bf16[32,8,128]{2,1,0:T(8,128)(2,1)S(1)}, u32[]{:S(2)}, u32[]{:S(2)}) async-start(bf16[32,8,128]{2,1,0:T(8,128)(2,1)} %get-tuple-element.66), calls=%async_computation.1 | async-start | bytes 131072 | tf_op jit(solution)/shard_map/all_to_all | solution.py:563
  54.1 89.6 %reduce-scatter.3.cloned.1.call-start = ((), (), s32[]{:S(2)}) async-start(), calls=%async_computation.7 | async-start | bytes 4718592 | tf_op jit(solution)/shard_map/reduce_scatter | solution.py:644
  74.7 0.8 copy-start.12
  74.7 0.9 copy-start.13
  74.7 1.1 copy-start.14
  95.9 0.7 copy-start.6
  95.9 95.8 %all-gather.5.cloned.1.call-start = ((), (), s32[]{:S(2)}) async-start(), calls=%async_computation.8 | async-start | bytes 4718592 | tf_op jit(solution)/shard_map/all_gather | solution.py:667
  146.3 133.5 %reduce-scatter.5.cloned.1.call-start = ((), (), s32[]{:S(2)}) async-start(), calls=%async_computation.9 | async-start | bytes 4718592 | tf_op jit(solution)/shard_map/reduce_scatter | solution.py:700
  218.6 1.0 copy-start.15
  218.6 10.2 %copy-start.10 = (f32[1,384]{1,0:T(1,128)S(1)}, f32[1,384]{1,0:T(1,128)}, u32[]{:S(2)}) copy-start(f32[1,384]{1,0:T(1,128)} %get-tuple-element.94) | copy-start | bytes 4612
  218.6 10.5 %copy-start.8 = (f32[1,1024]{1,0:T(1,128)S(1)}, f32[1,1024]{1,0:T(1,128)}, u32[]{:S(2)}) copy-start(f32[1,1024]{1,0:T(1,128)} %get-tuple-element.91) | copy-start | bytes 12292
  218.6 11.2 %copy-start.7 = (f32[1,1024]{1,0:T(1,128)S(1)}, f32[1,1024]{1,0:T(1,128)}, u32[]{:S(2)}) copy-start(f32[1,1024]{1,0:T(1,128)} %get-tuple-element.92) | copy-start | bytes 12292
  218.6 12.0 %copy-start.9 = (f32[1,512]{1,0:T(1,128)S(1)}, f32[1,512]{1,0:T(1,128)}, u32[]{:S(2)}) copy-start(f32[1,512]{1,0:T(1,128)} %get-tuple-element.95) | copy-start | bytes 6148
  219.6 13.3 %collective-permute-start.7 = (bf16[256,896]{1,0:T(8,128)(2,1)S(1)}, bf16[256,896]{1,0:T(8,128)(2,1)S(1)}, u32[]{:S(2)}, u32[]{:S(2)}) collective-permute-start(bf16[256,896]{1,0:T(8,128)(2,1)S(1)} %copy-done.15), channel_id=1, source_target_pairs={{0,8},{8,0},{16,24},{24,16},{1,9},{9,1},{17,25},{25,17},{2,10},{10... | collective-permute-start | bytes 1376264 | tf_op jit(solution)/shard_map/ppermute | solution.py:480
  221.1 23.9 %collective-permute-start.8 = (bf16[256,896]{1,0:T(8,128)(2,1)}, bf16[256,896]{1,0:T(8,128)(2,1)S(1)}, u32[]{:S(2)}, u32[]{:S(2)}) collective-permute-start(bf16[256,896]{1,0:T(8,128)(2,1)} %get-tuple-element.89), channel_id=1, source_target_pairs={{0,16},{8,24},{16,0},{24,8},{1,17},{9,25},{17,1},{25,9},{2,18},{10... | collective-permute-start | bytes 1376264 | tf_op jit(solution)/shard_map/ppermute | solution.py:480
  222.6 22.4 %collective-permute-start.9 = (bf16[256,896]{1,0:T(8,128)(2,1)}, bf16[256,896]{1,0:T(8,128)(2,1)S(1)}, u32[]{:S(2)}, u32[]{:S(2)}) collective-permute-start(bf16[256,896]{1,0:T(8,128)(2,1)} %get-tuple-element.90), channel_id=1, source_target_pairs={{0,24},{8,16},{16,8},{24,0},{1,25},{9,17},{17,9},{25,1},{2,26},{10... | collective-permute-start | bytes 1376264 | tf_op jit(solution)/shard_map/ppermute | solution.py:480
  233.0 12.0 %copy-start.1 = (f32[256,896]{1,0:T(8,128)S(1)}, f32[256,896]{1,0:T(8,128)}, u32[]{:S(2)}) copy-start(f32[256,896]{1,0:T(8,128)} %get-tuple-element.85) | copy-start | bytes 2752516
  239.8 16.6 %copy-start.4 = (bf16[128,1024]{1,0:T(8,128)(2,1)S(1)}, bf16[128,1024]{1,0:T(8,128)(2,1)}, u32[]{:S(2)}) copy-start(bf16[128,1024]{1,0:T(8,128)(2,1)} %get-tuple-element.106) | copy-start | bytes 786436
  240.8 15.6 %collective-permute-start.10 = (bf16[2,32,1024]{2,1,0:T(8,128)(2,1)S(1)}, bf16[2,32,1024]{2,1,0:T(8,128)(2,1)S(1)}, u32[]{:S(2)}, u32[]{:S(2)}) collective-permute-start(bf16[2,32,1024]{2,1,0:T(8,128)(2,1)S(1)} %dynamic-slice_bitcast_fusion), channel_id=1, source_target_pairs={{0,1},{1,0},{2,3},{3,2},{4,5},{5,4},{6,7},{7,6},{8,9},{9,8},{10,11... | collective-permute-start | bytes 393224 | tf_op jit(solution)/shard_map/ppermute | solution.py:751
  241.6 11.4 %all-to-all-start.2 = ((f32[32,1,384]{2,1,0:T(1,128)}), f32[32,1,384]{2,1,0:T(1,128)S(1)}, u32[]{:S(2)}, u32[]{:S(2)}) async-start(f32[32,1,384]{2,1,0:T(1,128)} %copy.53), calls=%async_computation.3 | async-start | bytes 98304 | tf_op jit(solution)/shard_map/all_to_all | solution.py:729
  245.0 31.1 %copy-start.2 = (f32[128,1024]{1,0:T(8,128)S(1)}, f32[128,1024]{1,0:T(8,128)}, u32[]{:S(2)}) copy-start(f32[128,1024]{1,0:T(8,128)} %get-tuple-element.108) | copy-start | bytes 1572868
  252.9 24.1 %all-to-all-start.3 = ((bf16[8,32,896]{2,1,0:T(8,128)(2,1)}), bf16[8,32,896]{2,1,0:T(8,128)(2,1)S(1)}, u32[]{:S(2)}, u32[]{:S(2)}) async-start(bf16[8,32,896]{2,1,0:T(8,128)(2,1)} %bitcast.49), calls=%async_computation.5 | async-start | bytes 917504 | tf_op jit(solution)/shard_map/all_to_all | solution.py:731
  256.6 5.3 %collective-permute-start.11 = (bf16[32,1024]{1,0:T(8,128)(2,1)S(1)}, bf16[32,1024]{1,0:T(8,128)(2,1)S(1)}, u32[]{:S(2)}, u32[]{:S(2)}) collective-permute-start(bf16[32,1024]{1,0:T(8,128)(2,1)S(1)} %get-tuple-element.121), channel_id=1, source_target_pairs={{0,8},{8,0},{16,24},{24,16},{1,9},{9,1},{17,25},{25,17},{2,10},{10... | collective-permute-start | bytes 196616 | tf_op jit(solution)/shard_map/ppermute | solution.py:497
  257.6 18.5 %collective-permute-start.14 = (bf16[128,1024]{1,0:T(8,128)(2,1)}, bf16[128,1024]{1,0:T(8,128)(2,1)S(1)}, u32[]{:S(2)}, u32[]{:S(2)}) collective-permute-start(bf16[128,1024]{1,0:T(8,128)(2,1)} %get-tuple-element.109), channel_id=1, source_target_pairs={{0,8},{8,0},{16,24},{24,16},{1,9},{9,1},{17,25},{25,17},{2,10},{10... | collective-permute-start | bytes 786440 | tf_op jit(solution)/shard_map/ppermute | solution.py:480
  258.7 17.4 %collective-permute-start.15 = (bf16[128,1024]{1,0:T(8,128)(2,1)}, bf16[128,1024]{1,0:T(8,128)(2,1)S(1)}, u32[]{:S(2)}, u32[]{:S(2)}) collective-permute-start(bf16[128,1024]{1,0:T(8,128)(2,1)} %get-tuple-element.110), channel_id=1, source_target_pairs={{0,16},{8,24},{16,0},{24,8},{1,17},{9,25},{17,1},{25,9},{2,18},{10... | collective-permute-start | bytes 786440 | tf_op jit(solution)/shard_map/ppermute | solution.py:480
  259.6 16.5 %collective-permute-start.16 = (bf16[128,1024]{1,0:T(8,128)(2,1)}, bf16[128,1024]{1,0:T(8,128)(2,1)S(1)}, u32[]{:S(2)}, u32[]{:S(2)}) collective-permute-start(bf16[128,1024]{1,0:T(8,128)(2,1)} %get-tuple-element.111), channel_id=1, source_target_pairs={{0,24},{8,16},{16,8},{24,0},{1,25},{9,17},{17,9},{25,1},{2,26},{10... | collective-permute-start | bytes 786440 | tf_op jit(solution)/shard_map/ppermute | solution.py:480
  261.1 14.3 %collective-permute-start.12 = (bf16[32,1024]{1,0:T(8,128)(2,1)S(1)}, bf16[32,1024]{1,0:T(8,128)(2,1)S(1)}, u32[]{:S(2)}, u32[]{:S(2)}) collective-permute-start(bf16[32,1024]{1,0:T(8,128)(2,1)S(1)} %get-tuple-element.122), channel_id=1, source_target_pairs={{0,16},{8,24},{16,0},{24,8},{1,17},{9,25},{17,1},{25,9},{2,18},{10... | collective-permute-start | bytes 196616 | tf_op jit(solution)/shard_map/ppermute | solution.py:497
  261.9 13.5 %collective-permute-start.13 = (bf16[32,1024]{1,0:T(8,128)(2,1)S(1)}, bf16[32,1024]{1,0:T(8,128)(2,1)S(1)}, u32[]{:S(2)}, u32[]{:S(2)}) collective-permute-start(bf16[32,1024]{1,0:T(8,128)(2,1)S(1)} %get-tuple-element.123), channel_id=1, source_target_pairs={{0,24},{8,16},{16,8},{24,0},{1,25},{9,17},{17,9},{25,1},{2,26},{10... | collective-permute-start | bytes 196616 | tf_op jit(solution)/shard_map/ppermute | solution.py:497
  264.3 18.5 %copy-start.11 = (f32[32]{0:T(128)}, f32[32]{0:T(128)S(1)}, u32[]{:S(2)}) copy-start(f32[32]{0:T(128)S(1)} %get-tuple-element.167) | copy-start | bytes 388
  277.0 0.8 copy-start
Sparse Core Ops, SparseCore 0:
  9.6 60.9 all-gather.2
  96.0 47.6 reduce-scatter.2
  146.4 45.2 all-gather.4
  218.8 55.0 reduce-scatter.4

commit v6 on v5

--- a/solution.py
+++ b/solution.py
@@ -409,6 +409,28 @@
             ]
 
 
+def vector_kernel(own, heads, size, n_dp, n_ctx, place, small, gain, shift, qkv_b, up_b, full):
+    rows = [small[d].astype(F32) for d in range(n_dp * n_ctx)]
+    gain[...] = jnp.concatenate([row[0:1, :own] for row in rows], axis=1)
+    shift[...] = jnp.concatenate([row[1:2, :own] for row in rows], axis=1)
+    full[...] = jnp.concatenate([row[4:5, : 3 * own] for row in rows], axis=1)
+    core, chip = place[0], place[1]
+    part, third = heads * size, full.shape[1] // 3
+    for p in range(3):
+        pairs = []
+        for h in range(heads):
+            head = (heads * core + h) * (n_ctx // 2) + chip
+            at = pl.multiple_of(p * third + (head // 2) * 2 * size, 2 * size)
+            pairs.append(full[:, pl.ds(at, 2 * size)])
+        low = jnp.concatenate([pair[:, :size] for pair in pairs], axis=1)
+        high = jnp.concatenate([pair[:, size:] for pair in pairs], axis=1)
+        qkv_b[:, p * part : (p + 1) * part] = jnp.where(lax.rem(chip, 2) == 0, low, high)
+    me = 2 * chip + core
+    block = up_b.shape[1] // n_dp
+    for i in range(n_dp):
+        up_b[:, i * block : (i + 1) * block] = small[i * n_ctx + me].astype(F32)[5:6, :block]
+
+
 def unpack_columns(heads, size, paired, units, n_dp, n_ctx, in_ref, qkv_ref, up_ref):
     part = heads * size
     width, unit_rows = n_ctx * part, units // n_dp
@@ -496,6 +518,26 @@
         block = lax.dynamic_index_in_dim(blocks, me_dp ^ k, 0, keepdims=False)
         total = total + lax.ppermute(block, "dp", pairs).astype(F32)
     return total
+
+
+def own_vectors(
+    small, own, part, units, unit_rows, n_dp, n_ctx, me_ctx, paired, heads, size, me_core, me_chip
+):
+    width = n_dp * n_ctx * own
+    gain = small[:, 0, :own].reshape(1, width)
+    shift = small[:, 1, :own].reshape(1, width)
+    qkv_b = small[:, 4, : 3 * own]
+    if paired:
+        qkv_b = lax.dynamic_slice(
+            qkv_b.reshape(3, 2, heads, n_ctx // 2, size), (0, me_core, 0, me_chip, 0),
+            (3, 1, heads, 1, size),
+        )
+    else:
+        qkv_b = lax.dynamic_index_in_dim(qkv_b.reshape(3, n_ctx, part), me_ctx, 1)
+    qkv_b = qkv_b.reshape(1, 3 * part)
+    up_b = small[:, 5, :unit_rows].reshape(n_dp, n_ctx, unit_rows)
+    up_b = lax.dynamic_index_in_dim(up_b, me_ctx, 1, keepdims=False).reshape(1, units)
+    return gain, shift, qkv_b, up_b
 
 
 def body(
@@ -560,21 +602,21 @@
     x_rows = lax.all_gather(tokens, "ctx", axis=1, tiled=True).reshape(all_rows, width)
     cols = lax.all_to_all(cols, "ctx", 0, 0, tiled=True).reshape(n_ctx * own, total_cols)
     cols, segments, small = lax.optimization_barrier((cols, segments, small))
-    small = lax.all_to_all(small, both, 0, 0, tiled=True).astype(F32)
-    gain = small[:, 0, :own].reshape(1, width)
-    shift = small[:, 1, :own].reshape(1, width)
+    small = lax.all_to_all(small, both, 0, 0, tiled=True)
+    if paired and 2 * size == 128 and (n_ctx // 2) % 2 == 0:
+        gain, shift, qkv_b, up_b = kernel_call(
+            functools.partial(vector_kernel, own, heads, size, n_dp, n_ctx), "vector_kernel",
+            [SCALAR, LOCAL],
+            [(LOCAL, shape_of((1, a), F32)) for a in (width, width, 3 * part, units)],
+            [pltpu.VMEM((1, 3 * width), F32)], flops=10**6, moved=10**5,
+        )(jnp.stack([me_core, me_chip]).astype(jnp.int32), small)
+    else:
+        gain, shift, qkv_b, up_b = own_vectors(
+            small.astype(F32), own, part, units, unit_rows, n_dp, n_ctx, me_ctx, paired, heads,
+            size, me_core, me_chip,
+        )
+    small = small.astype(F32)
     out_bias = (small[:, 2, :own] + small[:, 3, :own]).reshape(1, width)
-    qkv_b = small[:, 4, : 3 * own]
-    if paired:
-        qkv_b = lax.dynamic_slice(
-            qkv_b.reshape(3, 2, heads, n_ctx // 2, size), (0, me_core, 0, me_chip, 0),
-            (3, 1, heads, 1, size),
-        )
-    else:
-        qkv_b = lax.dynamic_index_in_dim(qkv_b.reshape(3, n_ctx, part), me_ctx, 1)
-    qkv_b = qkv_b.reshape(1, 3 * part)
-    up_b = small[:, 5, :unit_rows].reshape(n_dp, n_ctx, unit_rows)
-    up_b = lax.dynamic_index_in_dim(up_b, me_ctx, 1, keepdims=False).reshape(1, units)
     valid_count = 128.0 * jnp.sum(small[:, 6, 0]) + jnp.sum(small[:, 7, 0])
     sliced = (3 * part) % 128 == 0 and units % 128 == 0
     order = jnp.stack([me_dp ^ k for k in range(n_dp)]).astype(jnp.int32)

time: 295 us -> 295 us (level)
  transfers between devices with their start and end apart: 25 -> 25, of which waited for: 9 -> 8; matrix products, arithmetic and copies ran while one was open for 13% -> 12% of each run, Pallas kernels for 5% -> 5%
where the time goes in v6:
time: 295 us; the launch traced here: 290 us
  waiting for transfers between devices  132 us (45%)
  Pallas kernels  67.9 us (23%)
  starting transfers between devices  34.4 us (12%)
  other arithmetic  21.8 us (7%)
  between operations  17.6 us (6%)
  local copies, waits for them, and re-layouts  17.1 us (6%)
    all_gather x1, waiting for transfers between devices, body(): lax.all_gather(low.reshape(tokens.shape), 'ctx', axis=1, tiled=True)  45.4 us
    reduce_scatter x1, waiting for transfers between devices, body(): lax.psum_scatter(terms.reshape(seqs, length, width), 'ctx', scatter_dimen...  43.6 us
    pallas_call x1, Pallas kernels, body(): kernel_call(functools.partial(backward_kernel, first_len, heads, size, sc...  26.9 us
    pallas_call x1, Pallas kernels, body(): kernel_call(functools.partial(forward_kernel, first_len, heads, size, sca...  20.1 us
    all_to_all x1, waiting for transfers between devices, body(): small = lax.all_to_all(small, both, 0, 0, tiled=True)  9.61 us
    ppermute x3, waiting for transfers between devices, reduce_dp(): total = total + lax.ppermute(block, 'dp', pairs).astype(F32)  8.69 us
    all_to_all x1, waiting for transfers between devices, body(): lax.all_to_all(cols, 'ctx', 0, 0, tiled=True)  8.47 us
    ppermute x6, starting transfers between devices, reduce_blocks(): lax.ppermute(terms[k], 'dp', [(i, i ^ k) for i in range(n_dp)])  6.98 us
  transfers between devices with their start and end apart: 25, of which 8 were waited for; matrix products, arithmetic and copies ran while one was open for 12% of the time, Pallas kernels for 5%

profile of v6, /device:TPU:0, one launch (start us, length us, event | category | flops | bytes accessed | tf_op | source)
XLA Modules:
  0.0 290.5 jit_solution(2724855782947438981)
XLA Ops:
  7.9 2.0 pack_columns.1
  9.9 1.0 pad_maximum_fusion
  10.9 3.0 %collective-permute-start = (bf16[160,1024]{1,0:T(8,128)(2,1)S(1)}, bf16[160,1024]{1,0:T(8,128)(2,1)}, u32[]{:S(2)}, u32[]{:S(2)}) collective-permute-start(bf16[160,1024]{1,0:T(8,128)(2,1)S(1)} %pad_maximum_fusion), channel_id=1, source_target_pairs={{0,8},{8,0},{16,24},{24,16},{1,9},{9,1},{17,25},{25,17},{2,10},{10... | collective-permute-start | bytes 983048 | tf_op jit(solution)/shard_map/ppermute | solution.py:493
  13.9 1.5 collective-permute-start.1
  15.4 5.3 %all-to-all-start = ((bf16[8,32,896]{2,1,0:T(8,128)(2,1)}), bf16[8,32,896]{2,1,0:T(8,128)(2,1)S(1)}, u32[]{:S(2)}, u32[]{:S(2)}) async-start(bf16[8,32,896]{2,1,0:T(8,128)(2,1)} %get-tuple-element.68), calls=%async_computation | async-start | bytes 917504 | tf_op jit(solution)/shard_map/all_to_all | solution.py:603
  22.6 1.0 bitcast_dynamic-update-slice_fusion.2
  23.6 6.6 %collective-permute-done.1 = bf16[160,1024]{1,0:T(8,128)(2,1)} collective-permute-done((bf16[160,1024]{1,0:T(8,128)(2,1)S(1)}, bf16[160,1024]{1,0:T(8,128)(2,1)}, u32[]{:S(2)}, u32[]{:S(2)}) %collective-permute-start.1) | collective-permute-done | bytes 327712 | tf_op jit(solution)/shard_map/ppermute | solution.py:493
  30.2 1.0 bitcast_dynamic-update-slice_fusion.1
  32.0 5.1 %compare_select_fusion.9 = (f32[128]{0:T(128)S(1)}, f32[128]{0:T(128)S(1)}) fusion(f32[]{:T(128)} %bitcast.16, f32[]{:T(128)} %bitcast.15, f32[]{:T(128)} %bitcast.14, f32[]{:T(128)} %bitcast.13, f32[]{:T(128)} %bitcast.12, f32[]{:T(128)} %bitcast.11, f32[]{:T(128)} %bitcast.10, f32[]{:T(128)} %bitcast.9), kind=kLoop, calls=%fused_computation.56 | loop fusion | flops 5632 | bytes 1056 | tf_op jit(solution)/shard_map/jit(_where)/select_n | solution.py:643
  37.1 1.0 slice.69
  38.2 0.7 copy.40
  38.9 8.5 %all-to-all-done = bf16[8,32,896]{2,1,0:T(8,128)(2,1)S(1)} async-done(((bf16[8,32,896]{2,1,0:T(8,128)(2,1)}), bf16[8,32,896]{2,1,0:T(8,128)(2,1)S(1)}, u32[]{:S(2)}, u32[]{:S(2)}) %all-to-all-start) | async-done | bytes 458784 | tf_op jit(solution)/shard_map/all_to_all | solution.py:603
  47.8 2.5 collective-permute-start.5
  50.8 3.2 %all-to-all-start.1 = ((bf16[32,8,128]{2,1,0:T(8,128)(2,1)}), bf16[32,8,128]{2,1,0:T(8,128)(2,1)S(1)}, u32[]{:S(2)}, u32[]{:S(2)}) async-start(bf16[32,8,128]{2,1,0:T(8,128)(2,1)} %get-tuple-element.70), calls=%async_computation.1 | async-start | bytes 131072 | tf_op jit(solution)/shard_map/all_to_all | solution.py:605
  54.1 2.2 convert_reduce_fusion
  56.4 5.7 %fusion = (f32[2048,128]{1,0:T(8,128)}, f32[2048,128]{1,0:T(8,128)}) fusion(f32[128]{0:T(128)S(1)} %get-tuple-element.143, f32[128]{0:T(128)S(1)} %get-tuple-element.144, f32[2048]{0:T(1024)S(1)} %bitcast.127), kind=kLoop, calls=%fused_computation.4 | loop fusion | flops 524288 | bytes 2106368 | tf_op jit(solution)/shard_map/mul | solution.py:643
  62.1 9.6 %all-to-all-done.1.small = bf16[32,8,128]{2,1,0:T(8,128)(2,1)S(1)} async-done(((bf16[32,8,128]{2,1,0:T(8,128)(2,1)}), bf16[32,8,128]{2,1,0:T(8,128)(2,1)S(1)}, u32[]{:S(2)}, u32[]{:S(2)}) %all-to-all-start.1) | async-done | bytes 65568 | tf_op jit(solution)/shard_map/all_to_all | solution.py:605
  72.3 1.6 vector_kernel.1
  75.1 20.1 %forward_kernel.1 = (bf16[2048,1024]{1,0:T(8,128)(2,1)}, bf16[2048,128]{1,0:T(8,128)(2,1)}, bf16[2048,128]{1,0:T(8,128)(2,1)}, bf16[2048,128]{1,0:T(8,128)(2,1)}...) custom-call(s32[4]{0:T(128)} %pad_add_fusion.order, ...), custom_call_target="tpu_custom_call" | custom-call | flops 10000000000 | bytes 20000000 | tf_op jit(solution)/shard_map/forward_kernel/pallas_call | solution.py:667
  95.8 0.8 copy.41.valid
  99.4 43.6 %reduce-scatter.3.cloned.1.call-done = bf16[2,128,1024]{2,1,0:T(8,128)(2,1)} async-done(((bf16[2,1024,1024]{2,1,0:T(8,128)(2,1)}), bf16[2,128,1024]{2,1,0:T(8,128)(2,1)}) %reduce-scatter.3.cloned.1.call-update) | async-done | bytes 524304 | tf_op jit(solution)/shard_map/reduce_scatter | solution.py:686
  143.0 2.5 loss_kernel.1
  145.6 45.4 %all-gather.5.cloned.1.call-done = bf16[2,1024,1024]{2,1,0:T(8,128)(2,1)} async-done(((bf16[2,128,1024]{2,1,0:T(8,128)(2,1)}), bf16[2,1024,1024]{2,1,0:T(8,128)(2,1)}) %all-gather.5.cloned.1.call-update) | async-done | bytes 4194320 | tf_op jit(solution)/shard_map/all_gather | solution.py:709
  191.0 26.9 %backward_kernel.1 = (bf16[2048,1024]{1,0:T(8,128)(2,1)}, f32[1,1024]{1,0:T(1,128)}, f32[1,1024]{1,0:T(1,128)}, f32[1,512]{1,0:T(1,128)}, f32[1,384]{1,0:T(1,128...) custom-call(s32[4]{0:T(128)} %pad_add_fusion.order, ...), custom_call_target="tpu_custom_call" | custom-call | flops 12000000000 | bytes 20000000 | tf_op jit(solution)/shard_map/backward_kernel/pallas_call | solution.py:720
  218.0 0.9 copy-done.17
  218.9 1.5 collective-permute-start.7
  220.4 1.5 collective-permute-start.8
  222.4 0.8 copy.42.valid
  223.2 3.0 %output_kernel.1 = (bf16[256,1024]{1,0:T(8,128)(2,1)}, f32[256,1024]{1,0:T(8,128)}, f32[1,1024]{1,0:T(1,128)}, f32[1,1]{1,0:T(1,128)}) custom-call(bf16[256,1024]{1,0:T(8,128)(2,1)} %bitcast.106, bf16[256,1024]{1,0:T(8,128)(2,1)} %bitcast.97, bf16[256,1024]{1,0:T(8,128)(2,1)} %bitcast.104, f32[256,1]{1,0:T(8,128)} %copy.42.valid, f32[1,1024]{1,0:T(1,128)} %add.147.bias, ...), custom_call_target="tpu_custom_call" | custom-call | flops 1000000 | bytes 3000000 | tf_op jit(solution)/shard_map/output_kernel/pallas_call | solution.py:700
  226.7 1.3 reduce.18
  230.7 1.6 collective-permute-done.7
  232.3 6.8 %down_kernel.1 = (bf16[128,1024]{1,0:T(8,128)(2,1)}, f32[128,1024]{1,0:T(8,128)}, bf16[128,1024]{1,0:T(8,128)(2,1)}, bf16[128,1024]{1,0:T(8,128)(2,1)}, bf16[128,1024]{1,0:T(8,128)(2,1)}) custom-call(s32[4]{0:T(128)} %pad_add_fusion.order, bf16[2048,512]{1,0:T(8,128)(2,1)} %get-tuple-element.112.act, bf16[2048,128]{1,0:T(8,128)(2,1)} %get-tuple-element.113.mixed, ...), custom_call_target="tpu_custom_call" | custom-call | flops 1000000 | bytes 100000 | tf_op jit(solution)/shard_map/down_kernel/pallas_call | solution.py:784
  239.1 1.0 dynamic-slice_bitcast_fusion
  240.8 3.4 %all-to-all-start.2 = ((f32[32,1,384]{2,1,0:T(1,128)}), f32[32,1,384]{2,1,0:T(1,128)S(1)}, u32[]{:S(2)}, u32[]{:S(2)}) async-start(f32[32,1,384]{2,1,0:T(1,128)} %copy.45), calls=%async_computation.3 | async-start | bytes 98304 | tf_op jit(solution)/shard_map/all_to_all | solution.py:771
  244.3 1.0 add_convert_fusion
  245.3 6.9 %all-to-all-done.2 = f32[32,1,384]{2,1,0:T(1,128)S(1)} async-done(((f32[32,1,384]{2,1,0:T(1,128)}), f32[32,1,384]{2,1,0:T(1,128)S(1)}, u32[]{:S(2)}, u32[]{:S(2)}) %all-to-all-start.2) | async-done | bytes 49184 | tf_op jit(solution)/shard_map/all_to_all | solution.py:771
  252.2 3.5 %all-to-all-start.3 = ((bf16[8,32,896]{2,1,0:T(8,128)(2,1)}), bf16[8,32,896]{2,1,0:T(8,128)(2,1)S(1)}, u32[]{:S(2)}, u32[]{:S(2)}) async-start(bf16[8,32,896]{2,1,0:T(8,128)(2,1)} %bitcast.49), calls=%async_computation.5 | async-start | bytes 917504 | tf_op jit(solution)/shard_map/all_to_all | solution.py:773
  255.9 1.0 collective-permute-start.11
  256.9 1.1 collective-permute-start.14
  258.0 0.9 collective-permute-start.15
  258.9 1.4 collective-permute-start.16
  260.4 0.8 collective-permute-start.12
  261.2 1.9 collective-permute-start.13
  266.0 8.7 %collective-permute-done.12 = bf16[32,1024]{1,0:T(8,128)(2,1)S(1)} collective-permute-done((bf16[32,1024]{1,0:T(8,128)(2,1)S(1)}, bf16[32,1024]{1,0:T(8,128)(2,1)S(1)}, u32[]{:S(2)}, u32[]{:S(2)}) %collective-permute-start.12) | collective-permute-done | bytes 65568 | tf_op jit(solution)/shard_map/ppermute | solution.py:519
  275.4 0.9 convert_add_fusion
  276.3 0.8 copy-done
  277.1 2.0 unpack_columns.1
  279.1 3.0 %norm_back_kernel.1 = bf16[256,1024]{1,0:T(8,128)(2,1)} custom-call(bf16[256,1024]{1,0:T(8,128)(2,1)} %bitcast.112, bf16[256,1024]{1,0:T(8,128)(2,1)} %bitcast.98, f32[256,1024]{1,0:T(8,128)} %get-tuple-element.109.og, f32[1,1024]{1,0:T(1,128)} %get-tuple-element.71.gain), custom_call_target="tpu_custom_call" | custom-call | flops 1000000 | bytes 3000000 | tf_op jit(solution)/shard_map/norm_back_kernel/pallas_call | solution.py:804
  (112 shorter events, 16.2 us)
Async XLA Ops:
  7.2 66.8 %all-gather.3.cloned.1.call-start = ((), (), s32[]{:S(2)}) async-start(), calls=%async_computation.6 | async-start | bytes 4718592 | tf_op jit(solution)/shard_map/all_gather | solution.py:602
  10.9 11.7 %collective-permute-start = (bf16[160,1024]{1,0:T(8,128)(2,1)S(1)}, bf16[160,1024]{1,0:T(8,128)(2,1)}, u32[]{:S(2)}, u32[]{:S(2)}) collective-permute-start(bf16[160,1024]{1,0:T(8,128)(2,1)S(1)} %pad_maximum_fusion), channel_id=1, source_target_pairs={{0,8},{8,0},{16,24},{24,16},{1,9},{9,1},{17,25},{25,17},{2,10},{10... | collective-permute-start | bytes 983048 | tf_op jit(solution)/shard_map/ppermute | solution.py:493
  13.9 16.3 %collective-permute-start.1 = (bf16[160,1024]{1,0:T(8,128)(2,1)S(1)}, bf16[160,1024]{1,0:T(8,128)(2,1)}, u32[]{:S(2)}, u32[]{:S(2)}) collective-permute-start(bf16[160,1024]{1,0:T(8,128)(2,1)S(1)} %pad_maximum_fusion), channel_id=1, source_target_pairs={{0,16},{8,24},{16,0},{24,8},{1,17},{9,25},{17,1},{25,9},{2,18},{10... | collective-permute-start | bytes 983048 | tf_op jit(solution)/shard_map/ppermute | solution.py:493
  15.4 15.8 %collective-permute-start.2 = (bf16[160,1024]{1,0:T(8,128)(2,1)S(1)}, bf16[160,1024]{1,0:T(8,128)(2,1)S(1)}, u32[]{:S(2)}, u32[]{:S(2)}) collective-permute-start(bf16[160,1024]{1,0:T(8,128)(2,1)S(1)} %pad_maximum_fusion), channel_id=1, source_target_pairs={{0,24},{8,16},{16,8},{24,0},{1,25},{9,17},{17,9},{25,1},{2,26},{10... | collective-permute-start | bytes 983048 | tf_op jit(solution)/shard_map/ppermute | solution.py:493
  15.4 31.9 %all-to-all-start = ((bf16[8,32,896]{2,1,0:T(8,128)(2,1)}), bf16[8,32,896]{2,1,0:T(8,128)(2,1)S(1)}, u32[]{:S(2)}, u32[]{:S(2)}) async-start(bf16[8,32,896]{2,1,0:T(8,128)(2,1)} %get-tuple-element.68), calls=%async_computation | async-start | bytes 917504 | tf_op jit(solution)/shard_map/all_to_all | solution.py:603
  31.3 22.9 %copy-start.7 = (s32[2,1024]{1,0:T(2,128)S(1)}, s32[2,1024]{1,0:T(2,128)}, u32[]{:S(2)}) copy-start(s32[2,1024]{1,0:T(2,128)} %seg_row.1) | copy-start | bytes 24580
  31.3 6.8 %collective-permute-start.3 = (bf16[2,32,1024]{2,1,0:T(8,128)(2,1)S(1)}, bf16[2,32,1024]{2,1,0:T(8,128)(2,1)S(1)}, u32[]{:S(2)}, u32[]{:S(2)}) collective-permute-start(bf16[2,32,1024]{2,1,0:T(8,128)(2,1)S(1)} %dynamic-slice_bitcast_fusion.1), channel_id=1, source_target_pairs={{0,1},{1,0},{2,3},{3,2},{4,5},{5,4},{6,7},{7,6},{8,9},{9,8},{10,11... | collective-permute-start | bytes 393224 | tf_op jit(solution)/shard_map/ppermute | solution.py:650
  47.4 26.7 %copy-start.5 = (bf16[8,32,896]{2,1,0:T(8,128)(2,1)}, bf16[8,32,896]{2,1,0:T(8,128)(2,1)S(1)}, u32[]{:S(2)}) copy-start(bf16[8,32,896]{2,1,0:T(8,128)(2,1)S(1)} %all-to-all-done) | copy-start | bytes 1376260
  47.4 26.6 %collective-permute-start.4 = (bf16[256,896]{1,0:T(8,128)(2,1)S(1)}, bf16[256,896]{1,0:T(8,128)(2,1)S(1)}, u32[]{:S(2)}, u32[]{:S(2)}) collective-permute-start(bf16[256,896]{1,0:T(8,128)(2,1)S(1)} %bitcast.114), channel_id=1, source_target_pairs={{0,8},{8,0},{16,24},{24,16},{1,9},{9,1},{17,25},{25,17},{2,10},{10... | collective-permute-start | bytes 1376264 | tf_op jit(solution)/shard_map/ppermute | solution.py:625
  47.8 26.1 %collective-permute-start.5 = (bf16[256,896]{1,0:T(8,128)(2,1)S(1)}, bf16[256,896]{1,0:T(8,128)(2,1)S(1)}, u32[]{:S(2)}, u32[]{:S(2)}) collective-permute-start(bf16[256,896]{1,0:T(8,128)(2,1)S(1)} %bitcast.115), channel_id=1, source_target_pairs={{0,16},{8,24},{16,0},{24,8},{1,17},{9,25},{17,1},{25,9},{2,18},{10... | collective-permute-start | bytes 1376264 | tf_op jit(solution)/shard_map/ppermute | solution.py:625
  50.3 23.6 %collective-permute-start.6 = (bf16[256,896]{1,0:T(8,128)(2,1)S(1)}, bf16[256,896]{1,0:T(8,128)(2,1)S(1)}, u32[]{:S(2)}, u32[]{:S(2)}) collective-permute-start(bf16[256,896]{1,0:T(8,128)(2,1)S(1)} %bitcast.116), channel_id=1, source_target_pairs={{0,24},{8,16},{16,8},{24,0},{1,25},{9,17},{17,9},{25,1},{2,26},{10... | collective-permute-start | bytes 1376264 | tf_op jit(solution)/shard_map/ppermute | solution.py:625
  50.8 20.9 %all-to-all-start.1 = ((bf16[32,8,128]{2,1,0:T(8,128)(2,1)}), bf16[32,8,128]{2,1,0:T(8,128)(2,1)S(1)}, u32[]{:S(2)}, u32[]{:S(2)}) async-start(bf16[32,8,128]{2,1,0:T(8,128)(2,1)} %get-tuple-element.70), calls=%async_computation.1 | async-start | bytes 131072 | tf_op jit(solution)/shard_map/all_to_all | solution.py:605
  54.1 88.9 %reduce-scatter.3.cloned.1.call-start = ((), (), s32[]{:S(2)}) async-start(), calls=%async_computation.7 | async-start | bytes 4718592 | tf_op jit(solution)/shard_map/reduce_scatter | solution.py:686
  71.7 0.6 copy-start.2
  73.9 0.8 copy-start.14
  74.0 0.9 copy-start.15
  74.0 1.1 copy-start.16
  95.1 0.7 copy-start.8
  95.1 1.5 copy-start.3
  95.2 95.8 %all-gather.5.cloned.1.call-start = ((), (), s32[]{:S(2)}) async-start(), calls=%async_computation.8 | async-start | bytes 4718592 | tf_op jit(solution)/shard_map/all_gather | solution.py:709
  145.5 133.6 %reduce-scatter.5.cloned.1.call-start = ((), (), s32[]{:S(2)}) async-start(), calls=%async_computation.9 | async-start | bytes 4718592 | tf_op jit(solution)/shard_map/reduce_scatter | solution.py:742
  217.9 1.0 copy-start.17
  217.9 10.2 %copy-start.12 = (f32[1,384]{1,0:T(1,128)S(1)}, f32[1,384]{1,0:T(1,128)}, u32[]{:S(2)}) copy-start(f32[1,384]{1,0:T(1,128)} %get-tuple-element.102) | copy-start | bytes 4612
  217.9 10.5 %copy-start.10 = (f32[1,1024]{1,0:T(1,128)S(1)}, f32[1,1024]{1,0:T(1,128)}, u32[]{:S(2)}) copy-start(f32[1,1024]{1,0:T(1,128)} %get-tuple-element.99) | copy-start | bytes 12292
  217.9 11.2 %copy-start.9 = (f32[1,1024]{1,0:T(1,128)S(1)}, f32[1,1024]{1,0:T(1,128)}, u32[]{:S(2)}) copy-start(f32[1,1024]{1,0:T(1,128)} %get-tuple-element.100) | copy-start | bytes 12292
  217.9 12.0 %copy-start.11 = (f32[1,512]{1,0:T(1,128)S(1)}, f32[1,512]{1,0:T(1,128)}, u32[]{:S(2)}) copy-start(f32[1,512]{1,0:T(1,128)} %get-tuple-element.103) | copy-start | bytes 6148
  218.9 13.4 %collective-permute-start.7 = (bf16[256,896]{1,0:T(8,128)(2,1)S(1)}, bf16[256,896]{1,0:T(8,128)(2,1)S(1)}, u32[]{:S(2)}, u32[]{:S(2)}) collective-permute-start(bf16[256,896]{1,0:T(8,128)(2,1)S(1)} %copy-done.17), channel_id=1, source_target_pairs={{0,8},{8,0},{16,24},{24,16},{1,9},{9,1},{17,25},{25,17},{2,10},{10... | collective-permute-start | bytes 1376264 | tf_op jit(solution)/shard_map/ppermute | solution.py:502
  220.4 23.9 %collective-permute-start.8 = (bf16[256,896]{1,0:T(8,128)(2,1)}, bf16[256,896]{1,0:T(8,128)(2,1)S(1)}, u32[]{:S(2)}, u32[]{:S(2)}) collective-permute-start(bf16[256,896]{1,0:T(8,128)(2,1)} %get-tuple-element.97), channel_id=1, source_target_pairs={{0,16},{8,24},{16,0},{24,8},{1,17},{9,25},{17,1},{25,9},{2,18},{10... | collective-permute-start | bytes 1376264 | tf_op jit(solution)/shard_map/ppermute | solution.py:502
  221.9 22.4 %collective-permute-start.9 = (bf16[256,896]{1,0:T(8,128)(2,1)}, bf16[256,896]{1,0:T(8,128)(2,1)S(1)}, u32[]{:S(2)}, u32[]{:S(2)}) collective-permute-start(bf16[256,896]{1,0:T(8,128)(2,1)} %get-tuple-element.98), channel_id=1, source_target_pairs={{0,24},{8,16},{16,8},{24,0},{1,25},{9,17},{17,9},{25,1},{2,26},{10... | collective-permute-start | bytes 1376264 | tf_op jit(solution)/shard_map/ppermute | solution.py:502
  232.3 12.0 %copy-start.1 = (f32[256,896]{1,0:T(8,128)S(1)}, f32[256,896]{1,0:T(8,128)}, u32[]{:S(2)}) copy-start(f32[256,896]{1,0:T(8,128)} %get-tuple-element.93) | copy-start | bytes 2752516
  239.1 16.6 %copy-start.6 = (bf16[128,1024]{1,0:T(8,128)(2,1)S(1)}, bf16[128,1024]{1,0:T(8,128)(2,1)}, u32[]{:S(2)}) copy-start(bf16[128,1024]{1,0:T(8,128)(2,1)} %get-tuple-element.114) | copy-start | bytes 786436
  240.1 15.6 %collective-permute-start.10 = (bf16[2,32,1024]{2,1,0:T(8,128)(2,1)S(1)}, bf16[2,32,1024]{2,1,0:T(8,128)(2,1)S(1)}, u32[]{:S(2)}, u32[]{:S(2)}) collective-permute-start(bf16[2,32,1024]{2,1,0:T(8,128)(2,1)S(1)} %dynamic-slice_bitcast_fusion), channel_id=1, source_target_pairs={{0,1},{1,0},{2,3},{3,2},{4,5},{5,4},{6,7},{7,6},{8,9},{9,8},{10,11... | collective-permute-start | bytes 393224 | tf_op jit(solution)/shard_map/ppermute | solution.py:793
  240.8 11.4 %all-to-all-start.2 = ((f32[32,1,384]{2,1,0:T(1,128)}), f32[32,1,384]{2,1,0:T(1,128)S(1)}, u32[]{:S(2)}, u32[]{:S(2)}) async-start(f32[32,1,384]{2,1,0:T(1,128)} %copy.45), calls=%async_computation.3 | async-start | bytes 98304 | tf_op jit(solution)/shard_map/all_to_all | solution.py:771
  244.3 31.1 %copy-start.4 = (f32[128,1024]{1,0:T(8,128)S(1)}, f32[128,1024]{1,0:T(8,128)}, u32[]{:S(2)}) copy-start(f32[128,1024]{1,0:T(8,128)} %get-tuple-element.116) | copy-start | bytes 1572868
  252.2 24.1 %all-to-all-start.3 = ((bf16[8,32,896]{2,1,0:T(8,128)(2,1)}), bf16[8,32,896]{2,1,0:T(8,128)(2,1)S(1)}, u32[]{:S(2)}, u32[]{:S(2)}) async-start(bf16[8,32,896]{2,1,0:T(8,128)(2,1)} %bitcast.49), calls=%async_computation.5 | async-start | bytes 917504 | tf_op jit(solution)/shard_map/all_to_all | solution.py:773
  255.9 5.3 %collective-permute-start.11 = (bf16[32,1024]{1,0:T(8,128)(2,1)S(1)}, bf16[32,1024]{1,0:T(8,128)(2,1)S(1)}, u32[]{:S(2)}, u32[]{:S(2)}) collective-permute-start(bf16[32,1024]{1,0:T(8,128)(2,1)S(1)} %get-tuple-element.126), channel_id=1, source_target_pairs={{0,8},{8,0},{16,24},{24,16},{1,9},{9,1},{17,25},{25,17},{2,10},{10... | collective-permute-start | bytes 196616 | tf_op jit(solution)/shard_map/ppermute | solution.py:519
  256.9 18.5 %collective-permute-start.14 = (bf16[128,1024]{1,0:T(8,128)(2,1)}, bf16[128,1024]{1,0:T(8,128)(2,1)S(1)}, u32[]{:S(2)}, u32[]{:S(2)}) collective-permute-start(bf16[128,1024]{1,0:T(8,128)(2,1)} %get-tuple-element.117), channel_id=1, source_target_pairs={{0,8},{8,0},{16,24},{24,16},{1,9},{9,1},{17,25},{25,17},{2,10},{10... | collective-permute-start | bytes 786440 | tf_op jit(solution)/shard_map/ppermute | solution.py:502
  258.0 17.4 %collective-permute-start.15 = (bf16[128,1024]{1,0:T(8,128)(2,1)}, bf16[128,1024]{1,0:T(8,128)(2,1)S(1)}, u32[]{:S(2)}, u32[]{:S(2)}) collective-permute-start(bf16[128,1024]{1,0:T(8,128)(2,1)} %get-tuple-element.118), channel_id=1, source_target_pairs={{0,16},{8,24},{16,0},{24,8},{1,17},{9,25},{17,1},{25,9},{2,18},{10... | collective-permute-start | bytes 786440 | tf_op jit(solution)/shard_map/ppermute | solution.py:502
  258.9 16.5 %collective-permute-start.16 = (bf16[128,1024]{1,0:T(8,128)(2,1)}, bf16[128,1024]{1,0:T(8,128)(2,1)S(1)}, u32[]{:S(2)}, u32[]{:S(2)}) collective-permute-start(bf16[128,1024]{1,0:T(8,128)(2,1)} %get-tuple-element.119), channel_id=1, source_target_pairs={{0,24},{8,16},{16,8},{24,0},{1,25},{9,17},{17,9},{25,1},{2,26},{10... | collective-permute-start | bytes 786440 | tf_op jit(solution)/shard_map/ppermute | solution.py:502
  260.4 14.3 %collective-permute-start.12 = (bf16[32,1024]{1,0:T(8,128)(2,1)S(1)}, bf16[32,1024]{1,0:T(8,128)(2,1)S(1)}, u32[]{:S(2)}, u32[]{:S(2)}) collective-permute-start(bf16[32,1024]{1,0:T(8,128)(2,1)S(1)} %get-tuple-element.127), channel_id=1, source_target_pairs={{0,16},{8,24},{16,0},{24,8},{1,17},{9,25},{17,1},{25,9},{2,18},{10... | collective-permute-start | bytes 196616 | tf_op jit(solution)/shard_map/ppermute | solution.py:519
  261.2 13.5 %collective-permute-start.13 = (bf16[32,1024]{1,0:T(8,128)(2,1)S(1)}, bf16[32,1024]{1,0:T(8,128)(2,1)S(1)}, u32[]{:S(2)}, u32[]{:S(2)}) collective-permute-start(bf16[32,1024]{1,0:T(8,128)(2,1)S(1)} %get-tuple-element.128), channel_id=1, source_target_pairs={{0,24},{8,16},{16,8},{24,0},{1,25},{9,17},{17,9},{25,1},{2,26},{10... | collective-permute-start | bytes 196616 | tf_op jit(solution)/shard_map/ppermute | solution.py:519
  263.6 18.5 %copy-start.13 = (f32[32]{0:T(128)}, f32[32]{0:T(128)S(1)}, u32[]{:S(2)}) copy-start(f32[32]{0:T(128)S(1)} %get-tuple-element.172) | copy-start | bytes 388
  276.3 0.8 copy-start
Sparse Core Ops, SparseCore 0:
  9.6 60.9 all-gather.2
  95.3 47.6 reduce-scatter.2
  145.7 45.2 all-gather.4
  218.1 55.0 reduce-scatter.4
